TPU v7x, 32 devices: a whole 2x2x4 slice. The times are simulated.
32 devices in a mesh: dp: 4 (over z), expert: 2 (over y), ctx: 4 (over x, core).
Axes of the slice: x: 2, y: 2, z: 4, core: 2. Of those that a mesh axis runs over, the one named last changes fastest.
Arguments:
- tokens: bfloat16 [8192, 1536], P(('dp', 'expert', 'ctx')), may hold values from -6 to 6
- cotangent: bfloat16 [8192, 1536], P(('dp', 'expert', 'ctx')), may hold values from -6 to 6
- routes: int32 [8192, 8], P(('dp', 'expert', 'ctx')), may hold values from 0 to 39, all different within a row; in each aligned block of 256 rows (0 to 255, 256 to 511, ...) at most 64 rows name the same one
- positions: int32 [8192], P(('dp', 'expert', 'ctx')), may hold values from 0 to 2046, as said below
- gain_attend: bfloat16 [1536], P(('dp', 'expert', 'ctx')), may hold values from 0.5 to 1.5
- gain_attend_mean: float32 [1536], P(('dp', 'expert', 'ctx'))
- gain_attend_square: float32 [1536], P(('dp', 'expert', 'ctx'))
- project_in: bfloat16 [1536, 2560], P(('dp', 'expert', 'ctx')), may hold values from -0.625 to 0.625
- project_in_mean: float32 [1536, 2560], P(('dp', 'expert', 'ctx'))
- project_in_square: float32 [1536, 2560], P(('dp', 'expert', 'ctx'))
- project_out: bfloat16 [1536, 1536], P(('dp', 'expert', 'ctx')), may hold values from -0.5 to 0.5
- project_out_mean: float32 [1536, 1536], P(('dp', 'expert', 'ctx'))
- project_out_square: float32 [1536, 1536], P(('dp', 'expert', 'ctx'))
- gain_expert: bfloat16 [1536], P(('dp', 'expert', 'ctx')), may hold values from 0.5 to 1.5
- gain_expert_mean: float32 [1536], P(('dp', 'expert', 'ctx'))
- gain_expert_square: float32 [1536], P(('dp', 'expert', 'ctx'))
- router_weight: bfloat16 [1536, 40], P(('dp', 'expert', 'ctx')), may hold values from -0.078125 to 0.078125
- router_weight_mean: float32 [1536, 40], P(('dp', 'expert', 'ctx'))
- router_weight_square: float32 [1536, 40], P(('dp', 'expert', 'ctx'))
- expert_in: bfloat16 [40, 1536, 1024], P('expert', ('dp', 'ctx')), may hold values from -0.15625 to 0.15625
- expert_in_mean: float32 [40, 1536, 1024], P('expert', ('dp', 'ctx'))
- expert_in_square: float32 [40, 1536, 1024], P('expert', ('dp', 'ctx'))
- expert_out: bfloat16 [40, 512, 1536], P('expert', ('dp', 'ctx')), may hold values from -1.5 to 1.5
- expert_out_mean: float32 [40, 512, 1536], P('expert', ('dp', 'ctx'))
- expert_out_square: float32 [40, 512, 1536], P('expert', ('dp', 'ctx'))
Outputs:
- block_output: bfloat16 [8192, 1536], P(('dp', 'expert', 'ctx'))
- input_grad: float32 [8192, 1536], P(('dp', 'expert', 'ctx'))
- gain_attend_grad: float32 [1536], P(('dp', 'expert', 'ctx'))
- gain_attend_mean_out: float32 [1536], P(('dp', 'expert', 'ctx'))
- gain_attend_square_out: float32 [1536], P(('dp', 'expert', 'ctx'))
- gain_attend_new: float32 [1536], P(('dp', 'expert', 'ctx'))
- project_in_grad: float32 [1536, 2560], P(('dp', 'expert', 'ctx'))
- project_in_mean_out: float32 [1536, 2560], P(('dp', 'expert', 'ctx'))
- project_in_square_out: float32 [1536, 2560], P(('dp', 'expert', 'ctx'))
- project_in_new: float32 [1536, 2560], P(('dp', 'expert', 'ctx'))
- project_out_grad: float32 [1536, 1536], P(('dp', 'expert', 'ctx'))
- project_out_mean_out: float32 [1536, 1536], P(('dp', 'expert', 'ctx'))
- project_out_square_out: float32 [1536, 1536], P(('dp', 'expert', 'ctx'))
- project_out_new: float32 [1536, 1536], P(('dp', 'expert', 'ctx'))
- gain_expert_grad: float32 [1536], P(('dp', 'expert', 'ctx'))
- gain_expert_mean_out: float32 [1536], P(('dp', 'expert', 'ctx'))
- gain_expert_square_out: float32 [1536], P(('dp', 'expert', 'ctx'))
- gain_expert_new: float32 [1536], P(('dp', 'expert', 'ctx'))
- router_weight_grad: float32 [1536, 40], P(('dp', 'expert', 'ctx'))
- router_weight_mean_out: float32 [1536, 40], P(('dp', 'expert', 'ctx'))
- router_weight_square_out: float32 [1536, 40], P(('dp', 'expert', 'ctx'))
- router_weight_new: float32 [1536, 40], P(('dp', 'expert', 'ctx'))
- expert_in_grad: float32 [40, 1536, 1024], P('expert', ('dp', 'ctx'))
- expert_in_mean_out: float32 [40, 1536, 1024], P('expert', ('dp', 'ctx'))
- expert_in_square_out: float32 [40, 1536, 1024], P('expert', ('dp', 'ctx'))
- expert_in_new: float32 [40, 1536, 1024], P('expert', ('dp', 'ctx'))
- expert_out_grad: float32 [40, 512, 1536], P('expert', ('dp', 'ctx'))
- expert_out_mean_out: float32 [40, 512, 1536], P('expert', ('dp', 'ctx'))
- expert_out_square_out: float32 [40, 512, 1536], P('expert', ('dp', 'ctx'))
- expert_out_new: float32 [40, 512, 1536], P('expert', ('dp', 'ctx'))
Inputs may be any that keep to these rules, and one draw needn't show every extreme that they name: `routes`: each row names 8 different experts; in each device's 256 rows no expert is named by more than 64 rows. Within each sequence positions start at 0 and rise by 1 or 2 from one token to the next.
All inputs are finite; a program needn't handle non-finite values.
Results may differ from a plain program's by a relative error of at most 0.019.
Values may be sent and summed in bfloat16 or wider, within the bound.
A program may use at most 384 MiB of HBM per device.

v0:
```python
import jax
import jax.numpy as jnp
from jax import lax
from jax.sharding import PartitionSpec as P

D = 1536
H = 24
KV = 8
HD = 64
FFE = 512
EXPERTS = 40
TOP = 8
STEP = 8
CAP = 64


EPS_NORM = 1e-06
ATTN_SCALE = 0.015625
RESIDUAL_SCALE = 0.22
BETA_ONE = 0.9
BETA_TWO = 0.95
ADAM_EPS = 1e-08
DECAY_RATE = 0.1
ROPE_BASE = 10000.0


def normalize(rows):
    factor = lax.rsqrt(jnp.mean(rows * rows, axis=-1, keepdims=True) + EPS_NORM)
    return (rows * factor, factor)


def norm_back(grad_normed, normed, factor):
    return factor * (grad_normed - normed * jnp.mean(grad_normed * normed, axis=-1, keepdims=True))


def rope_tables(positions):
    half = HD // 2
    freqs = ROPE_BASE ** (-jnp.arange(half, dtype=jnp.float32) * 2.0 / HD)
    angles = positions.astype(jnp.float32)[:, None] * freqs[None, :]
    cosine = jnp.cos(angles)
    sine = jnp.sin(angles)
    return (jnp.concatenate([cosine, cosine], 1), jnp.concatenate([sine, sine], 1))


def rotate(values, cosine, sine):
    half = values.shape[-1] // 2
    turned = jnp.concatenate([-values[..., half:], values[..., :half]], -1)
    return values * cosine[:, None, :] + turned * sine[:, None, :]


def rotate_back(grads, cosine, sine):
    half = grads.shape[-1] // 2
    scaled = grads * sine[:, None, :]
    turned = jnp.concatenate([scaled[..., half:], -scaled[..., :half]], -1)
    return grads * cosine[:, None, :] + turned


def learn_rates():
    return (
        0.3,
        3.0 / (D // 16) ** 0.5,
        3.0 / (D // 12) ** 0.5,
        0.3,
        3.0 / (4 * D) ** 0.5,
        3.0 / D**0.5,
        3.0 / (FFE // 32) ** 0.5,
    )


def adam_step(weight, first, second, grad, decay, rate):
    new_first = BETA_ONE * first + (1.0 - BETA_ONE) * grad
    new_second = BETA_TWO * second + (1.0 - BETA_TWO) * grad * grad
    corrected = (
        new_first
        / (1.0 - BETA_ONE**STEP)
        / (jnp.sqrt(new_second / (1.0 - BETA_TWO**STEP)) + ADAM_EPS)
    )
    old = weight.astype(jnp.float32)
    return (grad, new_first, new_second, old - rate * (corrected + decay * old))


def local(
    tokens,
    cotangent,
    routes,
    positions,
    gain_attend,
    gain_attend_mean,
    gain_attend_square,
    project_in,
    project_in_mean,
    project_in_square,
    project_out,
    project_out_mean,
    project_out_square,
    gain_expert,
    gain_expert_mean,
    gain_expert_square,
    router_weight,
    router_weight_mean,
    router_weight_square,
    expert_in,
    expert_in_mean,
    expert_in_square,
    expert_out,
    expert_out_mean,
    expert_out_square,
):
    full_attend, full_in, full_out, full_expert, full_router = (
        lax.all_gather(gain_attend, ("dp", "expert", "ctx"), axis=0, tiled=True),
        lax.all_gather(project_in, ("dp", "expert", "ctx"), axis=0, tiled=True),
        lax.all_gather(project_out, ("dp", "expert", "ctx"), axis=0, tiled=True),
        lax.all_gather(gain_expert, ("dp", "expert", "ctx"), axis=0, tiled=True),
        lax.all_gather(router_weight, ("dp", "expert", "ctx"), axis=0, tiled=True),
    )
    whole_in, whole_out = (
        lax.all_gather(expert_in, ("dp", "ctx"), axis=1, tiled=True),
        lax.all_gather(expert_out, ("dp", "ctx"), axis=1, tiled=True),
    )
    rows_local = tokens.shape[0]
    repeat = H // KV
    query_width = H * HD
    key_width = KV * HD
    hidden_in = tokens.astype(jnp.float32)
    normed_one, factor_one = normalize(hidden_in)
    gain_one = full_attend.astype(jnp.float32)
    attend_in = (normed_one * gain_one).astype(jnp.bfloat16)
    mixed = jnp.dot(attend_in, full_in, preferred_element_type=jnp.float32)
    cosine, sine = rope_tables(positions)
    query = rotate(mixed[:, :query_width].reshape(rows_local, H, HD), cosine, sine).astype(
        jnp.bfloat16
    )
    keys_flat = (
        rotate(
            mixed[:, query_width : query_width + key_width].reshape(rows_local, KV, HD),
            cosine,
            sine,
        )
        .astype(jnp.bfloat16)
        .reshape(rows_local, key_width)
    )
    values_flat = mixed[:, query_width + key_width :].astype(jnp.bfloat16)
    all_keys, all_values = (
        lax.all_gather(keys_flat, "ctx", axis=0, tiled=True),
        lax.all_gather(values_flat, "ctx", axis=0, tiled=True),
    )
    seq_rows = all_keys.shape[0]
    offset = lax.axis_index("ctx") * rows_local
    query_index = offset + jnp.arange(rows_local, dtype=jnp.int32)
    key_index = jnp.arange(seq_rows, dtype=jnp.int32)
    allowed = key_index[None, :] <= query_index[:, None]
    query_groups = query.reshape(rows_local, KV, repeat, HD).transpose(1, 2, 0, 3)
    key_groups = all_keys.reshape(seq_rows, KV, HD).transpose(1, 0, 2)
    value_groups = all_values.reshape(seq_rows, KV, HD).transpose(1, 0, 2)

    def attend_group(operands):
        group_query, group_keys, group_values = operands
        scores = (
            jnp.einsum("rtd,sd->rts", group_query, group_keys, preferred_element_type=jnp.float32)
            * ATTN_SCALE
        )
        scores = jnp.where(allowed[None], scores, -1e30)
        peak = jnp.max(scores, axis=-1, keepdims=True)
        raised = jnp.exp(scores - peak)
        total = jnp.sum(raised, axis=-1, keepdims=True)
        probs = (raised / total).astype(jnp.bfloat16)
        output = jnp.einsum("rts,sd->rtd", probs, group_values, preferred_element_type=jnp.float32)
        return (output, (peak + jnp.log(total))[..., 0])

    group_outputs, group_lse = lax.map(attend_group, (query_groups, key_groups, value_groups))
    attended = (
        group_outputs.transpose(2, 0, 1, 3).reshape(rows_local, query_width).astype(jnp.bfloat16)
    )
    branch = jnp.dot(attended, full_out, preferred_element_type=jnp.float32)
    after = hidden_in + RESIDUAL_SCALE * branch
    normed_two, factor_two = normalize(after)
    gain_two = full_expert.astype(jnp.float32)
    expert_input = (normed_two * gain_two).astype(jnp.bfloat16)
    logits = jnp.dot(expert_input, full_router, preferred_element_type=jnp.float32)
    chosen = routes[:, :, None] == jnp.arange(EXPERTS, dtype=jnp.int32)[None, None, :]
    picked = jnp.sum(jnp.where(chosen, logits[:, None, :], 0.0), axis=-1)
    top_logit = jnp.max(picked, axis=-1, keepdims=True)
    raised_gates = jnp.exp(picked - top_logit)
    gates = raised_gates / jnp.sum(raised_gates, axis=-1, keepdims=True)
    flat_routes = routes.reshape(-1)
    marks = (flat_routes[:, None] == jnp.arange(EXPERTS, dtype=jnp.int32)[None, :]).astype(
        jnp.int32
    )
    rank = jnp.sum((jnp.cumsum(marks, axis=0) - marks) * marks, axis=1)
    slot = flat_routes * CAP + rank
    owners = lax.axis_size("expert")
    local_count = expert_in.shape[0]
    send_rows = jnp.broadcast_to(expert_input[:, None, :], (rows_local, TOP, D)).reshape(
        rows_local * TOP, D
    )
    outgoing = jnp.zeros((EXPERTS * CAP, D), jnp.bfloat16).at[slot].set(send_rows)
    received = lax.all_to_all(
        outgoing.reshape(owners, local_count, CAP, D),
        "expert",
        split_axis=0,
        concat_axis=2,
        tiled=True,
    )
    received = received.reshape(local_count, owners * CAP, D)
    gate_up = jnp.einsum("erd,edf->erf", received, whole_in, preferred_element_type=jnp.float32)
    gate_half = gate_up[..., :FFE]
    up_half = gate_up[..., FFE:]
    sigma = jax.nn.sigmoid(gate_half)
    activated = gate_half * sigma
    middle = (activated * up_half).astype(jnp.bfloat16)
    produced = jnp.einsum(
        "erf,efd->erd", middle, whole_out, preferred_element_type=jnp.float32
    ).astype(jnp.bfloat16)
    returned = lax.all_to_all(
        produced.reshape(local_count, owners, CAP, D),
        "expert",
        split_axis=1,
        concat_axis=0,
        tiled=True,
    )
    route_out = returned.reshape(EXPERTS * CAP, D)[slot].reshape(rows_local, TOP, D)
    moe = jnp.sum(gates[:, :, None] * route_out, axis=1)
    block_output = (after + RESIDUAL_SCALE * moe).astype(jnp.bfloat16)
    grad_final = cotangent.astype(jnp.float32)
    grad_moe = RESIDUAL_SCALE * grad_final
    grad_gates = jnp.sum(route_out * grad_moe[:, None, :], axis=-1)
    grad_picked = gates * (grad_gates - jnp.sum(gates * grad_gates, axis=-1, keepdims=True))
    grad_logits = jnp.sum(jnp.where(chosen, grad_picked[:, :, None], 0.0), axis=1).astype(
        jnp.bfloat16
    )
    grad_router = jnp.einsum(
        "td,te->de", expert_input, grad_logits, preferred_element_type=jnp.float32
    )
    grad_from_router = jnp.einsum(
        "te,de->td", grad_logits, full_router, preferred_element_type=jnp.float32
    )
    route_grad = (
        (gates[:, :, None] * grad_moe[:, None, :]).astype(jnp.bfloat16).reshape(rows_local * TOP, D)
    )
    outgoing_grad = jnp.zeros((EXPERTS * CAP, D), jnp.bfloat16).at[slot].set(route_grad)
    received_grad = lax.all_to_all(
        outgoing_grad.reshape(owners, local_count, CAP, D),
        "expert",
        split_axis=0,
        concat_axis=2,
        tiled=True,
    )
    received_grad = received_grad.reshape(local_count, owners * CAP, D)
    back_in, back_out = (
        lax.all_gather(expert_in, ("dp", "ctx"), axis=1, tiled=True),
        lax.all_gather(expert_out, ("dp", "ctx"), axis=1, tiled=True),
    )
    grad_expert_out = jnp.einsum(
        "erf,erd->efd", middle, received_grad, preferred_element_type=jnp.float32
    )
    grad_middle = jnp.einsum(
        "erd,efd->erf", received_grad, back_out, preferred_element_type=jnp.float32
    )
    slope = sigma * (1.0 + gate_half * (1.0 - sigma))
    grad_gate_up = jnp.concatenate(
        [grad_middle * up_half * slope, grad_middle * activated], -1
    ).astype(jnp.bfloat16)
    grad_expert_in = jnp.einsum(
        "erd,erf->edf", received, grad_gate_up, preferred_element_type=jnp.float32
    )
    grad_rows = jnp.einsum(
        "erf,edf->erd", grad_gate_up, back_in, preferred_element_type=jnp.float32
    ).astype(jnp.bfloat16)
    returned_grad = lax.all_to_all(
        grad_rows.reshape(local_count, owners, CAP, D),
        "expert",
        split_axis=1,
        concat_axis=0,
        tiled=True,
    )
    route_input_grad = returned_grad.reshape(EXPERTS * CAP, D)[slot].reshape(rows_local, TOP, D)
    grad_input = grad_from_router + jnp.sum(route_input_grad.astype(jnp.float32), axis=1)
    grad_gain_expert = jnp.sum(grad_input * normed_two, axis=0)
    grad_after = grad_final + norm_back(grad_input * gain_two, normed_two, factor_two)
    grad_branch = (RESIDUAL_SCALE * grad_after).astype(jnp.bfloat16)
    grad_project_out = jnp.einsum(
        "tc,td->cd", attended, grad_branch, preferred_element_type=jnp.float32
    )
    grad_attended = jnp.einsum(
        "td,cd->tc", grad_branch, full_out, preferred_element_type=jnp.float32
    ).astype(jnp.bfloat16)
    keys_back, values_back = (
        lax.all_gather(keys_flat, "ctx", axis=0, tiled=True),
        lax.all_gather(values_flat, "ctx", axis=0, tiled=True),
    )
    key_groups = keys_back.reshape(seq_rows, KV, HD).transpose(1, 0, 2)
    value_groups = values_back.reshape(seq_rows, KV, HD).transpose(1, 0, 2)
    grad_groups = grad_attended.reshape(rows_local, KV, repeat, HD).transpose(1, 2, 0, 3)

    def attend_back(operands):
        group_query, group_keys, group_values, group_grad, lse = operands
        scores = (
            jnp.einsum("rtd,sd->rts", group_query, group_keys, preferred_element_type=jnp.float32)
            * ATTN_SCALE
        )
        scores = jnp.where(allowed[None], scores, -1e30)
        probs = jnp.exp(scores - lse[..., None])
        grad_probs = jnp.einsum(
            "rtd,sd->rts", group_grad, group_values, preferred_element_type=jnp.float32
        )
        grad_scores = (
            probs * (grad_probs - jnp.sum(probs * grad_probs, axis=-1, keepdims=True))
        ).astype(jnp.bfloat16)
        grad_query = (
            jnp.einsum("rts,sd->rtd", grad_scores, group_keys, preferred_element_type=jnp.float32)
            * ATTN_SCALE
        )
        grad_keys = (
            jnp.einsum("rts,rtd->sd", grad_scores, group_query, preferred_element_type=jnp.float32)
            * ATTN_SCALE
        )
        grad_values = jnp.einsum(
            "rts,rtd->sd",
            probs.astype(jnp.bfloat16),
            group_grad,
            preferred_element_type=jnp.float32,
        )
        return (grad_query, grad_keys, grad_values)

    group_dq, group_dk, group_dv = lax.map(
        attend_back, (query_groups, key_groups, value_groups, grad_groups, group_lse)
    )
    grad_query = group_dq.transpose(2, 0, 1, 3).reshape(rows_local, H, HD)
    seq_dk = group_dk.transpose(1, 0, 2).reshape(seq_rows, key_width)
    seq_dv = group_dv.transpose(1, 0, 2).reshape(seq_rows, key_width)
    own_dk, own_dv = (
        lax.psum_scatter(
            seq_dk.astype(jnp.bfloat16), "ctx", scatter_dimension=0, tiled=True
        ).astype(jnp.float32),
        lax.psum_scatter(
            seq_dv.astype(jnp.bfloat16), "ctx", scatter_dimension=0, tiled=True
        ).astype(jnp.float32),
    )
    grad_query_raw = rotate_back(grad_query, cosine, sine).reshape(rows_local, query_width)
    grad_keys_raw = rotate_back(own_dk.reshape(rows_local, KV, HD), cosine, sine).reshape(
        rows_local, key_width
    )
    grad_mixed = jnp.concatenate([grad_query_raw, grad_keys_raw, own_dv], 1).astype(jnp.bfloat16)
    grad_project_in = jnp.einsum(
        "td,tc->dc", attend_in, grad_mixed, preferred_element_type=jnp.float32
    )
    grad_attend = jnp.einsum("tc,dc->td", grad_mixed, full_in, preferred_element_type=jnp.float32)
    grad_gain_attend = jnp.sum(grad_attend * normed_one, axis=0)
    input_grad = grad_after + norm_back(grad_attend * gain_one, normed_one, factor_one)
    shard_attend, shard_in, shard_out, shard_expert, shard_router = (
        lax.psum_scatter(
            grad_gain_attend, ("dp", "expert", "ctx"), scatter_dimension=0, tiled=True
        ),
        lax.psum_scatter(grad_project_in, ("dp", "expert", "ctx"), scatter_dimension=0, tiled=True),
        lax.psum_scatter(
            grad_project_out, ("dp", "expert", "ctx"), scatter_dimension=0, tiled=True
        ),
        lax.psum_scatter(
            grad_gain_expert, ("dp", "expert", "ctx"), scatter_dimension=0, tiled=True
        ),
        lax.psum_scatter(grad_router, ("dp", "expert", "ctx"), scatter_dimension=0, tiled=True),
    )
    shard_expert_in, shard_expert_out = (
        lax.psum_scatter(
            grad_expert_in.astype(jnp.bfloat16), ("dp", "ctx"), scatter_dimension=1, tiled=True
        ).astype(jnp.float32),
        lax.psum_scatter(
            grad_expert_out.astype(jnp.bfloat16), ("dp", "ctx"), scatter_dimension=1, tiled=True
        ).astype(jnp.float32),
    )
    rates = learn_rates()
    results = [block_output, input_grad]
    results.extend(
        adam_step(gain_attend, gain_attend_mean, gain_attend_square, shard_attend, 0.0, rates[0])
    )
    results.extend(
        adam_step(project_in, project_in_mean, project_in_square, shard_in, DECAY_RATE, rates[1])
    )
    results.extend(
        adam_step(
            project_out, project_out_mean, project_out_square, shard_out, DECAY_RATE, rates[2]
        )
    )
    results.extend(
        adam_step(gain_expert, gain_expert_mean, gain_expert_square, shard_expert, 0.0, rates[3])
    )
    results.extend(
        adam_step(
            router_weight,
            router_weight_mean,
            router_weight_square,
            shard_router,
            DECAY_RATE,
            rates[4],
        )
    )
    results.extend(
        adam_step(
            expert_in, expert_in_mean, expert_in_square, shard_expert_in, DECAY_RATE, rates[5]
        )
    )
    results.extend(
        adam_step(
            expert_out, expert_out_mean, expert_out_square, shard_expert_out, DECAY_RATE, rates[6]
        )
    )
    return tuple(results)


def solution(mesh):
    placed = (
        P(("dp", "expert", "ctx"), None),
        P(("dp", "expert", "ctx"), None),
        P(("dp", "expert", "ctx"), None),
        P(("dp", "expert", "ctx")),
        P(("dp", "expert", "ctx")),
        P(("dp", "expert", "ctx")),
        P(("dp", "expert", "ctx")),
        P(("dp", "expert", "ctx"), None),
        P(("dp", "expert", "ctx"), None),
        P(("dp", "expert", "ctx"), None),
        P(("dp", "expert", "ctx"), None),
        P(("dp", "expert", "ctx"), None),
        P(("dp", "expert", "ctx"), None),
        P(("dp", "expert", "ctx")),
        P(("dp", "expert", "ctx")),
        P(("dp", "expert", "ctx")),
        P(("dp", "expert", "ctx"), None),
        P(("dp", "expert", "ctx"), None),
        P(("dp", "expert", "ctx"), None),
        P("expert", ("dp", "ctx"), None),
        P("expert", ("dp", "ctx"), None),
        P("expert", ("dp", "ctx"), None),
        P("expert", ("dp", "ctx"), None),
        P("expert", ("dp", "ctx"), None),
        P("expert", ("dp", "ctx"), None),
    )
    return jax.shard_map(
        local,
        mesh=mesh,
        in_specs=placed,
        out_specs=(
            P(("dp", "expert", "ctx"), None),
            P(("dp", "expert", "ctx"), None),
            P(("dp", "expert", "ctx")),
            P(("dp", "expert", "ctx")),
            P(("dp", "expert", "ctx")),
            P(("dp", "expert", "ctx")),
            P(("dp", "expert", "ctx"), None),
            P(("dp", "expert", "ctx"), None),
            P(("dp", "expert", "ctx"), None),
            P(("dp", "expert", "ctx"), None),
            P(("dp", "expert", "ctx"), None),
            P(("dp", "expert", "ctx"), None),
            P(("dp", "expert", "ctx"), None),
            P(("dp", "expert", "ctx"), None),
            P(("dp", "expert", "ctx")),
            P(("dp", "expert", "ctx")),
            P(("dp", "expert", "ctx")),
            P(("dp", "expert", "ctx")),
            P(("dp", "expert", "ctx"), None),
            P(("dp", "expert", "ctx"), None),
            P(("dp", "expert", "ctx"), None),
            P(("dp", "expert", "ctx"), None),
            P("expert", ("dp", "ctx"), None),
            P("expert", ("dp", "ctx"), None),
            P("expert", ("dp", "ctx"), None),
            P("expert", ("dp", "ctx"), None),
            P("expert", ("dp", "ctx"), None),
            P("expert", ("dp", "ctx"), None),
            P("expert", ("dp", "ctx"), None),
            P("expert", ("dp", "ctx"), None),
        ),
        check_vma=False,
    )
```

profile of v0, /device:TPU:0, one launch (start us, length us, event | category | flops | bytes accessed | tf_op | source)
XLA Modules:
  0.0 2410.8 jit_solution(4534808495184770970)
XLA Ops:
  9.7 42.6 %all-reduce.5 = (bf16[1536]{0:T(1024)(128)(2,1)S(1)}, bf16[1536]{0:T(1024)(128)(2,1)S(1)}) all-reduce(bf16[1536]{0:T(1024)(128)(2,1)S(1)} %dynamic-update-slice, bf16[1536]{0:T(1024)(128)(2,1)S(1)} %dynamic-update-slice.1), channel_id=1, replica_groups=mesh['dp'=4,'expert'=2,'ctx'=4] {'dp','expert','ctx'}, use_global_device_ids=true, to_apply=%add | all-reduce | flops 3072 | bytes 12288
  54.9 34.6 %all-gather.8.cloned.1.call-done = bf16[1536,2560]{1,0:T(8,128)(2,1)} async-done(((bf16[48,2560]{1,0:T(8,128)(2,1)}), bf16[1536,2560]{1,0:T(8,128)(2,1)}) %all-gather.8.cloned.1.call-update) | async-done | bytes 7864336 | tf_op jit(solution)/shard_map/all_gather | solution.py:111
  89.6 5.8 fusion.104
  96.2 2.2 copy.140
  107.5 11.3 reduce-window.6
  119.9 2.7 slice.65
  127.5 11.2 all-gather.12.cloned.1.call-done
  138.7 2.3 copy.143
  140.9 43.3 %while.30 = (s32[]{:T(128)}, bf16[8,3,256,64]{2,3,1,0:T(8,128)(2,1)S(1)}, f32[8,3,256]{2,1,0:T(4,128)}, bf16[8,3,256,64]{2,3,1,0:T(8,128)(2,1)}, bf16[8,1024,64]...) while((s32[]{:T(128)}, ...), condition=%wide.region_4.5_spmd.clone.clone, body=%wide.region_1.4_spmd.clone.sunk.clone | while | flops 211025152 | bytes 11073625 | solution.py:170
  184.2 20.8 all-gather.14.cloned.1.call-done
  205.1 3.9 multiply_reduce_fusion.3
  210.4 14.9 scatter_custom_fusion
  225.3 7.2 all-to-all-start
  232.5 43.1 %all-gather = bf16[32,48,40]{1,2,0:T(8,128)(2,1)S(1)} all-gather(bf16[1,48,40]{1,2,0:T(8,128)(2,1)S(1)} %bitcast.288), channel_id=1, replica_groups=mesh['dp'=4,'expert'=2,'ctx'=4] {'dp','expert','ctx'}, dimensions={0}, use_global_device_ids=true | all-gather | bytes 126720 | tf_op jit(solution)/shard_map/all_gather | solution.py:114
  277.6 15.5 scatter_custom_fusion.1
  293.2 28.5 %all-to-all-done = bf16[2,20,64,1536]{3,2,1,0:T(8,128)(2,1)} async-done(((bf16[2,20,64,1536]{3,2,1,0:T(8,128)(2,1)}), bf16[2,20,64,1536]{3,2,1,0:T(8,128)(2,1)}, u32[]{:S(2)}, u32[]{:S(2)}) %all-to-all-start) | async-done | bytes 7864352 | tf_op jit(solution)/shard_map/all_to_all | solution.py:197
  321.7 7.3 all-to-all-start.2
  329.0 7.3 copy.151
  336.4 79.3 %all-to-all-done.2 = bf16[2,20,64,1536]{3,2,1,0:T(8,128)(2,1)} async-done(((bf16[2,20,64,1536]{3,2,1,0:T(8,128)(2,1)}), bf16[2,20,64,1536]{3,2,1,0:T(8,128)(2,1)}, u32[]{:S(2)}, u32[]{:S(2)}) %all-to-all-start.2) | async-done | bytes 7864352 | tf_op jit(solution)/shard_map/all_to_all | solution.py:241
  415.7 7.6 copy.156
  423.3 91.0 %all-gather.16.cloned.1.call-done = bf16[20,1536,1024]{2,1,0:T(8,128)(2,1)} async-done(((bf16[20,96,1024]{2,1,0:T(8,128)(2,1)}), bf16[20,1536,1024]{2,1,0:T(8,128)(2,1)}) %all-gather.16.cloned.1.call-update) | async-done | bytes 62914576 | tf_op jit(solution)/shard_map/all_gather | solution.py:117
  514.3 29.8 %fusion.132 = f32[20,128,1024]{2,1,0:T(8,128)} fusion(bf16[20,128,1536]{2,1,0:T(8,128)(2,1)} %bitcast.262, bf16[20,1536,1024]{2,1,0:T(8,128)(2,1)} %all-gather.16.cloned.1.call-done), kind=kOutput, calls=%fused_computation.223 | convolution fusion | flops 8053063680 | bytes 81264640 | tf_op jit(solution)/shard_map/erd,edf->erf/dot_general | solution.py:205
  544.1 130.5 %all-gather.18.cloned.1.call-done = bf16[20,512,1536]{2,1,0:T(8,128)(2,1)} async-done(((bf16[20,32,1536]{2,1,0:T(8,128)(2,1)}), bf16[20,512,1536]{2,1,0:T(8,128)(2,1)}) %all-gather.18.cloned.1.call-update) | async-done | bytes 31457296 | tf_op jit(solution)/shard_map/all_gather | solution.py:118
  674.6 20.8 multiply_convert_fusion.2
  695.4 30.2 %convolution_convert_fusion.2 = bf16[20,128,1536]{2,1,0:T(8,128)(2,1)} fusion(bf16[20,1536,1024]{2,1,0:T(8,128)(2,1)} %all-gather.16.cloned.1.call-done, bf16[20,128,512]{2,1,0:T(8,128)(2,1)} %get-tuple-element.241, bf16[20,128,512]{2,1,0:T(8,128)(2,1)} %get-tuple-element.240), kind=kOutput, calls=%fused_computation.84 | convolution fusion | flops 8067481600 | bytes 76021760 | tf_op jit(solution)/shard_map/erf,edf->erd/dot_general | solution.py:266
  725.6 7.3 copy.157
  732.9 7.0 all-to-all-start.3
  739.9 16.3 convolution_convert_fusion.3
  756.2 7.2 copy.152
  763.5 63.8 %all-to-all-done.3 = bf16[20,2,64,1536]{3,2,0,1:T(8,128)(2,1)} async-done(((bf16[20,2,64,1536]{3,2,0,1:T(8,128)(2,1)}), bf16[20,2,64,1536]{3,2,0,1:T(8,128)(2,1)}, u32[]{:S(2)}, u32[]{:S(2)}) %all-to-all-start.3) | async-done | bytes 7864352 | tf_op jit(solution)/shard_map/all_to_all | solution.py:269
  827.3 6.8 all-to-all-start.1
  834.3 17.5 gather_fusion.1
  851.8 8.1 convert_reduce_fusion
  859.9 60.7 %all-to-all-done.1 = bf16[20,2,64,1536]{3,2,0,1:T(8,128)(2,1)} async-done(((bf16[20,2,64,1536]{3,2,0,1:T(8,128)(2,1)}), bf16[20,2,64,1536]{3,2,0,1:T(8,128)(2,1)}, u32[]{:S(2)}, u32[]{:S(2)}) %all-to-all-start.1) | async-done | bytes 7864352 | tf_op jit(solution)/shard_map/all_to_all | solution.py:214
  920.7 17.5 gather_fusion
  938.2 9.8 fusion.54
  951.9 2.5 convert_add_fusion
  954.4 3.8 convolution_convert_fusion.4
  958.5 81.5 %while.31 = (s32[]{:T(128)}, f32[8,3,256,64]{2,3,1,0:T(8,128)}, bf16[8,1024,64]{1,2,0:T(8,128)(2,1)}, bf16[8,1024,64]{1,2,0:T(8,128)(2,1)}, bf16[8,3,256,64]{2,3...) while((s32[]{:T(128)}, f32[8,3,256,64]{2,3,1,0:T(8,128)}, ...), condition=%wide.region_22.23_spmd.clone.clone, body=%wide.region_20.22_spmd.clone.sunk.clone | while | flops 510770432 | bytes 25646192 | solution.py:325
  961.0 2.2 multiply_reduce_fusion.7
  971.1 2.2 multiply_reduce_fusion.7
  981.3 2.2 multiply_reduce_fusion.7
  991.5 2.2 multiply_reduce_fusion.7
  1001.7 2.2 multiply_reduce_fusion.7
  1011.8 2.2 multiply_reduce_fusion.7
  1022.0 2.2 multiply_reduce_fusion.7
  1032.2 2.2 multiply_reduce_fusion.7
  1042.2 5.0 fusion.99
  1050.5 13.6 reduce-scatter.10.cloned.1.call-done
  1066.3 25.5 %reduce-scatter.12.cloned.1.call-done = bf16[256,512]{0,1:T(8,128)(2,1)} async-done(((bf16[1024,512]{0,1:T(8,128)(2,1)}), bf16[256,512]{0,1:T(8,128)(2,1)}) %reduce-scatter.12.cloned.1.call-update) | async-done | bytes 262160 | tf_op jit(solution)/shard_map/reduce_scatter | solution.py:335
  1091.8 8.9 fusion.89
  1100.8 17.3 convolution_convert_fusion.1
  1118.1 27.9 %convolution_convert_fusion = bf16[20,1536,1024]{2,1,0:T(8,128)(2,1)} fusion(bf16[20,128,1536]{2,1,0:T(8,128)(2,1)} %bitcast.263, bf16[20,128,512]{2,1,0:T(8,128)(2,1)} %get-tuple-element.241, bf16[20,128,512]{2,1,0:T(8,128)(2,1)} %get-tuple-element.240), kind=kOutput, calls=%fused_computation.63 | convolution fusion | flops 8095006720 | bytes 76021760 | tf_op jit(solution)/shard_map/erd,erf->edf/dot_general | solution.py:263
  1146.0 47.0 %reduce-scatter.22.cloned.1.call-done = f32[48,40]{1,0:T(8,128)} async-done(((f32[1536,40]{1,0:T(8,128)}), f32[48,40]{1,0:T(8,128)}) %reduce-scatter.22.cloned.1.call-update) | async-done | bytes 7696
  1194.5 6.9 fusion.82
  1201.5 40.3 %all-reduce.4 = (f32[1536]{0:T(1024)S(1)}, f32[1536]{0:T(1024)S(1)}) all-reduce(f32[1536]{0:T(1024)S(1)} %get-tuple-element.171, f32[1536]{0:T(1024)S(1)} %get-tuple-element.169), channel_id=4, replica_groups=mesh['dp'=4,'expert'=2,'ctx'=4] {'dp','expert','ctx'}, use_global_device_ids=true, to_apply=%region_27.28.clone | all-reduce | flops 3072 | bytes 24576
  1242.4 3.0 fusion.81
  1245.5 88.6 %reduce-scatter.16.cloned.1.call-done = f32[48,1536]{1,0:T(8,128)} async-done(((f32[1536,1536]{1,0:T(8,128)}), f32[48,1536]{1,0:T(8,128)}) %reduce-scatter.16.cloned.1.call-update) | async-done | bytes 294928 | tf_op jit(solution)/shard_map/reduce_scatter | solution.py:355
  1336.3 175.0 %reduce-scatter.14.cloned.1.call-done = f32[48,2560]{1,0:T(8,128)} async-done(((f32[1536,2560]{1,0:T(8,128)}), f32[48,2560]{1,0:T(8,128)}) %reduce-scatter.14.cloned.1.call-update) | async-done | bytes 491536 | tf_op jit(solution)/shard_map/reduce_scatter | solution.py:354
  1511.3 2.7 convert_subtract_fusion.2
  1514.0 295.7 %reduce-scatter.20.cloned.1.call-done = bf16[20,32,1536]{2,1,0:T(8,128)(2,1)} async-done(((bf16[20,512,1536]{2,1,0:T(8,128)(2,1)}), bf16[20,32,1536]{2,1,0:T(8,128)(2,1)}) %reduce-scatter.20.cloned.1.call-update) | async-done | bytes 1966096 | tf_op jit(solution)/shard_map/reduce_scatter | solution.py:367
  1809.7 9.4 convert_subtract_fusion.1
  1819.1 566.9 %reduce-scatter.18.cloned.1.call-done = bf16[20,96,1024]{2,1,0:T(8,128)(2,1)} async-done(((bf16[20,1536,1024]{2,1,0:T(8,128)(2,1)}), bf16[20,96,1024]{2,1,0:T(8,128)(2,1)}) %reduce-scatter.18.cloned.1.call-update) | async-done | bytes 3932176 | tf_op jit(solution)/shard_map/reduce_scatter | solution.py:364
  2386.1 18.0 convert_subtract_fusion
  (305 shorter events, 146.8 us)
Async XLA Ops:
  7.2 82.3 %all-gather.8.cloned.1.call-start = ((), (), s32[]{:S(2)}) async-start(), calls=%async_computation.11 | async-start | bytes 8110080 | tf_op jit(solution)/shard_map/all_gather | solution.py:111
  7.9 118.0 %all-gather.10.cloned.1.call-start = ((), (), s32[]{:S(2)}) async-start(), calls=%async_computation.12 | async-start | bytes 1310720 | tf_op jit(solution)/shard_map/all_gather | solution.py:144
  52.3 43.0 %copy-start.27 = (f32[1536]{0:T(1024)}, f32[1536]{0:T(1024)S(1)}, u32[]{:S(2)}) copy-start(f32[1536]{0:T(1024)S(1)} %convert_element_type.155) | copy-start | bytes 18436
  53.2 71.4 %copy-start.15 = (f32[256,64]{0,1:T(8,128)}, f32[256,64]{0,1:T(8,128)S(1)}, u32[]{:S(2)}) copy-start(f32[256,64]{0,1:T(8,128)S(1)} %pad_maximum_fusion.8) | copy-start | bytes 196612
  53.5 71.2 %copy-start.17 = (f32[256,64]{0,1:T(8,128)}, f32[256,64]{0,1:T(8,128)S(1)}, u32[]{:S(2)}) copy-start(f32[256,64]{0,1:T(8,128)S(1)} %pad_maximum_fusion.9) | copy-start | bytes 196612
  54.9 40.4 %copy-start.38 = (f32[256]{0:T(256)}, f32[256]{0:T(256)S(1)}, u32[]{:S(2)}) copy-start(f32[256]{0:T(256)S(1)} %add_rsqrt_fusion.1) | copy-start | bytes 3076
  95.3 9.0 copy-start.13
  104.3 34.4 %all-gather.12.cloned.1.call-start = ((), (), s32[]{:S(2)}) async-start(), calls=%async_computation.13 | async-start | bytes 1310720 | tf_op jit(solution)/shard_map/all_gather | solution.py:145
  105.1 1.8 copy-start.31
  105.1 100.0 %all-gather.14.cloned.1.call-start = ((), (), s32[]{:S(2)}) async-start(), calls=%async_computation.14 | async-start | bytes 4866048 | tf_op jit(solution)/shard_map/all_gather | solution.py:112
  105.7 408.6 %all-gather.16.cloned.1.call-start = ((), (), s32[]{:S(2)}) async-start(), calls=%async_computation.15 | async-start | bytes 66846720 | tf_op jit(solution)/shard_map/all_gather | solution.py:117
  106.3 568.3 %all-gather.18.cloned.1.call-start = ((), (), s32[]{:S(2)}) async-start(), calls=%async_computation.16 | async-start | bytes 33423360 | tf_op jit(solution)/shard_map/all_gather | solution.py:118
  107.2 101.8 %copy-start.29 = (f32[1536]{0:T(1024)}, f32[1536]{0:T(1024)S(1)}, u32[]{:S(2)}) copy-start(f32[1536]{0:T(1024)S(1)} %convert_element_type.163) | copy-start | bytes 18436
  140.9 64.2 %copy-start.2 = (bf16[256,1536]{1,0:T(8,128)(2,1)S(1)}, bf16[256,1536]{1,0:T(8,128)(2,1)}, u32[]{:S(2)}) copy-start(bf16[256,1536]{1,0:T(8,128)(2,1)} %param.29) | copy-start | bytes 2359300
  184.2 24.7 %copy-start.4 = (bf16[8,3,256,64]{2,3,1,0:T(8,128)(2,1)}, bf16[8,3,256,64]{2,3,1,0:T(8,128)(2,1)S(1)}, u32[]{:S(2)}) copy-start(bf16[8,3,256,64]{2,3,1,0:T(8,128)(2,1)S(1)} %get-tuple-element.122) | copy-start | bytes 2359300
  184.2 24.7 %copy-start.12 = (bf16[8,1024,64]{1,2,0:T(8,128)(2,1)}, bf16[8,1024,64]{1,2,0:T(8,128)(2,1)S(1)}, u32[]{:S(2)}) copy-start(bf16[8,1024,64]{1,2,0:T(8,128)(2,1)S(1)} %get-tuple-element.504) | copy-start | bytes 3145732
  184.2 24.7 %copy-start.33 = (s32[256]{0:T(256)}, s32[256]{0:T(256)S(1)}, u32[]{:S(2)}) copy-start(s32[256]{0:T(256)S(1)} %get-tuple-element.529) | copy-start | bytes 3076
  209.0 16.3 copy-start.43
  210.3 66.0 %copy-start.6 = (bf16[256,1536]{1,0:T(8,128)(2,1)}, bf16[256,1536]{1,0:T(8,128)(2,1)S(1)}, u32[]{:S(2)}) copy-start(bf16[256,1536]{1,0:T(8,128)(2,1)S(1)} %multiply_convert_fusion.5) | copy-start | bytes 2359300
  225.3 7.2 copy-start.36
  225.3 50.8 %copy-start.14 = (bf16[256,1536]{1,0:T(8,128)(2,1)S(1)}, bf16[256,1536]{1,0:T(8,128)(2,1)}, u32[]{:S(2)}) copy-start(bf16[256,1536]{1,0:T(8,128)(2,1)} %param.30) | copy-start | bytes 2359300
  225.3 96.4 %all-to-all-start = ((bf16[2,20,64,1536]{3,2,1,0:T(8,128)(2,1)}), bf16[2,20,64,1536]{3,2,1,0:T(8,128)(2,1)}, u32[]{:S(2)}, u32[]{:S(2)}) async-start(bf16[2,20,64,1536]{3,2,1,0:T(8,128)(2,1)} %bitcast.267), calls=%async_computation | async-start | bytes 15728640 | tf_op jit(solution)/shard_map/all_to_all | solution.py:197
  276.1 17.0 copy-start.21
  276.8 16.4 copy-start.40
  277.3 15.8 copy-start.45
  277.5 15.7 copy-start.19
  321.7 94.0 %all-to-all-start.2 = ((bf16[2,20,64,1536]{3,2,1,0:T(8,128)(2,1)}), bf16[2,20,64,1536]{3,2,1,0:T(8,128)(2,1)}, u32[]{:S(2)}, u32[]{:S(2)}) async-start(bf16[2,20,64,1536]{3,2,1,0:T(8,128)(2,1)} %bitcast.268), calls=%async_computation.2 | async-start | bytes 15728640 | tf_op jit(solution)/shard_map/all_to_all | solution.py:241
  732.9 94.4 %all-to-all-start.3 = ((bf16[20,2,64,1536]{3,2,0,1:T(8,128)(2,1)}), bf16[20,2,64,1536]{3,2,0,1:T(8,128)(2,1)}, u32[]{:S(2)}, u32[]{:S(2)}) async-start(bf16[20,2,64,1536]{3,2,0,1:T(8,128)(2,1)} %copy.157), calls=%async_computation.3 | async-start | bytes 15728640 | tf_op jit(solution)/shard_map/all_to_all | solution.py:269
  827.3 93.4 %all-to-all-start.1 = ((bf16[20,2,64,1536]{3,2,0,1:T(8,128)(2,1)}), bf16[20,2,64,1536]{3,2,0,1:T(8,128)(2,1)}, u32[]{:S(2)}, u32[]{:S(2)}) async-start(bf16[20,2,64,1536]{3,2,0,1:T(8,128)(2,1)} %copy.152), calls=%async_computation.1 | async-start | bytes 15728640 | tf_op jit(solution)/shard_map/all_to_all | solution.py:214
  834.1 230.1 %reduce-scatter.10.cloned.1.call-start = ((), (), s32[]{:S(2)}) async-start(), calls=%async_computation.17 | async-start | bytes 1310720 | tf_op jit(solution)/shard_map/reduce_scatter | solution.py:332
  920.7 17.5 copy-start.20
  938.2 9.9 copy-start.26
  938.2 11.5 copy-start.32
  938.2 11.5 copy-start.1
  938.2 11.5 copy-start.22
  938.2 11.5 copy-start.30
  948.0 3.8 copy-start.44
  948.1 3.7 copy-start.9
  954.4 4.0 copy-start.34
  958.4 82.3 %copy-start.7 = (bf16[256,1536]{1,0:T(8,128)(2,1)S(1)}, bf16[256,1536]{1,0:T(8,128)(2,1)}, u32[]{:S(2)}) copy-start(bf16[256,1536]{1,0:T(8,128)(2,1)} %copy-done.6) | copy-start | bytes 2359300
  1040.0 2.2 copy-start.5
  1040.0 51.8 %reduce-scatter.12.cloned.1.call-start = ((), (), s32[]{:S(2)}) async-start(), calls=%async_computation.18 | async-start | bytes 1310720 | tf_op jit(solution)/shard_map/reduce_scatter | solution.py:335
  1040.7 152.3 %reduce-scatter.22.cloned.1.call-start = ((), (), s32[]{:S(2)}) async-start(), calls=%async_computation.23 | async-start | bytes 811008
  1042.1 292.0 %reduce-scatter.16.cloned.1.call-start = ((), (), s32[]{:S(2)}) async-start(), calls=%async_computation.20 | async-start | bytes 9732096 | tf_op jit(solution)/shard_map/reduce_scatter | solution.py:355
  1047.2 1.5 copy-start.18
  1047.2 464.1 %reduce-scatter.14.cloned.1.call-start = ((), (), s32[]{:S(2)}) async-start(), calls=%async_computation.19 | async-start | bytes 16220160 | tf_op jit(solution)/shard_map/reduce_scatter | solution.py:354
  1050.2 41.5 %copy-start.3 = (bf16[256,1536]{1,0:T(8,128)(2,1)S(1)}, bf16[256,1536]{1,0:T(8,128)(2,1)}, u32[]{:S(2)}) copy-start(bf16[256,1536]{1,0:T(8,128)(2,1)} %param.29) | copy-start | bytes 2359300
  1050.2 41.5 %copy-start.28 = (f32[1536]{0:T(1024)S(1)}, f32[1536]{0:T(1024)}, u32[]{:S(2)}) copy-start(f32[1536]{0:T(1024)} %copy-done.27) | copy-start | bytes 18436
  1050.2 41.5 %copy-start.39 = (f32[256]{0:T(256)S(1)}, f32[256]{0:T(256)}, u32[]{:S(2)}) copy-start(f32[256]{0:T(256)} %copy-done.38) | copy-start | bytes 3076
  1100.7 709.0 %reduce-scatter.20.cloned.1.call-start = ((), (), s32[]{:S(2)}) async-start(), calls=%async_computation.22 | async-start | bytes 33423360 | tf_op jit(solution)/shard_map/reduce_scatter | solution.py:367
  1118.1 1268.0 %reduce-scatter.18.cloned.1.call-start = ((), (), s32[]{:S(2)}) async-start(), calls=%async_computation.21 | async-start | bytes 66846720 | tf_op jit(solution)/shard_map/reduce_scatter | solution.py:364
  1146.0 47.8 %copy-start.37 = (bf16[48,40]{0,1:T(8,128)(2,1)S(1)}, bf16[48,40]{0,1:T(8,128)(2,1)}, u32[]{:S(2)}) copy-start(bf16[48,40]{0,1:T(8,128)(2,1)} %param.45) | copy-start | bytes 11524
  1146.0 47.8 %copy-start.41 = (f32[48,40]{0,1:T(8,128)S(1)}, f32[48,40]{0,1:T(8,128)}, u32[]{:S(2)}) copy-start(f32[48,40]{0,1:T(8,128)} %param.47) | copy-start | bytes 23044
  1146.0 47.8 %copy-start.42 = (f32[48,40]{0,1:T(8,128)S(1)}, f32[48,40]{0,1:T(8,128)}, u32[]{:S(2)}) copy-start(f32[48,40]{0,1:T(8,128)} %param.46) | copy-start | bytes 23044
  1193.8 7.6 copy-start.35
  1194.5 47.3 %copy-start.46 = (bf16[48]{0:T(256)(128)(2,1)S(1)}, bf16[48]{0:T(256)(128)(2,1)}, u32[]{:S(2)}) copy-start(bf16[48]{0:T(256)(128)(2,1)} %param.33) | copy-start | bytes 292
  1194.5 47.3 %copy-start.47 = (bf16[48]{0:T(256)(128)(2,1)S(1)}, bf16[48]{0:T(256)(128)(2,1)}, u32[]{:S(2)}) copy-start(bf16[48]{0:T(256)(128)(2,1)} %param.42) | copy-start | bytes 292
  1194.5 47.3 %copy-start.48 = (f32[48]{0:T(128)S(1)}, f32[48]{0:T(128)}, u32[]{:S(2)}) copy-start(f32[48]{0:T(128)} %param.44) | copy-start | bytes 580
  1194.5 47.3 %copy-start.49 = (f32[48]{0:T(128)S(1)}, f32[48]{0:T(128)}, u32[]{:S(2)}) copy-start(f32[48]{0:T(128)} %param.43) | copy-start | bytes 580
  1194.5 47.3 %copy-start.50 = (f32[48]{0:T(128)S(1)}, f32[48]{0:T(128)}, u32[]{:S(2)}) copy-start(f32[48]{0:T(128)} %param.35) | copy-start | bytes 580
  1194.5 47.3 %copy-start.51 = (f32[48]{0:T(128)S(1)}, f32[48]{0:T(128)}, u32[]{:S(2)}) copy-start(f32[48]{0:T(128)} %param.34) | copy-start | bytes 580
  1201.5 132.6 %copy-start.24 = (bf16[48,1536]{1,0:T(8,128)(2,1)S(1)}, bf16[48,1536]{1,0:T(8,128)(2,1)}, u32[]{:S(2)}) copy-start(bf16[48,1536]{1,0:T(8,128)(2,1)} %param.39) | copy-start | bytes 442372
  1242.4 268.8 %copy-start.23 = (bf16[48,2560]{1,0:T(8,128)(2,1)S(1)}, bf16[48,2560]{1,0:T(8,128)(2,1)}, u32[]{:S(2)}) copy-start(bf16[48,2560]{1,0:T(8,128)(2,1)} %param.36) | copy-start | bytes 737284
  1245.4 564.3 %copy-start.8 = (bf16[20,32,1536]{2,1,0:T(8,128)(2,1)S(1)}, bf16[20,32,1536]{2,1,0:T(8,128)(2,1)}, u32[]{:S(2)}) copy-start(bf16[20,32,1536]{2,1,0:T(8,128)(2,1)} %param.51) | copy-start | bytes 5898244
  (5 other events, 6.0 us)
Sparse Core Ops, SparseCore 0:
  10.9 78.5 all-gather.7
  104.4 15.3 all-gather.9
  121.9 16.6 all-gather.11
  141.4 63.6 all-gather.13
  206.5 307.7 all-gather.15
  515.7 158.8 all-gather.17
  1040.1 23.9 reduce-scatter.9
  1066.8 24.8 reduce-scatter.11
  1097.4 95.5 reduce-scatter.21
  1199.3 134.6 reduce-scatter.15
  1341.7 169.5 reduce-scatter.13
  1515.8 293.8 reduce-scatter.19
  1814.5 571.4 reduce-scatter.17
where the time goes:
time: 2420 us; the launch traced here: 2410 us
  waiting for transfers between devices  1740 us (72%)
  matrix products  281 us (12%)
  blocking collectives  126 us (5%)
  other arithmetic  115 us (5%)
  local copies, waits for them, and re-layouts  108 us (4%)
  starting transfers between devices  29.1 us (1%)
    reduce_scatter x1, waiting for transfers between devices, local(): lax.psum_scatter(grad_expert_in.astype(jnp.bfloat16), ('dp', 'ctx'), scat...  567 us
    reduce_scatter x1, waiting for transfers between devices, local(): lax.psum_scatter(grad_expert_out.astype(jnp.bfloat16), ('dp', 'ctx'), sca...  296 us
    reduce_scatter x1, waiting for transfers between devices, local(): lax.psum_scatter(grad_project_in, ('dp', 'expert', 'ctx'), scatter_dimens...  175 us
    all_gather x1, waiting for transfers between devices, local(): lax.all_gather(expert_out, ('dp', 'ctx'), axis=1, tiled=True)  130 us
    all_gather x1, waiting for transfers between devices, local(): lax.all_gather(expert_in, ('dp', 'ctx'), axis=1, tiled=True)  91 us
    reduce_scatter x1, waiting for transfers between devices, local(): lax.psum_scatter(grad_project_out, ('dp', 'expert', 'ctx'), scatter_dimen...  88.6 us
    unnamed x2, blocking collectives  82.9 us
    all_to_all x1, waiting for transfers between devices, local(): lax.all_to_all(outgoing_grad.reshape(owners, local_count, CAP, D), 'exper...  79.3 us
  transfers between devices with their start and end apart: 17, of which 16 were waited for; matrix products, arithmetic and copies ran while one was open for 12% of the time, Pallas kernels for 0%

commit v1 on v0

v1 whole, which is shorter than its diff:
```python
import jax
import jax.numpy as jnp
from jax import lax
from jax.experimental import pallas as pl
from jax.experimental.pallas import tpu as pltpu
from jax.sharding import PartitionSpec as P

D = 1536
H = 24
KV = 8
HD = 64
FFE = 512
EXPERTS = 40
TOP = 8
STEP = 8
CAP = 64


EPS_NORM = 1e-06
ATTN_SCALE = 0.015625
RESIDUAL_SCALE = 0.22
BETA_ONE = 0.9
BETA_TWO = 0.95
ADAM_EPS = 1e-08
DECAY_RATE = 0.1
ROPE_BASE = 10000.0


def normalize(rows):
    factor = lax.rsqrt(jnp.mean(rows * rows, axis=-1, keepdims=True) + EPS_NORM)
    return (rows * factor, factor)


def norm_back(grad_normed, normed, factor):
    return factor * (grad_normed - normed * jnp.mean(grad_normed * normed, axis=-1, keepdims=True))


def learn_rates():
    return (
        0.3,
        3.0 / (D // 16) ** 0.5,
        3.0 / (D // 12) ** 0.5,
        0.3,
        3.0 / (4 * D) ** 0.5,
        3.0 / D**0.5,
        3.0 / (FFE // 32) ** 0.5,
    )


def adam_step(weight, first, second, grad, decay, rate):
    new_first = BETA_ONE * first + (1.0 - BETA_ONE) * grad
    new_second = BETA_TWO * second + (1.0 - BETA_TWO) * grad * grad
    corrected = (
        new_first
        / (1.0 - BETA_ONE**STEP)
        / (jnp.sqrt(new_second / (1.0 - BETA_TWO**STEP)) + ADAM_EPS)
    )
    old = weight.astype(jnp.float32)
    return (grad, new_first, new_second, old - rate * (corrected + decay * old))


def lane_tables(table):
    half = HD // 2
    source = lax.broadcasted_iota(jnp.int32, (128, 128), 0)
    target = lax.broadcasted_iota(jnp.int32, (128, 128), 1)
    same = (source % half) == (target % half)
    group = source // half
    first = (target % HD) < half
    cosine = jnp.where(same & (group < 2), 1.0, 0.0).astype(jnp.bfloat16)
    ahead = jnp.where(same & (group >= 2) & first, -1.0, 0.0).astype(jnp.bfloat16)
    behind = jnp.where(same & (group >= 2) & jnp.logical_not(first), 1.0, 0.0).astype(jnp.bfloat16)
    return tuple(
        jnp.dot(table, item, preferred_element_type=jnp.float32)
        for item in (cosine, ahead, behind)
    )


def turn_lanes(block, tables, sign):
    cosine, ahead, behind = tables
    half = HD // 2
    turned = pltpu.roll(block, 128 - half, 1) * ahead + pltpu.roll(block, half, 1) * behind
    return block * cosine + sign * turned


def scores_of(keys, query, start, length):
    scores = (
        lax.dot_general(
            keys, query, (((1,), (1,)), ((), ())), preferred_element_type=jnp.float32
        )
        * ATTN_SCALE
    )
    rows = lax.broadcasted_iota(jnp.int32, scores.shape, 0)
    columns = lax.broadcasted_iota(jnp.int32, scores.shape, 1) + start
    return jnp.where(rows <= columns, scores, -1e30)


def project_rows(rows_ref, weight, normed_ref, query_ref, keys_ref, values_ref, flipped):
    blocks, block = rows_ref.shape[:2]
    heads, groups = query_ref.shape[0], keys_ref.shape[0]
    wide = heads * HD
    for index in range(blocks):
        span = pl.ds(index * block, block)
        rows = rows_ref[index, :, :D].astype(jnp.float32)
        factor = lax.rsqrt(jnp.mean(rows * rows, axis=-1, keepdims=True) + EPS_NORM)
        normed = (rows * factor).astype(jnp.bfloat16)
        normed_ref[span, :] = normed
        tables = lane_tables(rows_ref[index, :, D : D + 128])
        mixed = jnp.dot(normed, weight, preferred_element_type=jnp.float32)
        for column in range(0, wide + 2 * groups * HD, 128):
            part = mixed[:, column : column + 128]
            if column < wide + groups * HD:
                part = turn_lanes(part, tables, 1.0)
            else:
                flipped[column - wide - groups * HD : column - wide - groups * HD + 128, span] = (
                    part.T.astype(jnp.bfloat16)
                )
            part = part.astype(jnp.bfloat16)
            for half in range(2):
                head = column // HD + half
                piece = part[:, half * HD : (half + 1) * HD]
                if head < heads:
                    query_ref[head, span, :] = piece
                elif head < heads + groups:
                    keys_ref[head - heads, span, :] = piece
                else:
                    values_ref[head - heads - groups, span, :] = piece


def attend_rows(index, block, query_ref, keys_ref, out_ref, flipped):
    heads, groups = query_ref.shape[0], keys_ref.shape[0]
    length = (index + 1) * block
    span = pl.ds(index * block, block)
    outputs = []
    for head in range(heads):
        group = head // (heads // groups)
        scores = scores_of(
            keys_ref[group, :length, :], query_ref[head, span, :], index * block, length
        )
        peak = jnp.max(scores, axis=0, keepdims=True)
        raised = jnp.exp(scores - peak)
        total = jnp.sum(raised, axis=0, keepdims=True)
        probs = (raised * (1.0 / total)).astype(jnp.bfloat16)
        outputs.append(
            jnp.dot(
                flipped[group * HD : (group + 1) * HD, :length],
                probs,
                preferred_element_type=jnp.float32,
            )
        )
    out_ref[index] = jnp.concatenate(outputs, 0).T.astype(jnp.bfloat16)


def attend_kernel(rows_ref, weight_ref, normed_ref, query_ref, keys_ref, values_ref, out_ref, flipped):
    project_rows(rows_ref, weight_ref[...], normed_ref, query_ref, keys_ref, values_ref, flipped)
    for index in range(rows_ref.shape[0]):
        attend_rows(index, rows_ref.shape[1], query_ref, keys_ref, out_ref, flipped)


def attend_shapes(rows, heads, groups):
    blocks, block = rows[:2]
    length = blocks * block
    return (
        jax.ShapeDtypeStruct((length, D), jnp.bfloat16),
        jax.ShapeDtypeStruct((heads, length, HD), jnp.bfloat16),
        jax.ShapeDtypeStruct((groups, length, HD), jnp.bfloat16),
        jax.ShapeDtypeStruct((groups, length, HD), jnp.bfloat16),
        jax.ShapeDtypeStruct((blocks, block, heads * HD), jnp.bfloat16),
    )


def attend_back_kernel(rows_ref, query_ref, keys_ref, values_ref, grad_ref, out_ref, flipped, grad_keys, grad_values):
    block = 256
    blocks = rows_ref.shape[0] // block
    heads, groups = query_ref.shape[0], keys_ref.shape[0]
    repeat = heads // groups
    wide = heads * HD
    for group in range(groups):
        flipped[group * HD : (group + 1) * HD, :] = (
            keys_ref[group].astype(jnp.float32).T.astype(jnp.bfloat16)
        )
    grad_keys[...] = jnp.zeros_like(grad_keys)
    grad_values[...] = jnp.zeros_like(grad_values)
    for index in range(blocks):
        length = (index + 1) * block
        span = pl.ds(index * block, block)
        outputs = []
        for head in range(heads):
            group = head // repeat
            query = query_ref[head, span, :]
            grad = grad_ref[span, head * HD : (head + 1) * HD]
            scores = scores_of(keys_ref[group, :length, :], query, index * block, length)
            peak = jnp.max(scores, axis=0, keepdims=True)
            raised = jnp.exp(scores - peak)
            total = jnp.sum(raised, axis=0, keepdims=True)
            probs = raised * (1.0 / total)
            grad_probs = lax.dot_general(
                values_ref[group, :length, :],
                grad,
                (((1,), (1,)), ((), ())),
                preferred_element_type=jnp.float32,
            )
            middle = jnp.sum(probs * grad_probs, axis=0, keepdims=True)
            grad_scores = (probs * (grad_probs - middle)).astype(jnp.bfloat16)
            grad_keys[group, :length, :] += jnp.dot(
                grad_scores, query, preferred_element_type=jnp.float32
            )
            grad_values[group, :length, :] += jnp.dot(
                probs.astype(jnp.bfloat16), grad, preferred_element_type=jnp.float32
            )
            outputs.append(
                jnp.dot(
                    flipped[group * HD : (group + 1) * HD, :length],
                    grad_scores,
                    preferred_element_type=jnp.float32,
                )
            )
        tables = lane_tables(rows_ref[span, :])
        stacked = jnp.concatenate(outputs, 0).T * ATTN_SCALE
        for column in range(0, wide, 128):
            out_ref[span, column : column + 128] = turn_lanes(
                stacked[:, column : column + 128], tables, -1.0
            ).astype(jnp.bfloat16)
    for index in range(blocks):
        span = pl.ds(index * block, block)
        tables = lane_tables(rows_ref[span, :])
        keys = jnp.concatenate([grad_keys[group, span, :] for group in range(groups)], 1)
        values = jnp.concatenate([grad_values[group, span, :] for group in range(groups)], 1)
        keys = turn_lanes(keys * ATTN_SCALE, tables, -1.0)
        out_ref[span, wide : wide + groups * HD] = keys.astype(jnp.bfloat16)
        out_ref[span, wide + groups * HD :] = values.astype(jnp.bfloat16)


def attend_forward(rows, weight, heads, groups):
    return pl.pallas_call(
        attend_kernel,
        out_shape=attend_shapes(rows.shape, heads, groups),
        scratch_shapes=[pltpu.VMEM((groups * HD, rows.shape[0] * rows.shape[1]), jnp.bfloat16)],
        compiler_params=pltpu.CompilerParams(vmem_limit_bytes=48 * 1024 * 1024),
        cost_estimate=pl.CostEstimate(flops=1, bytes_accessed=1, transcendentals=0),
    )(rows, weight)


def attend_backward(table, query, keys, values, grad):
    heads, length = query.shape[:2]
    groups = keys.shape[0]
    return pl.pallas_call(
        attend_back_kernel,
        out_shape=jax.ShapeDtypeStruct((length, (heads + 2 * groups) * HD), jnp.bfloat16),
        scratch_shapes=[
            pltpu.VMEM((groups * HD, length), jnp.bfloat16),
            pltpu.VMEM((groups, length, HD), jnp.float32),
            pltpu.VMEM((groups, length, HD), jnp.float32),
        ],
        compiler_params=pltpu.CompilerParams(vmem_limit_bytes=48 * 1024 * 1024),
        cost_estimate=pl.CostEstimate(flops=1, bytes_accessed=1, transcendentals=0),
    )(table, query, keys, values, grad)


def dispatch_kernel(first_ref, rows_ref, grads_ref, out_rows, out_grads, out_pick):
    count = out_rows.shape[0]
    tokens = rows_ref.shape[1]
    padded = -(-count // 16) * 16
    tail = rows_ref[0, :, D:]
    lane = lax.broadcasted_iota(jnp.int32, (padded, 128), 1)
    row = lax.broadcasted_iota(jnp.int32, (padded, 128), 0)
    wanted = (lane == 2 * EXPERTS + first_ref[0] + row) & (row < count)
    marks = lax.dot_general(
        wanted.astype(jnp.bfloat16),
        tail,
        (((1,), (1,)), ((), ())),
        preferred_element_type=jnp.float32,
    )
    earlier = lax.broadcasted_iota(jnp.int32, (tokens, tokens), 0) < lax.broadcasted_iota(
        jnp.int32, (tokens, tokens), 1
    )
    rank = jnp.dot(
        marks.astype(jnp.bfloat16),
        earlier.astype(jnp.bfloat16),
        preferred_element_type=jnp.float32,
    )
    slot = lax.broadcasted_iota(jnp.int32, (CAP, tokens), 0).astype(jnp.float32)
    pick = jnp.concatenate(
        [
            jnp.where(
                rank[item : item + 1, :] == slot, marks[item : item + 1, :], 0.0
            ).astype(jnp.bfloat16)
            for item in range(count)
        ],
        0,
    )
    out_pick[0] = pick
    moved = jnp.dot(pick, rows_ref[0], preferred_element_type=jnp.float32).astype(jnp.bfloat16)
    moved_grads = jnp.dot(pick, grads_ref[0], preferred_element_type=jnp.float32).astype(
        jnp.bfloat16
    )
    for item in range(count):
        out_rows[item] = moved[item * CAP : (item + 1) * CAP]
        out_grads[item] = moved_grads[item * CAP : (item + 1) * CAP]


def dispatch(first, rows, grads, count):
    sources, tokens, wide = rows.shape
    return pl.pallas_call(
        dispatch_kernel,
        grid_spec=pltpu.PrefetchScalarGridSpec(
            num_scalar_prefetch=1,
            grid=(sources,),
            in_specs=[
                pl.BlockSpec((1, tokens, wide), lambda s, f: (s, 0, 0)),
                pl.BlockSpec((1, tokens, D), lambda s, f: (s, 0, 0)),
            ],
            out_specs=(
                pl.BlockSpec((count, CAP, wide), lambda s, f: (0, s, 0)),
                pl.BlockSpec((count, CAP, D), lambda s, f: (0, s, 0)),
                pl.BlockSpec((1, count * CAP, tokens), lambda s, f: (s, 0, 0)),
            ),
        ),
        out_shape=(
            jax.ShapeDtypeStruct((count, sources * CAP, wide), jnp.bfloat16),
            jax.ShapeDtypeStruct((count, sources * CAP, D), jnp.bfloat16),
            jax.ShapeDtypeStruct((sources, count * CAP, tokens), jnp.bfloat16),
        ),
        compiler_params=pltpu.CompilerParams(vmem_limit_bytes=40 * 1024 * 1024),
        cost_estimate=pl.CostEstimate(flops=1, bytes_accessed=1, transcendentals=0),
    )(first, rows, grads)


def combine_kernel(pick_ref, rows_ref, out_ref):
    rows = jnp.concatenate([rows_ref[item] for item in range(rows_ref.shape[0])], 0)
    out_ref[0] = lax.dot_general(
        pick_ref[0], rows, (((0,), (0,)), ((), ())), preferred_element_type=jnp.float32
    ).astype(jnp.bfloat16)


def combine(pick, rows):
    sources, slots, tokens = pick.shape
    count, _, wide = rows.shape
    return pl.pallas_call(
        combine_kernel,
        grid=(sources,),
        in_specs=[
            pl.BlockSpec((1, slots, tokens), lambda s: (s, 0, 0)),
            pl.BlockSpec((count, CAP, wide), lambda s: (0, s, 0)),
        ],
        out_specs=pl.BlockSpec((1, tokens, wide), lambda s: (s, 0, 0)),
        out_shape=jax.ShapeDtypeStruct((sources, tokens, wide), jnp.bfloat16),
        compiler_params=pltpu.CompilerParams(vmem_limit_bytes=40 * 1024 * 1024),
        cost_estimate=pl.CostEstimate(flops=1, bytes_accessed=1, transcendentals=0),
    )(pick, rows)


def expert_kernel(first_ref, order_ref, rows_ref, grads_ref, *refs):
    produced_ref, grad_rows_ref, grad_hidden_ref, gated_ref, whole_in, whole_out = refs[-6:]
    pieces = refs[:-6]
    expert = first_ref[0] + pl.program_id(0)

    @pl.when(pl.program_id(1) == 0)
    def assemble():
        if len(pieces) == 2:
            whole_in[...] = pieces[0][0]
            whole_out[...] = pieces[1][0]
            return
        (folded,) = pieces
        deep = folded.shape[2]
        wide = whole_in.shape[1]
        folds = (folded.shape[3] - D) // wide
        for index in range(folded.shape[0]):
            block = order_ref[index]
            for fold in range(folds):
                start = pl.multiple_of((block * folds + fold) * deep, deep)
                whole_in[pl.ds(start, deep), :] = folded[
                    index, 0, :, fold * wide : (fold + 1) * wide
                ]
            start = pl.multiple_of(block * deep, deep)
            whole_out[pl.ds(start, deep), :] = folded[index, 0, :, folds * wide :]

    tail = rows_ref[0, :, D:].astype(jnp.float32)
    lane = lax.broadcasted_iota(jnp.int32, tail.shape, 1)
    own = (lane == expert) | (lane == EXPERTS + expert)
    gate = jnp.sum(jnp.where(own, tail, 0.0), axis=-1, keepdims=True)
    hidden = whole_out.shape[0]
    gate_up = jnp.dot(rows_ref[0, :, :D], whole_in[...], preferred_element_type=jnp.float32)
    gate_half = gate_up[:, :hidden]
    up_half = gate_up[:, hidden:]
    sigma = 1.0 / (1.0 + jnp.exp(-gate_half))
    activated = gate_half * sigma
    middle = activated * up_half
    gated = (gate * middle).astype(jnp.bfloat16)
    gated_ref[0] = gated
    produced_ref[0] = jnp.dot(gated, whole_out[...], preferred_element_type=jnp.float32).astype(
        jnp.bfloat16
    )
    grad_middle = RESIDUAL_SCALE * lax.dot_general(
        grads_ref[0],
        whole_out[...],
        (((1,), (1,)), ((), ())),
        preferred_element_type=jnp.float32,
    )
    grad_gate = jnp.sum(middle * grad_middle, axis=-1, keepdims=True)
    grad_middle = gate * grad_middle
    slope = sigma * (1.0 + gate_half * (1.0 - sigma))
    grad_hidden = jnp.concatenate(
        [grad_middle * up_half * slope, grad_middle * activated], -1
    ).astype(jnp.bfloat16)
    grad_hidden_ref[0] = grad_hidden
    grad_rows_ref[0, :, :D] = lax.dot_general(
        grad_hidden,
        whole_in[...],
        (((1,), (1,)), ((), ())),
        preferred_element_type=jnp.float32,
    ).astype(jnp.bfloat16)
    high = grad_gate.astype(jnp.bfloat16).astype(jnp.float32)
    spread = jnp.where(
        lane == expert, high, jnp.where(lane == EXPERTS + expert, grad_gate - high, 0.0)
    )
    grad_rows_ref[0, :, D:] = spread.astype(jnp.bfloat16)


def run_experts(first, order, rows, grads, pieces, hidden):
    count, slots, wide = rows.shape
    chunk = min(512, slots)
    by_chunk = lambda e, c, *_: (e, c, 0)
    if len(pieces) == 1:
        folded = pieces[0].shape
        piece_specs = [pl.BlockSpec((folded[0], 1) + folded[2:], lambda e, c, *_: (0, e, 0, 0))]
    else:
        piece_specs = [
            pl.BlockSpec((1,) + piece.shape[1:], lambda e, c, *_: (e, 0, 0)) for piece in pieces
        ]
    return pl.pallas_call(
        expert_kernel,
        grid_spec=pltpu.PrefetchScalarGridSpec(
            num_scalar_prefetch=2,
            grid=(count, slots // chunk),
            in_specs=[
                pl.BlockSpec((1, chunk, wide), by_chunk),
                pl.BlockSpec((1, chunk, D), by_chunk),
            ]
            + piece_specs,
            out_specs=(
                pl.BlockSpec((1, chunk, D), by_chunk),
                pl.BlockSpec((1, chunk, wide), by_chunk),
                pl.BlockSpec((1, chunk, 2 * hidden), by_chunk),
                pl.BlockSpec((1, chunk, hidden), by_chunk),
            ),
            scratch_shapes=[
                pltpu.VMEM((D, 2 * hidden), jnp.bfloat16),
                pltpu.VMEM((hidden, D), jnp.bfloat16),
            ],
        ),
        out_shape=(
            jax.ShapeDtypeStruct((count, slots, D), jnp.bfloat16),
            jax.ShapeDtypeStruct((count, slots, wide), jnp.bfloat16),
            jax.ShapeDtypeStruct((count, slots, 2 * hidden), jnp.bfloat16),
            jax.ShapeDtypeStruct((count, slots, hidden), jnp.bfloat16),
        ),
        compiler_params=pltpu.CompilerParams(vmem_limit_bytes=56 * 1024 * 1024),
        cost_estimate=pl.CostEstimate(flops=1, bytes_accessed=1, transcendentals=0),
    )(first, order, rows, grads, *pieces)


def weight_grad_kernel(order_ref, rows_ref, grads_ref, hidden_ref, gated_ref, *refs):
    outs, total_in, total_out = refs[:-2], refs[-2], refs[-1]
    chunk = pl.program_id(1)
    part_in = lax.dot_general(
        rows_ref[0, :, :D],
        hidden_ref[0],
        (((0,), (0,)), ((), ())),
        preferred_element_type=jnp.float32,
    )
    part_out = RESIDUAL_SCALE * lax.dot_general(
        gated_ref[0],
        grads_ref[0],
        (((0,), (0,)), ((), ())),
        preferred_element_type=jnp.float32,
    )

    @pl.when(chunk == 0)
    def store():
        total_in[...] = part_in
        total_out[...] = part_out

    @pl.when(chunk > 0)
    def add():
        total_in[...] += part_in
        total_out[...] += part_out

    @pl.when(chunk == pl.num_programs(1) - 1)
    def finish():
        if len(outs) == 2:
            outs[0][0] = total_in[...].astype(jnp.bfloat16)
            outs[1][0] = total_out[...].astype(jnp.bfloat16)
            return
        wide = total_in.shape[1]
        turns = outs[0].shape[0]
        deep = outs[0].shape[2]
        folds = (outs[0].shape[3] - D) // wide
        for number, out in enumerate(outs):
            for turn in range(turns):
                block = order_ref[number * turns + turn]
                for fold in range(folds):
                    start = pl.multiple_of((block * folds + fold) * deep, deep)
                    out[turn, 0, :, fold * wide : (fold + 1) * wide] = total_in[
                        pl.ds(start, deep), :
                    ].astype(jnp.bfloat16)
                start = pl.multiple_of(block * deep, deep)
                out[turn, 0, :, folds * wide :] = total_out[pl.ds(start, deep), :].astype(
                    jnp.bfloat16
                )


def weight_grads(order, rows, grads, grad_hidden, gated, shapes):
    count, slots, wide = rows.shape
    hidden = gated.shape[2]
    chunk = min(512, slots)
    by_chunk = lambda e, c, *_: (e, c, 0)
    if len(shapes) == 2:
        out_specs = tuple(pl.BlockSpec((1,) + s[1:], lambda e, c, *_: (e, 0, 0)) for s in shapes)
    else:
        out_specs = tuple(
            pl.BlockSpec((s[0], 1) + s[2:], lambda e, c, *_: (0, e, 0, 0)) for s in shapes
        )
    return pl.pallas_call(
        weight_grad_kernel,
        grid_spec=pltpu.PrefetchScalarGridSpec(
            num_scalar_prefetch=1,
            grid=(count, slots // chunk),
            in_specs=[
                pl.BlockSpec((1, chunk, wide), by_chunk),
                pl.BlockSpec((1, chunk, D), by_chunk),
                pl.BlockSpec((1, chunk, 2 * hidden), by_chunk),
                pl.BlockSpec((1, chunk, hidden), by_chunk),
            ],
            out_specs=out_specs,
            scratch_shapes=[
                pltpu.VMEM((D, 2 * hidden), jnp.float32),
                pltpu.VMEM((hidden, D), jnp.float32),
            ],
        ),
        out_shape=tuple(jax.ShapeDtypeStruct(s, jnp.bfloat16) for s in shapes),
        compiler_params=pltpu.CompilerParams(vmem_limit_bytes=56 * 1024 * 1024),
        cost_estimate=pl.CostEstimate(flops=1, bytes_accessed=1, transcendentals=0),
    )(order, rows, grads, grad_hidden, gated)


def swap(rows, axis, flip):
    size = lax.axis_size(axis)
    return lax.ppermute(rows, axis, [(i, i ^ flip) for i in range(size)])


def near(place, axis, flip):
    if lax.axis_size(axis) == 2:
        return 1 - place
    if flip == 1:
        return place + 1 - 2 * lax.rem(place, 2)
    if flip == 2:
        return lax.rem(place + 2, 4)
    return 3 - place


def greet(partners):
    barrier = pltpu.get_barrier_semaphore()
    for axis, flip in partners:
        pl.semaphore_signal(
            barrier,
            inc=1,
            device_id={axis: near(lax.axis_index(axis), axis, flip)},
            device_id_type=pl.DeviceIdType.MESH,
        )
    pl.semaphore_wait(barrier, len(partners))


class Link:
    def __init__(self, sends, receives):
        self.sends, self.receives, self.used, self.started = sends, receives, 0, []

    def push(self, source, target, axis, flip):
        copy = pltpu.make_async_remote_copy(
            src_ref=source,
            dst_ref=target,
            send_sem=self.sends.at[self.used],
            recv_sem=self.receives.at[self.used],
            device_id={axis: near(lax.axis_index(axis), axis, flip)},
            device_id_type=pl.DeviceIdType.MESH,
        )
        copy.start()
        self.used += 1
        self.started.append(copy)
        return copy

    def finish(self):
        for copy in self.started:
            copy.wait_send()


class Line:
    def __init__(self, rows_ref, out_ref, sends, receives):
        z, y = lax.axis_index("dp"), lax.axis_index("expert")
        self.inner = z * (3 - z) > 0
        self.outer = z * (3 - z) < 1

        def slot(flip):
            return 2 * (near(z, "dp", flip) if flip else z) + y

        def hand(sent, received, source, target, flip, axis="dp"):
            return pltpu.make_async_remote_copy(
                src_ref=source,
                dst_ref=target,
                send_sem=sends.at[sent],
                recv_sem=receives.at[received],
                device_id={axis: near(lax.axis_index(axis), axis, flip)},
                device_id_type=pl.DeviceIdType.MESH,
            )

        def block(flip):
            return out_ref.at[slot(flip)]

        self.to_first = hand(0, 1, rows_ref, block(0), 1)
        self.across_own = hand(1, 3, rows_ref, block(0), 3)
        self.across_first = hand(2, 2, block(1), block(1), 3)
        self.pass_third = hand(3, 2, block(3), block(3), 1)
        self.pass_second = hand(8, 3, block(2), block(2), 1)
        self.over = [
            hand(4 + flip, 4 + flip, block(flip) if flip else rows_ref, block(flip), 1, "expert")
            for flip in range(4)
        ]
        self.got = [None] + [hand(0, flip, block(flip), block(flip), 1) for flip in range(1, 4)]
        self.got_over = [
            hand(0, 4 + flip, block(flip), out_ref.at[slot(flip) + 1 - 2 * y], 1, "expert")
            for flip in range(4)
        ]

    def start(self):
        self.to_first.start()

        @pl.when(self.inner)
        def inner():
            self.across_own.start()

        self.over[0].start()

    def first(self):
        self.got[1].wait_recv()

        @pl.when(self.inner)
        def inner():
            self.across_first.start()

        self.over[1].start()

    def second(self):
        @pl.when(self.inner)
        def inner():
            self.got[3].wait_recv()
            self.pass_third.start()
            self.over[3].start()

        @pl.when(self.outer)
        def outer():
            self.got[2].wait_recv()
            self.over[2].start()

    def third(self):
        @pl.when(self.inner)
        def inner():
            self.got[2].wait_recv()
            self.pass_second.start()
            self.over[2].start()

        @pl.when(self.outer)
        def outer():
            self.got[3].wait_recv()
            self.over[3].start()

    def finish(self):
        self.to_first.wait_send()

        @pl.when(self.inner)
        def inner():
            for copy in (self.across_own, self.across_first, self.pass_third, self.pass_second):
                copy.wait_send()

        for copy in self.over:
            copy.wait_send()
        for copy in self.got_over:
            copy.wait_recv()


def gather_kernel(rows_ref, out_ref, sends, receives, local):
    greet([("dp", 1), ("dp", 3), ("expert", 1)])
    own = 2 * lax.axis_index("dp") + lax.axis_index("expert")
    keep = pltpu.make_async_copy(rows_ref, out_ref.at[own], local)
    keep.start()
    line = Line(rows_ref, out_ref, sends, receives)
    line.start()
    line.first()
    line.second()
    line.third()
    line.finish()
    keep.wait()


def gather_owners(rows, number):
    return pl.pallas_call(
        gather_kernel,
        out_shape=jax.ShapeDtypeStruct((8,) + rows.shape, rows.dtype),
        in_specs=[pl.BlockSpec(memory_space=pl.ANY)],
        out_specs=pl.BlockSpec(memory_space=pl.ANY),
        scratch_shapes=[
            pltpu.SemaphoreType.DMA((9,)),
            pltpu.SemaphoreType.DMA((8,)),
            pltpu.SemaphoreType.DMA,
        ],
        compiler_params=pltpu.CompilerParams(collective_id=number, has_side_effects=True),
    )(rows)


def scatter_kernel(blocks_ref, out_ref, over, sums, parts, sends, receives):
    greet([("dp", 1), ("dp", 3), ("expert", 1)])
    z, y = lax.axis_index("dp"), lax.axis_index("expert")
    inner = z * (3 - z) > 0

    def slot(flip, plane):
        return 2 * (near(z, "dp", flip) if flip else z) + plane

    def hand(number, source, target, flip, axis="dp"):
        return pltpu.make_async_remote_copy(
            src_ref=source,
            dst_ref=target,
            send_sem=sends.at[number],
            recv_sem=receives.at[number],
            device_id={axis: near(lax.axis_index(axis), axis, flip)},
            device_id_type=pl.DeviceIdType.MESH,
        )

    across = [
        hand(flip, blocks_ref.at[slot(flip, 1 - y)], over.at[flip], 1, "expert") for flip in range(4)
    ]
    to_line = [hand(4 + k, sums.at[3 - k], parts.at[k], 1) for k in range(3)]
    to_middle = [hand(7 + k, sums.at[2 + k], parts.at[3 + k], 3) for k in range(2)]
    to_end = hand(9, sums.at[1], parts.at[5], 1)

    def fold(flip):
        across[flip].wait_recv()
        return blocks_ref[slot(flip, y)].astype(jnp.float32) + over[flip].astype(jnp.float32)

    def part(number):
        return parts[number].astype(jnp.float32)

    @pl.when(inner)
    def middle():
        for flip in (2, 3, 1, 0):
            across[flip].start()
        second = fold(2)
        to_line[0].wait_recv()
        sums[2] = (second + part(0)).astype(jnp.bfloat16)
        to_middle[0].start()
        third = fold(3)
        to_line[1].wait_recv()
        sums[3] = (third + part(1)).astype(jnp.bfloat16)
        to_middle[1].start()
        first = fold(1)
        to_middle[0].wait_recv()
        sums[1] = (first + part(3)).astype(jnp.bfloat16)
        to_end.start()
        own = fold(0)
        to_line[2].wait_recv()
        to_middle[1].wait_recv()
        out_ref[...] = own + part(2) + part(4)
        to_middle[0].wait_send()
        to_middle[1].wait_send()
        to_end.wait_send()

    @pl.when(jnp.logical_not(inner))
    def ends():
        for flip in (3, 2, 1, 0):
            across[flip].start()
        for k in range(3):
            sums[3 - k] = fold(3 - k).astype(jnp.bfloat16)
            to_line[k].start()
        own = fold(0)
        to_end.wait_recv()
        out_ref[...] = own + part(5)
        for k in range(3):
            to_line[k].wait_send()

    for flip in range(4):
        across[flip].wait_send()


def scatter_owners(blocks, number):
    shape = blocks.shape[1:]
    return pl.pallas_call(
        scatter_kernel,
        out_shape=jax.ShapeDtypeStruct(shape, jnp.float32),
        scratch_shapes=[
            pltpu.VMEM((4,) + shape, jnp.bfloat16),
            pltpu.VMEM((4,) + shape, jnp.bfloat16),
            pltpu.VMEM((6,) + shape, jnp.bfloat16),
            pltpu.SemaphoreType.DMA((10,)),
            pltpu.SemaphoreType.DMA((10,)),
        ],
        compiler_params=pltpu.CompilerParams(
            collective_id=number, has_side_effects=True, vmem_limit_bytes=48 * 1024 * 1024
        ),
    )(blocks)


def opening_kernel(
    rows_ref, columns_ref, pack_ref, weights_ref, grads_ref,
    all_rows, all_columns, all_pack, pieces, all_grads,
    normed_ref, query_ref, keys_ref, values_ref, attended_ref,
    outgoing, flipped, sends, receives, line_sends, line_receives, locals_,
):
    z, y, c = lax.axis_index("dp"), lax.axis_index("expert"), lax.axis_index("ctx")
    greet([("dp", 1), ("dp", 2), ("dp", 3), ("expert", 1), ("ctx", 1), ("ctx", 2), ("ctx", 3)])
    link = Link(sends, receives)
    line = Line(grads_ref, all_grads, line_sends, line_receives)
    own = 2 * z + y
    count = weights_ref.shape[1]

    def z_at(flip):
        return near(z, "dp", flip) if flip else z

    def c_at(flip):
        return near(c, "ctx", flip) if flip else c

    keeps = [
        pltpu.make_async_copy(source, target, locals_.at[number])
        for number, (source, target) in enumerate(
            [
                (columns_ref.at[c], all_columns.at[own, c]),
                (rows_ref, all_rows.at[c]),
                (pack_ref, all_pack.at[z, y, c]),
                (grads_ref, all_grads.at[own]),
                (weights_ref.at[z], pieces.at[0, 0]),
            ]
        )
    ]
    for keep in keeps:
        keep.start()
    cut = [
        link.push(columns_ref.at[c_at(flip)], all_columns.at[own, c], "ctx", flip)
        for flip in (1, 2, 3)
    ]

    def share(*place):
        step, rest = place[0], place[1:]
        source = pieces.at[(step, 0) + rest]
        over = link.push(source, pieces.at[(step, 2) + rest], "ctx", 2)
        core = link.push(source, pieces.at[(step, 1) + rest], "ctx", 1)
        return over, core

    def hand_on(*place):
        step, rest = place[0], place[1:]
        return link.push(pieces.at[(step, 2) + rest], pieces.at[(step, 3) + rest], "ctx", 1)

    moved = {
        step: link.push(weights_ref.at[z_at(step)], pieces.at[step, 0], "dp", step)
        for step in (1, 2)
    }
    line.start()
    keeps[4].wait()
    shared = [share(0)]
    keeps[0].wait()
    for copy in cut:
        copy.wait_recv()
    column_line = [
        link.push(all_columns.at[own], all_columns.at[own], "dp", flip) for flip in (1, 2, 3)
    ]
    column_over = [link.push(all_columns.at[own], all_columns.at[own], "expert", 1)]
    rows_over = link.push(rows_ref, all_rows.at[c], "ctx", 2)
    rows_core = link.push(rows_ref, all_rows.at[c], "ctx", 1)
    pack_line = [link.push(pack_ref, all_pack.at[z, y, c], "dp", flip) for flip in (1, 2, 3)]
    line.first()
    for flip in (1, 2, 3):
        column_line[flip - 1].wait_recv()
        block = all_columns.at[2 * z_at(flip) + y]
        column_over.append(link.push(block, block, "expert", 1))
    rows_over.wait_recv()
    rows_pass = link.push(all_rows.at[c_at(2)], all_rows.at[c_at(2)], "ctx", 1)
    moved[1].wait_recv()
    shared.append(share(1))
    line.second()
    for copy in pack_line:
        copy.wait_recv()
    keeps[2].wait()
    pack_over = link.push(all_pack.at[:, y, c], all_pack.at[:, y, c], "expert", 1)
    for copy in [rows_core, rows_pass] + column_over:
        copy.wait_recv()
    keeps[1].wait()
    project_rows(
        all_rows,
        all_columns[...].reshape(D, all_columns.shape[-1]),
        normed_ref,
        query_ref,
        keys_ref,
        values_ref,
        flipped,
    )
    line.third()
    pack_over.wait_recv()
    pack_pair = link.push(all_pack.at[:, :, c], all_pack.at[:, :, c], "ctx", 2)
    pack_core = link.push(all_pack.at[:, :, c], all_pack.at[:, :, c], "ctx", 1)
    shared[0][0].wait_recv()
    passed = [hand_on(0)]
    moved[2].wait_recv()
    shared.append(share(2))

    def last_piece(item):
        return link.push(weights_ref.at[z_at(3), item], pieces.at[3, 0, item], "dp", 3)

    last = [last_piece(0), last_piece(1)]
    for index in range(all_rows.shape[0]):
        attend_rows(index, all_rows.shape[1], query_ref, keys_ref, outgoing, flipped)
    attended = [
        link.push(outgoing.at[c_at(flip)], attended_ref.at[c], "ctx", flip) for flip in (1, 2, 3)
    ]
    attended_ref[c] = outgoing[c]
    shared[1][0].wait_recv()
    passed.append(hand_on(1))
    for item in range(count):
        last[item].wait_recv()
        if item + 2 < count:
            last.append(last_piece(item + 2))
        shared.append(share(3, item))
    pack_pair.wait_recv()
    pack_last = link.push(all_pack.at[:, :, c_at(2)], all_pack.at[:, :, c_at(2)], "ctx", 1)
    shared[2][0].wait_recv()
    passed.append(hand_on(2))
    for item in range(count):
        shared[3 + item][0].wait_recv()
        passed.append(hand_on(3, item))
    keeps[3].wait()
    for copy in attended + [pack_core, pack_last] + passed:
        copy.wait_recv()
    for over, core in shared:
        core.wait_recv()
    line.finish()
    link.finish()


def opening(rows, columns, pack, weights, grads, heads, groups, number):
    ctx = columns.shape[0]
    shards, count = weights.shape[:2]
    kind = jnp.bfloat16
    copies = 24 + 10 + 4 * count
    far = pl.BlockSpec(memory_space=pl.ANY)
    held = pl.BlockSpec(memory_space=pltpu.VMEM)
    all_rows = (ctx,) + rows.shape
    return pl.pallas_call(
        opening_kernel,
        out_shape=(
            jax.ShapeDtypeStruct(all_rows, kind),
            jax.ShapeDtypeStruct((8,) + columns.shape, kind),
            jax.ShapeDtypeStruct((shards, 2, ctx) + pack.shape, kind),
            jax.ShapeDtypeStruct((shards, ctx) + weights.shape[1:], kind),
            jax.ShapeDtypeStruct((8,) + grads.shape, kind),
        )
        + attend_shapes(all_rows, heads, groups),
        in_specs=[far] * 5,
        out_specs=(held, held, far, far, far) + (held,) * 5,
        scratch_shapes=[
            pltpu.VMEM((ctx, rows.shape[0], heads * HD), kind),
            pltpu.VMEM((groups * HD, ctx * rows.shape[0]), kind),
            pltpu.SemaphoreType.DMA((copies,)),
            pltpu.SemaphoreType.DMA((copies,)),
            pltpu.SemaphoreType.DMA((9,)),
            pltpu.SemaphoreType.DMA((8,)),
            pltpu.SemaphoreType.DMA((5,)),
        ],
        compiler_params=pltpu.CompilerParams(
            collective_id=number, has_side_effects=True, vmem_limit_bytes=48 * 1024 * 1024
        ),
    )(rows, columns, pack, weights, grads)


def split_high_low(values):
    high = values.astype(jnp.bfloat16)
    return high, (values - high.astype(jnp.float32)).astype(jnp.bfloat16)


def pad_columns(like, columns):
    return jnp.zeros((like.shape[0], columns), like.dtype)


def gather_ctx(rows):
    ctx = lax.axis_size("ctx")
    column = lax.axis_index("ctx")
    pieces = {0: rows}
    flip = ctx // 2
    while flip:
        pieces.update({turn ^ flip: swap(item, "ctx", flip) for turn, item in pieces.items()})
        flip //= 2
    out = jnp.zeros((ctx,) + rows.shape, rows.dtype)
    for turn in range(ctx):
        out = lax.dynamic_update_index_in_dim(out, pieces[turn], column ^ turn, 0)
    return out


def exchange_ctx(blocks):
    column = lax.axis_index("ctx")
    out = jnp.zeros(blocks.shape, blocks.dtype)
    for turn in range(blocks.shape[0]):
        item = lax.dynamic_index_in_dim(blocks, column ^ turn, 0, keepdims=False)
        if turn:
            item = swap(item, "ctx", turn)
        out = lax.dynamic_update_index_in_dim(out, item, column ^ turn, 0)
    return out


def scatter_ctx(blocks):
    column = lax.axis_index("ctx")
    flip = 1
    held = blocks
    while flip < lax.axis_size("ctx"):
        pairs = held.reshape((held.shape[0] // 2, 2) + held.shape[1:])
        bit = (column // flip) % 2
        keep = lax.dynamic_index_in_dim(pairs, bit, 1, keepdims=False)
        give = lax.dynamic_index_in_dim(pairs, 1 - bit, 1, keepdims=False)
        held = keep.astype(jnp.float32) + swap(give, "ctx", flip).astype(jnp.float32)
        flip *= 2
        if flip < lax.axis_size("ctx"):
            held = held.astype(jnp.bfloat16)
    return held[0]


def group_columns(rows, ctx):
    depth = rows.shape[0]
    cuts = (rows[:, : H * HD], rows[:, H * HD : (H + KV) * HD], rows[:, (H + KV) * HD :])
    return jnp.concatenate([cut.reshape(depth, ctx, -1) for cut in cuts], -1).transpose(1, 0, 2)


def ungroup_columns(groups):
    ctx, depth, _ = groups.shape
    query, key = H * HD // ctx, KV * HD // ctx
    cuts = (groups[..., :query], groups[..., query : query + key], groups[..., query + key :])
    return jnp.concatenate([cut.transpose(1, 0, 2).reshape(depth, -1) for cut in cuts], 1)


def block_order():
    shards, ctx = lax.axis_size("dp"), lax.axis_size("ctx")
    place, column = lax.axis_index("dp"), lax.axis_index("ctx")
    return place, column, shards, ctx


def fold_weights(expert_in, expert_out):
    deep = expert_out.shape[1]
    folds = expert_in.shape[1] // deep
    cuts = [expert_in[:, fold * deep : (fold + 1) * deep] for fold in range(folds)]
    return jnp.concatenate(cuts + [expert_out], -1)


def piece_order():
    place, column, shards, ctx = block_order()
    blocks = [
        (place ^ step) * ctx + (column ^ turn) for step in range(shards) for turn in range(ctx)
    ]
    return jnp.stack(blocks).astype(jnp.int32)


def spread_weights(expert_in, expert_out):
    shards = lax.axis_size("dp")
    count, depth = expert_in.shape[:2]
    part = FFE // shards
    cut = expert_in.reshape(count, depth, 2, shards, part).transpose(3, 0, 1, 2, 4)
    moved_in = lax.all_to_all(cut, "dp", split_axis=0, concat_axis=0, tiled=True)
    all_in = lax.all_gather(moved_in.transpose(1, 0, 2, 3, 4), "ctx", axis=2, tiled=True)
    all_out = lax.all_gather(expert_out, "ctx", axis=1, tiled=True)
    return [all_in.reshape(count, -1, 2 * part), all_out]


def collect_weights(order, rows, grads, grad_hidden, gated, expert_in, expert_out, close):
    place, column, shards, ctx = block_order()
    depth_in, depth_out = expert_in.shape[1], expert_out.shape[1]
    if close:
        count = expert_in.shape[0] // shards
        folds = depth_in // depth_out
        sent, slots = [], []
        for step in reversed(range(shards)):
            for bit in (1, 0):
                sent.append((ctx // 2, count, depth_out, folds * 2 * FFE + D))
                slots += [step * ctx + turn for turn in range(bit, ctx, 2)]
        order = jnp.stack([order[slot] for slot in slots])
        parts = weight_grads(order, rows, grads, grad_hidden, gated, sent)
        received = []
        for number, step in enumerate(reversed(range(shards))):
            give, keep = parts[2 * number], parts[2 * number + 1]
            flip = 1
            while True:
                total = keep.astype(jnp.float32) + swap(give, "ctx", flip).astype(jnp.float32)
                total = total.astype(jnp.bfloat16)
                flip *= 2
                if flip == ctx:
                    break
                keep, give = total[0::2], total[1::2]
            piece = swap(total[0], "dp", step) if step else total[0]
            received.append((place ^ step, piece))
        return received
    count = expert_in.shape[0]
    part = FFE // shards
    blocks = shards * ctx
    shapes = ((count, blocks * depth_in, 2 * part), (count, part, D))
    grad_in, grad_out = weight_grads(order, rows, grads, grad_hidden, gated, shapes)
    part_in = lax.psum_scatter(
        grad_in.reshape(count, shards, -1, 2, part), "ctx", scatter_dimension=2, tiled=True
    )
    own_in = lax.all_to_all(
        part_in.transpose(1, 0, 2, 3, 4), "dp", split_axis=0, concat_axis=0, tiled=True
    )
    own_in = own_in.transpose(1, 2, 3, 0, 4).reshape(count, -1, 2 * FFE)
    own_out = lax.psum_scatter(grad_out, "ctx", scatter_dimension=1, tiled=True)
    return [(0, fold_weights(own_in, own_out))]


def expert_step_kernel(first_ref, grad_ref, *refs):
    states, outs = refs[:6], refs[-8:]
    wide = states[0].shape[2]
    deep = states[3].shape[1]
    folds = states[0].shape[1] // deep
    rates = learn_rates()
    for fold in range(folds):
        span = pl.ds(fold * deep, deep)
        grad = grad_ref[0, :, fold * wide : (fold + 1) * wide].astype(jnp.float32)
        news = adam_step(
            states[0][0, span, :], states[1][0, span, :], states[2][0, span, :], grad, DECAY_RATE, rates[5]
        )
        for out, new in zip(outs[:4], news):
            out[0, span, :] = new
    grad = grad_ref[0, :, folds * wide :].astype(jnp.float32)
    news = adam_step(states[3][0], states[4][0], states[5][0], grad, DECAY_RATE, rates[6])
    for out, new in zip(outs[4:], news):
        out[0] = new


def expert_step(first, folded, states, outs):
    shapes = [states[1].shape] * 4 + [states[4].shape] * 4
    moved = lambda e, f: (f[0] + e, 0, 0)
    block = lambda shape: pl.BlockSpec((1,) + shape[1:], moved)
    begun = [] if outs is None else list(outs)
    return pl.pallas_call(
        expert_step_kernel,
        grid_spec=pltpu.PrefetchScalarGridSpec(
            num_scalar_prefetch=1,
            grid=(folded.shape[0],),
            in_specs=[pl.BlockSpec((1,) + folded.shape[1:], lambda e, f: (e, 0, 0))]
            + [block(state.shape) for state in states]
            + [pl.BlockSpec(memory_space=pl.ANY) for _ in begun],
            out_specs=tuple(block(shape) for shape in shapes),
        ),
        out_shape=tuple(jax.ShapeDtypeStruct(shape, jnp.float32) for shape in shapes),
        input_output_aliases={8 + index: index for index in range(len(begun))},
        compiler_params=pltpu.CompilerParams(vmem_limit_bytes=40 * 1024 * 1024),
        cost_estimate=pl.CostEstimate(flops=1, bytes_accessed=1, transcendentals=0),
    )(first, folded, *states, *begun)


def local(
    tokens,
    cotangent,
    routes,
    positions,
    gain_attend,
    gain_attend_mean,
    gain_attend_square,
    project_in,
    project_in_mean,
    project_in_square,
    project_out,
    project_out_mean,
    project_out_square,
    gain_expert,
    gain_expert_mean,
    gain_expert_square,
    router_weight,
    router_weight_mean,
    router_weight_square,
    expert_in,
    expert_in_mean,
    expert_in_square,
    expert_out,
    expert_out_mean,
    expert_out_square,
):
    everywhere = ("dp", "expert", "ctx")
    owners = ("dp", "expert")
    shards = lax.axis_size("dp")
    planes = lax.axis_size("expert")
    ctx = lax.axis_size("ctx")
    rows_local = tokens.shape[0]
    local_count = expert_in.shape[0]
    close = (shards, planes, ctx) == (4, 2, 4) and local_count % shards == 0
    heads, groups = H // ctx, KV // ctx
    hidden_in = tokens.astype(jnp.float32)

    half = HD // 2
    freqs = ROPE_BASE ** (-jnp.arange(half, dtype=jnp.float32) * 2.0 / HD)
    angles = positions.astype(jnp.float32)[:, None] * freqs[None, :]
    table = jnp.concatenate(split_high_low(jnp.cos(angles)) + split_high_low(jnp.sin(angles)), 1)
    gain_attend_wide = gain_attend.astype(jnp.float32)[:, None]
    scaled_in = (gain_attend_wide * project_in.astype(jnp.float32)).astype(jnp.bfloat16)
    rows = jnp.concatenate([tokens, table], 1)
    columns = group_columns(scaled_in, ctx)
    pack_out = jnp.concatenate(
        [project_out, router_weight, gain_expert[:, None], pad_columns(project_out, 87)], 1
    )
    order = piece_order()
    if close:
        folded = fold_weights(expert_in, expert_out)
        folded = folded.reshape((shards, -1) + folded.shape[1:])
        (
            seq_rows, own_in, full_pack_out, pieces, all_grads,
            seq_normed, query, keys, values, attended,
        ) = opening(rows, columns, pack_out, folded, cotangent, heads, groups, 1)
        pieces = [pieces.reshape((-1,) + pieces.shape[2:])]
    else:
        seq_rows = gather_ctx(rows)
        own_in = lax.all_gather(exchange_ctx(columns), owners, axis=0, tiled=False)
        full_pack_out = lax.all_gather(pack_out, everywhere, axis=0, tiled=True)
        all_grads = lax.all_gather(cotangent, owners, axis=0, tiled=False)
        pieces = spread_weights(expert_in, expert_out)
        seq_normed, query, keys, values, seq_attended = attend_forward(
            seq_rows, own_in.reshape(D, -1), heads, groups
        )
        attended = exchange_ctx(seq_attended)
    seq_rows = seq_rows.reshape(-1, D + 128)
    own_in = own_in.reshape(D, -1)
    full_pack_out = full_pack_out.reshape(H * HD, -1)
    full_out = full_pack_out[:, :D]
    full_router = full_pack_out[:, D : D + EXPERTS]
    gain_two = full_pack_out[:, D + EXPERTS].astype(jnp.float32)

    attended = attended.transpose(1, 0, 2).reshape(rows_local, H * HD)
    branch = jnp.dot(attended, full_out, preferred_element_type=jnp.float32)
    after = hidden_in + RESIDUAL_SCALE * branch
    normed_two, factor_two = normalize(after)
    expert_input = (normed_two * gain_two).astype(jnp.bfloat16)
    logits = jnp.dot(expert_input, full_router, preferred_element_type=jnp.float32)
    chosen = jnp.any(routes[:, :, None] == jnp.arange(EXPERTS, dtype=jnp.int32), axis=1)
    peak = jnp.max(jnp.where(chosen, logits, -3e38), axis=-1, keepdims=True)
    raised = jnp.where(chosen, jnp.exp(jnp.where(chosen, logits - peak, 0.0)), 0.0)
    gates = raised / jnp.sum(raised, axis=-1, keepdims=True)
    packed = jnp.concatenate(
        (expert_input,)
        + split_high_low(gates)
        + (chosen.astype(jnp.bfloat16), pad_columns(expert_input, 128 - 3 * EXPERTS)),
        1,
    )
    if close:
        all_packed = gather_owners(packed, 2)
    else:
        all_packed = lax.all_gather(packed, owners, axis=0, tiled=False)

    first = lax.axis_index("expert") * local_count
    count = local_count
    hidden = FFE // shards
    if close:
        count = local_count // shards
        hidden = FFE
        first = first + lax.axis_index("dp") * count
    first = first.astype(jnp.int32).reshape(1)
    slot_rows, slot_grads, pick = dispatch(first, all_packed, all_grads, count)
    produced, grad_rows, grad_hidden, gated = run_experts(
        first, order, slot_rows, slot_grads, pieces, hidden
    )
    shared_grads = combine(pick, grad_rows)
    if close:
        grad_routed = scatter_owners(shared_grads, 3)
    else:
        grad_routed = lax.psum_scatter(
            shared_grads, owners, scatter_dimension=0, tiled=False
        ).astype(jnp.float32)
    expert_grads = collect_weights(
        order, slot_rows, slot_grads, grad_hidden, gated, expert_in, expert_out, close
    )
    produced, grad_routed = lax.optimization_barrier((produced, grad_routed))
    moe = lax.psum_scatter(
        combine(pick, produced), owners, scatter_dimension=0, tiled=False
    ).astype(jnp.float32)
    block_output = (after + RESIDUAL_SCALE * moe).astype(jnp.bfloat16)

    grad_final = cotangent.astype(jnp.float32)
    grad_gates = grad_routed[:, D : D + EXPERTS] + grad_routed[:, D + EXPERTS : D + 2 * EXPERTS]
    grad_picked = gates * (grad_gates - jnp.sum(gates * grad_gates, axis=-1, keepdims=True))
    grad_logits = grad_picked.astype(jnp.bfloat16)
    grad_from_router = jnp.einsum(
        "te,de->td", grad_logits, full_router, preferred_element_type=jnp.float32
    )
    grad_input = grad_from_router + grad_routed[:, :D]
    grad_after = grad_final + norm_back(grad_input * gain_two, normed_two, factor_two)
    grad_branch = (RESIDUAL_SCALE * grad_after).astype(jnp.bfloat16)
    grad_attended = jnp.einsum(
        "td,cd->tc", grad_branch, full_out, preferred_element_type=jnp.float32
    ).astype(jnp.bfloat16)
    seq_grad = exchange_ctx(
        grad_attended.reshape(rows_local, ctx, heads * HD).transpose(1, 0, 2)
    ).reshape(ctx * rows_local, heads * HD)
    grad_mixed = attend_backward(seq_rows[:, D:], query, keys, values, seq_grad)
    grad_in_part = jnp.einsum(
        "td,tc->dc", seq_normed, grad_mixed, preferred_element_type=jnp.float32
    ).astype(jnp.bfloat16)
    grad_in_part = grad_in_part.reshape(shards * planes, -1, grad_in_part.shape[1])
    if close:
        shard_columns = scatter_owners(grad_in_part, 4).astype(jnp.bfloat16)
    else:
        shard_columns = lax.psum_scatter(
            grad_in_part, owners, scatter_dimension=0, tiled=False
        )
    shard_scaled = ungroup_columns(
        exchange_ctx(shard_columns.reshape(ctx, -1, shard_columns.shape[-1]))
    ).astype(jnp.float32)
    shard_in = gain_attend_wide * shard_scaled
    shard_attend = jnp.sum(shard_scaled * project_in.astype(jnp.float32), axis=1)
    grad_scaled = jnp.einsum(
        "tc,dc->td", grad_mixed, own_in, preferred_element_type=jnp.float32
    ).astype(jnp.bfloat16)
    grad_normed = scatter_ctx(grad_scaled.reshape(ctx, rows_local, D))
    normed_one, factor_one = normalize(hidden_in)
    input_grad = grad_after + norm_back(grad_normed, normed_one, factor_one)

    grad_project_out = jnp.einsum(
        "tc,td->cd", attended, grad_branch, preferred_element_type=jnp.float32
    ).astype(jnp.bfloat16)
    ones = jnp.where(jnp.arange(128) == EXPERTS, 1.0, 0.0).astype(jnp.bfloat16)
    grad_small = jnp.einsum(
        "td,te->de",
        jnp.concatenate([expert_input, (grad_input * normed_two).astype(jnp.bfloat16)], 0),
        jnp.concatenate(
            [
                jnp.pad(grad_logits, ((0, 0), (0, 128 - EXPERTS))),
                jnp.broadcast_to(ones, (rows_local, 128)),
            ],
            0,
        ),
        preferred_element_type=jnp.float32,
    ).astype(jnp.bfloat16)
    grad_pack_out = jnp.concatenate([grad_project_out, grad_small], 1)
    shard_pack_out = lax.psum_scatter(
        grad_pack_out, everywhere, scatter_dimension=0, tiled=True
    ).astype(jnp.float32)
    shard_out = shard_pack_out[:, :D]
    shard_router = shard_pack_out[:, D : D + EXPERTS]
    shard_expert = shard_pack_out[:, D + EXPERTS]
    rates = learn_rates()
    results = [block_output, input_grad]
    results.extend(
        adam_step(gain_attend, gain_attend_mean, gain_attend_square, shard_attend, 0.0, rates[0])
    )
    results.extend(
        adam_step(project_in, project_in_mean, project_in_square, shard_in, DECAY_RATE, rates[1])
    )
    results.extend(
        adam_step(
            project_out, project_out_mean, project_out_square, shard_out, DECAY_RATE, rates[2]
        )
    )
    results.extend(
        adam_step(gain_expert, gain_expert_mean, gain_expert_square, shard_expert, 0.0, rates[3])
    )
    results.extend(
        adam_step(
            router_weight,
            router_weight_mean,
            router_weight_square,
            shard_router,
            DECAY_RATE,
            rates[4],
        )
    )
    states = (expert_in, expert_in_mean, expert_in_square, expert_out, expert_out_mean, expert_out_square)
    expert_outs = None
    for place, folded in expert_grads:
        base = jnp.asarray(place * folded.shape[0], jnp.int32).reshape(1)
        expert_outs = expert_step(base, folded, states, expert_outs)
    results.extend(expert_outs)
    return tuple(results)


def solution(mesh):
    placed = (
        P(("dp", "expert", "ctx"), None),
        P(("dp", "expert", "ctx"), None),
        P(("dp", "expert", "ctx"), None),
        P(("dp", "expert", "ctx")),
        P(("dp", "expert", "ctx")),
        P(("dp", "expert", "ctx")),
        P(("dp", "expert", "ctx")),
        P(("dp", "expert", "ctx"), None),
        P(("dp", "expert", "ctx"), None),
        P(("dp", "expert", "ctx"), None),
        P(("dp", "expert", "ctx"), None),
        P(("dp", "expert", "ctx"), None),
        P(("dp", "expert", "ctx"), None),
        P(("dp", "expert", "ctx")),
        P(("dp", "expert", "ctx")),
        P(("dp", "expert", "ctx")),
        P(("dp", "expert", "ctx"), None),
        P(("dp", "expert", "ctx"), None),
        P(("dp", "expert", "ctx"), None),
        P("expert", ("dp", "ctx"), None),
        P("expert", ("dp", "ctx"), None),
        P("expert", ("dp", "ctx"), None),
        P("expert", ("dp", "ctx"), None),
        P("expert", ("dp", "ctx"), None),
        P("expert", ("dp", "ctx"), None),
    )
    return jax.shard_map(
        local,
        mesh=mesh,
        in_specs=placed,
        out_specs=(
            P(("dp", "expert", "ctx"), None),
            P(("dp", "expert", "ctx"), None),
            P(("dp", "expert", "ctx")),
            P(("dp", "expert", "ctx")),
            P(("dp", "expert", "ctx")),
            P(("dp", "expert", "ctx")),
            P(("dp", "expert", "ctx"), None),
            P(("dp", "expert", "ctx"), None),
            P(("dp", "expert", "ctx"), None),
            P(("dp", "expert", "ctx"), None),
            P(("dp", "expert", "ctx"), None),
            P(("dp", "expert", "ctx"), None),
            P(("dp", "expert", "ctx"), None),
            P(("dp", "expert", "ctx"), None),
            P(("dp", "expert", "ctx")),
            P(("dp", "expert", "ctx")),
            P(("dp", "expert", "ctx")),
            P(("dp", "expert", "ctx")),
            P(("dp", "expert", "ctx"), None),
            P(("dp", "expert", "ctx"), None),
            P(("dp", "expert", "ctx"), None),
            P(("dp", "expert", "ctx"), None),
            P("expert", ("dp", "ctx"), None),
            P("expert", ("dp", "ctx"), None),
            P("expert", ("dp", "ctx"), None),
            P("expert", ("dp", "ctx"), None),
            P("expert", ("dp", "ctx"), None),
            P("expert", ("dp", "ctx"), None),
            P("expert", ("dp", "ctx"), None),
            P("expert", ("dp", "ctx"), None),
        ),
        check_vma=False,
    )
```

time: 2420 us -> 951 us (0.39)
  waiting for transfers between devices: 1740 us -> 89.7 us
  Pallas kernels: 0 us -> 666 us
  matrix products: 281 us -> 23.7 us
  blocking collectives: 126 us -> 0 us
  other arithmetic: 115 us -> 50.8 us
  local copies, waits for them, and re-layouts: 108 us -> 71.1 us
    reduce_scatter x6 -> x2, waiting for transfers between devices: 1170 us -> 0.01 us  [the longest x1 0.01 us: local(): lax.psum_scatter(combine(pick, produced), owners, scatter_dimension=0, ti...]
    pallas_call x0 -> x14, Pallas kernels: none -> 666 us  [the longest x1 273 us: opening(): pl.pallas_call(opening_kernel, out_shape=(jax.ShapeDtypeStruct(all_rows,...]
    all_gather x6 -> x0, waiting for transfers between devices: 288 us -> none  [the longest x1 130 us: local(): lax.all_gather(expert_out, ('dp', 'ctx'), axis=1, tiled=True)]
    dot_general x65 -> x3, matrix products: 265 us -> 5.95 us  [the longest x1 2.88 us: local(): jnp.einsum('tc,dc->td', grad_mixed, own_in, preferred_element_type=jnp.fl...]
    all_to_all x4 -> x0, waiting for transfers between devices: 232 us -> none  [the longest x1 79.3 us: local(): lax.all_to_all(outgoing_grad.reshape(owners, local_count, CAP, D), 'exper...]
    ppermute x0 -> x19, waiting for transfers between devices: none -> 89.7 us  [swap(): return lax.ppermute(rows, axis, [(i, i ^ flip) for i in range(size)])]
    unnamed x2 -> x0, blocking collectives: 82.9 us -> none
    unnamed x14 -> x2, waiting for transfers between devices: 49.9 us -> 0.03 us
  transfers between devices with their start and end apart: 17 -> 21, of which waited for: 16 -> 4; matrix products, arithmetic and copies ran while one was open for 12% -> 9% of each run, Pallas kernels for 0% -> 18%
where the time goes in v1:
time: 951 us; the launch traced here: 938 us
  Pallas kernels  666 us (70%)
  waiting for transfers between devices  89.7 us (9%)
  local copies, waits for them, and re-layouts  71.1 us (7%)
  other arithmetic  50.8 us (5%)
  matrix products  23.7 us (2%)
  starting transfers between devices  21.2 us (2%)
  between operations  15.4 us (2%)
    pallas_call x1, Pallas kernels, opening(): pl.pallas_call(opening_kernel, out_shape=(jax.ShapeDtypeStruct(all_rows,...  273 us
    pallas_call x2, Pallas kernels, scatter_owners(): pl.pallas_call(scatter_kernel, out_shape=jax.ShapeDtypeStruct(shape, jnp....  177 us
    ppermute x19, waiting for transfers between devices, swap(): return lax.ppermute(rows, axis, [(i, i ^ flip) for i in range(size)])  89.7 us
    pallas_call x1, Pallas kernels, gather_owners(): pl.pallas_call(gather_kernel, out_shape=jax.ShapeDtypeStruct((8,) + rows....  79.9 us
    unnamed x134, local copies, waits for them, and re-layouts  39.2 us
    pallas_call x4, Pallas kernels, expert_step(): pl.pallas_call(expert_step_kernel, grid_spec=pltpu.PrefetchScalarGridSpec...  34.9 us
    pallas_call x1, Pallas kernels, run_experts(): pl.pallas_call(expert_kernel, grid_spec=pltpu.PrefetchScalarGridSpec(num_...  34.2 us
    pallas_call x1, Pallas kernels, weight_grads(): pl.pallas_call(weight_grad_kernel, grid_spec=pltpu.PrefetchScalarGridSpec...  22.9 us
  transfers between devices with their start and end apart: 21, of which 4 were waited for; matrix products, arithmetic and copies ran while one was open for 9% of the time, Pallas kernels for 18%

profile of v1, /device:TPU:0, one launch (start us, length us, event | category | flops | bytes accessed | tf_op | source)
XLA Modules:
  0.0 938.2 jit_solution(8959193872560738793)
XLA Ops:
  12.4 4.3 fusion.74
  18.1 5.1 pad_maximum_fusion
  25.6 273.4 %shard_map.472 = (bf16[4,256,1664]{2,1,0:T(8,128)(2,1)}, bf16[8,4,48,640]{3,2,1,0:T(8,128)(2,1)}, bf16[4,2,4,48,1664]{4,3,2,1,0:T(8,128)(2,1)}, bf16[4,4,5,32,46...) custom-call(bf16[256,1664]{1,0:T(8,128)(2,1)S(1)} %concatenate.27.ro, ...), custom_call_target="tpu_custom_call" | custom-call | tf_op jit(solution)/shard_map/pallas_call | solution.py:951
  304.1 1.4 slice.120
  305.8 4.1 multiply_reduce_fusion.1
  311.3 1.6 select_reduce_fusion
  315.1 79.9 %shard_map.473.rows_ref = bf16[8,256,1664]{2,1,0:T(8,128)(2,1)} custom-call(bf16[256,1664]{1,0:T(8,128)(2,1)} %concatenate.31.rows_ref), custom_call_target="tpu_custom_call" | custom-call | tf_op jit(solution)/shard_map/pallas_call | solution.py:704
  395.0 2.9 copy-done.3
  398.0 2.8 copy-done.7
  400.7 10.0 %shard_map.474 = (bf16[5,512,1664]{2,1,0:T(8,128)(2,1)}, bf16[5,512,1536]{2,1,0:T(8,128)(2,1)}, bf16[8,320,256]{2,1,0:T(8,128)(2,1)S(1)}) custom-call(s32[1]{0:T(128)} %bitcast.6.first_ref, bf16[8,256,1664]{2,1,0:T(8,128)(2,1)S(1)} %copy-done.3, bf16[8,256,1536]{2,1,0:T(8,128)(2,1)S(1)} %copy-done.7), custom_call_target="tpu_custom_call" | custom-call | flops 1 | bytes 1 | tf_op jit(solution)/shard_map/pallas_call | solution.py:303
  411.3 34.2 %shard_map.475 = (bf16[5,512,1536]{2,1,0:T(8,128)(2,1)}, bf16[5,512,1664]{2,1,0:T(8,128)(2,1)}, bf16[5,512,1024]{2,1,0:T(8,128)(2,1)}, bf16[5,512,512]{2,1,0:T(8,128)(2,1)}) custom-call(s32[1]{0:T(128)} %bitcast.6.first_ref, s32[16]{0:T(128)} %stack.70.order_ref, bf16[5,512,1664]{2,1,0:T(8,128)(2,1)} %get-tuple-element.93.rows_ref, ...), custom_call_target="tpu_custom_call" | custom-call | flops 1 | bytes 1 | tf_op jit(solution)/shard_map/pallas_call | solution.py:430
  445.5 8.5 shard_map.476.blocks_ref
  454.1 2.9 copy-done.4
  456.9 79.4 %shard_map.477 = f32[256,1664]{1,0:T(8,128)S(1)} custom-call(bf16[8,256,1664]{2,1,0:T(8,128)(2,1)} %copy-done.4), custom_call_target="tpu_custom_call" | custom-call | tf_op jit(solution)/shard_map/pallas_call | solution.py:793
  537.6 8.1 shard_map.478
  545.7 2.7 copy-done.5
  549.1 22.9 %shard_map.481 = (bf16[2,5,32,4608]{3,2,1,0:T(8,128)(2,1)}, bf16[2,5,32,4608]{3,2,1,0:T(8,128)(2,1)}, bf16[2,5,32,4608]{3,2,1,0:T(8,128)(2,1)}, bf16[2,5,32,4608...) custom-call(s32[16]{0:T(128)} %stack.71.order_ref, ...), custom_call_target="tpu_custom_call" | custom-call | flops 1 | bytes 1 | tf_op jit(solution)/shard_map/pallas_call | solution.py:523
  573.0 1.4 copy.222
  574.4 1.4 copy.223
  575.8 1.7 slice.122.rows_ref
  579.2 1.4 fusion.20
  582.1 3.2 multiply_reduce_fusion
  585.2 2.9 add_convert_fusion.3
  589.4 2.9 collective-permute-start.9
  592.3 2.7 add_convert_fusion.2
  595.1 2.2 collective-permute-start.11
  597.4 2.8 add_convert_fusion.1
  600.3 1.7 collective-permute-start.14
  602.0 2.7 add_convert_fusion
  606.0 1.7 collective-permute-start.17
  607.7 49.4 %collective-permute-done.11 = bf16[1,5,32,4608]{3,2,1,0:T(8,128)(2,1)S(1)} collective-permute-done((bf16[1,5,32,4608]{3,2,1,0:T(8,128)(2,1)S(1)}, bf16[1,5,32,4608]{3,2,1,0:T(8,128)(2,1)S(1)}, u32[]{:S(2)}, u32[]{:S(2)}) %collective-permute-start.11) | collective-permute-done | bytes 1474592 | tf_op jit(solution)/shard_map/ppermute | solution.py:548
  657.1 1.4 fusion.26
  659.3 29.5 %collective-permute-done.14 = bf16[1,5,32,4608]{3,2,1,0:T(8,128)(2,1)S(1)} collective-permute-done((bf16[1,5,32,4608]{3,2,1,0:T(8,128)(2,1)S(1)}, bf16[1,5,32,4608]{3,2,1,0:T(8,128)(2,1)S(1)}, u32[]{:S(2)}, u32[]{:S(2)}) %collective-permute-start.14) | collective-permute-done | bytes 1474592 | tf_op jit(solution)/shard_map/ppermute | solution.py:548
  688.7 1.4 fusion.27
  691.1 3.9 multiply_convert_fusion
  695.0 5.3 fusion.11
  700.2 3.6 convolution_convert_fusion
  703.8 2.1 reshape.194
  706.0 2.4 constant_dynamic-slice_fusion.1
  711.0 2.6 pad_maximum_fusion.1
  713.6 7.8 copy.229
  722.7 2.1 collective-permute-start.1
  725.8 4.8 collective-permute-done.1
  731.9 5.9 collective-permute-done.2
  740.9 17.6 %shard_map.479 = bf16[1024,640]{1,0:T(8,128)(2,1)S(1)} custom-call(bf16[1024,128]{1,0:T(8,128)(2,1)S(1)} %copy-done.12, bf16[6,1024,64]{2,1,0:T(8,128)(2,1)S(1)} %copy-done.11, bf16[2,1024,64]{2,1,0:T(8,128)(2,1)S(1)} %copy-done.15, bf16[2,1024,64]{2,1,0:T(8,128)(2,1)S(1)} %copy-done.17, bf16[1024,384]{1,0:T(8,128)(2,1)S(1)} %bitcast.119), custom_call_target="tpu_custom_call" | custom-call | flops 1 | bytes 1 | tf_op jit(solution)/shard_map/pallas_call | solution.py:246
  758.5 2.9 convolution_convert_fusion.1
  763.2 1.8 fusion.28
  765.0 2.3 collective-permute-start.18
  767.2 2.7 convolution_convert_fusion.2
  769.9 97.5 %shard_map.480 = f32[192,640]{1,0:T(8,128)S(1)} custom-call(bf16[8,192,640]{2,1,0:T(8,128)(2,1)S(1)} %bitcast.120), custom_call_target="tpu_custom_call" | custom-call | tf_op jit(solution)/shard_map/pallas_call | solution.py:793
  869.0 1.9 collective-permute-start.6
  871.1 1.7 collective-permute-start.4
  872.7 1.8 fusion.25.grad_ref
  874.5 8.4 shard_map.482
  882.9 9.1 shard_map.483
  891.9 9.1 shard_map.484
  901.0 8.4 shard_map.485
  909.9 2.0 dynamic_update_slice.31
  911.9 2.0 dynamic_update_slice.32
  914.0 2.0 dynamic_update_slice.33
  916.2 3.0 convert_subtract_fusion
  920.4 1.6 fusion.16
  922.2 1.6 fusion.19
  929.0 2.2 convert_subtract_fusion.1
  (222 shorter events, 48.3 us)
Async XLA Ops:
  7.2 683.9 %reduce-scatter.5.cloned.1.call-start = ((), (), s32[]{:S(2)}) async-start(), calls=%async_computation.2 | async-start | bytes 7077888 | tf_op jit(solution)/shard_map/reduce_scatter | solution.py:1277
  11.4 6.5 copy-start.44
  12.3 5.6 copy-start.40
  12.4 5.7 copy-start.2
  304.1 5.8 copy-start.32
  311.2 83.8 %copy-start.30 = (bf16[256,1536]{1,0:T(8,128)(2,1)}, bf16[256,1536]{1,0:T(8,128)(2,1)S(1)}, u32[]{:S(2)}) copy-start(bf16[256,1536]{1,0:T(8,128)(2,1)S(1)} %multiply_convert_fusion.2) | copy-start | bytes 2359300
  395.0 2.9 copy-start.3
  398.0 2.8 copy-start.7
  454.1 2.9 copy-start.4
  548.4 375.4 %reduce-scatter.7.cloned.1.call-start = ((), (), s32[]{:S(2)}) async-start(), calls=%async_computation.3 | async-start | bytes 5271552 | tf_op jit(solution)/shard_map/reduce_scatter | solution.py:1338
  571.9 10.1 %copy-start.20 = (f32[256,1536]{1,0:T(8,128)S(1)}, f32[256,1536]{1,0:T(8,128)}, u32[]{:S(2)}) copy-start(f32[256,1536]{1,0:T(8,128)} %copy-done.19) | copy-start | bytes 4718596
  571.9 13.3 %collective-permute-start.8 = (bf16[2,5,32,4608]{3,2,1,0:T(8,128)(2,1)}, bf16[2,5,32,4608]{3,2,1,0:T(8,128)(2,1)}, u32[]{:S(2)}, u32[]{:S(2)}) collective-permute-start(bf16[2,5,32,4608]{3,2,1,0:T(8,128)(2,1)} %get-tuple-element.109), channel_id=1, source_target_pairs={{0,1},{1,0},{2,3},{3,2},{4,5},{5,4},{6,7},{7,6},{8,9},{9,8},{10,11... | collective-permute-start | bytes 8847368 | tf_op jit(solution)/shard_map/ppermute | solution.py:548
  572.0 20.3 %collective-permute-start.10 = (bf16[2,5,32,4608]{3,2,1,0:T(8,128)(2,1)}, bf16[2,5,32,4608]{3,2,1,0:T(8,128)(2,1)}, u32[]{:S(2)}, u32[]{:S(2)}) collective-permute-start(bf16[2,5,32,4608]{3,2,1,0:T(8,128)(2,1)} %get-tuple-element.111), channel_id=1, source_target_pairs={{0,1},{1,0},{2,3},{3,2},{4,5},{5,4},{6,7},{7,6},{8,9},{9,8},{10,11... | collective-permute-start | bytes 8847368 | tf_op jit(solution)/shard_map/ppermute | solution.py:548
  572.5 24.8 %collective-permute-start.13 = (bf16[2,5,32,4608]{3,2,1,0:T(8,128)(2,1)}, bf16[2,5,32,4608]{3,2,1,0:T(8,128)(2,1)}, u32[]{:S(2)}, u32[]{:S(2)}) collective-permute-start(bf16[2,5,32,4608]{3,2,1,0:T(8,128)(2,1)} %get-tuple-element.113), channel_id=1, source_target_pairs={{0,1},{1,0},{2,3},{3,2},{4,5},{5,4},{6,7},{7,6},{8,9},{9,8},{10,11... | collective-permute-start | bytes 8847368 | tf_op jit(solution)/shard_map/ppermute | solution.py:548
  572.6 29.4 %collective-permute-start.16 = (bf16[2,5,32,4608]{3,2,1,0:T(8,128)(2,1)}, bf16[2,5,32,4608]{3,2,1,0:T(8,128)(2,1)}, u32[]{:S(2)}, u32[]{:S(2)}) collective-permute-start(bf16[2,5,32,4608]{3,2,1,0:T(8,128)(2,1)} %get-tuple-element.115), channel_id=1, source_target_pairs={{0,1},{1,0},{2,3},{3,2},{4,5},{5,4},{6,7},{7,6},{8,9},{9,8},{10,11... | collective-permute-start | bytes 8847368 | tf_op jit(solution)/shard_map/ppermute | solution.py:548
  580.7 4.6 copy-start.37
  582.1 3.2 copy-start.42
  588.1 6.9 copy-start.24
  588.1 4.2 copy-start.36
  589.4 279.6 %collective-permute-start.9 = (bf16[1,5,32,4608]{3,2,1,0:T(8,128)(2,1)}, bf16[1,5,32,4608]{3,2,1,0:T(8,128)(2,1)}, u32[]{:S(2)}, u32[]{:S(2)}) collective-permute-start(bf16[1,5,32,4608]{3,2,1,0:T(8,128)(2,1)} %slice.130), channel_id=1, source_target_pairs={{0,2},{1,3},{2,0},{3,1},{4,6},{5,7},{6,4},{7,5},{8,10},{9,11},{10,... | collective-permute-start | bytes 4423688 | tf_op jit(solution)/shard_map/ppermute | solution.py:548
  595.1 62.0 %collective-permute-start.11 = (bf16[1,5,32,4608]{3,2,1,0:T(8,128)(2,1)S(1)}, bf16[1,5,32,4608]{3,2,1,0:T(8,128)(2,1)S(1)}, u32[]{:S(2)}, u32[]{:S(2)}) collective-permute-start(bf16[1,5,32,4608]{3,2,1,0:T(8,128)(2,1)S(1)} %slice.132), channel_id=1, source_target_pairs={{0,2},{1,3},{2,0},{3,1},{4,6},{5,7},{6,4},{7,5},{8,10},{9,11},{10,... | collective-permute-start | bytes 4423688 | tf_op jit(solution)/shard_map/ppermute | solution.py:548
  600.3 88.5 %collective-permute-start.14 = (bf16[1,5,32,4608]{3,2,1,0:T(8,128)(2,1)S(1)}, bf16[1,5,32,4608]{3,2,1,0:T(8,128)(2,1)S(1)}, u32[]{:S(2)}, u32[]{:S(2)}) collective-permute-start(bf16[1,5,32,4608]{3,2,1,0:T(8,128)(2,1)S(1)} %slice.134), channel_id=1, source_target_pairs={{0,2},{1,3},{2,0},{3,1},{4,6},{5,7},{6,4},{7,5},{8,10},{9,11},{10,... | collective-permute-start | bytes 4423688 | tf_op jit(solution)/shard_map/ppermute | solution.py:548
  604.7 53.9 %copy-start.26 = (bf16[2,5,32,4608]{3,2,1,0:T(8,128)(2,1)}, bf16[2,5,32,4608]{3,2,1,0:T(8,128)(2,1)S(1)}, u32[]{:S(2)}) copy-start(bf16[2,5,32,4608]{3,2,1,0:T(8,128)(2,1)S(1)} %add_convert_fusion) | copy-start | bytes 8847364
  606.0 156.1 %collective-permute-start.17 = (bf16[1,5,32,4608]{3,2,1,0:T(8,128)(2,1)}, bf16[1,5,32,4608]{3,2,1,0:T(8,128)(2,1)}, u32[]{:S(2)}, u32[]{:S(2)}) collective-permute-start(bf16[1,5,32,4608]{3,2,1,0:T(8,128)(2,1)} %slice.136), channel_id=1, source_target_pairs={{0,2},{1,3},{2,0},{3,1},{4,6},{5,7},{6,4},{7,5},{8,10},{9,11},{10,... | collective-permute-start | bytes 4423688 | tf_op jit(solution)/shard_map/ppermute | solution.py:548
  658.6 32.5 %copy-start.9 = (bf16[256,1536]{1,0:T(8,128)(2,1)S(1)}, bf16[256,1536]{1,0:T(8,128)(2,1)}, u32[]{:S(2)}) copy-start(bf16[256,1536]{1,0:T(8,128)(2,1)} %grads_ref.1) | copy-start | bytes 2359300
  658.6 233.3 %collective-permute-start.12 = (bf16[5,32,4608]{2,1,0:T(8,128)(2,1)}, bf16[5,32,4608]{2,1,0:T(8,128)(2,1)}, u32[]{:S(2)}, u32[]{:S(2)}) collective-permute-start(bf16[5,32,4608]{2,1,0:T(8,128)(2,1)} %fusion.26), channel_id=1, source_target_pairs={{0,8},{8,0},{16,24},{24,16},{1,9},{9,1},{17,25},{25,17},{2,10},{10... | collective-permute-start | bytes 4423688 | tf_op jit(solution)/shard_map/ppermute | solution.py:548
  690.2 180.7 %collective-permute-start.15 = (bf16[5,32,4608]{2,1,0:T(8,128)(2,1)}, bf16[5,32,4608]{2,1,0:T(8,128)(2,1)}, u32[]{:S(2)}, u32[]{:S(2)}) collective-permute-start(bf16[5,32,4608]{2,1,0:T(8,128)(2,1)} %fusion.27), channel_id=1, source_target_pairs={{0,16},{8,24},{16,0},{24,8},{1,17},{9,25},{17,1},{25,9},{2,18},{10... | collective-permute-start | bytes 4423688 | tf_op jit(solution)/shard_map/ppermute | solution.py:548
  694.9 5.3 copy-start.21
  695.0 5.3 copy-start.33
  703.8 6.7 copy-start.53
  703.8 6.7 copy-start.31
  706.0 4.5 copy-start.39
  706.0 4.5 copy-start.43
  710.5 12.2 %collective-permute-start = (bf16[256,384]{1,0:T(8,128)(2,1)}, bf16[256,384]{1,0:T(8,128)(2,1)}, u32[]{:S(2)}, u32[]{:S(2)}) collective-permute-start(bf16[256,384]{1,0:T(8,128)(2,1)} %bitcast.115), channel_id=1, source_target_pairs={{0,1},{1,0},{2,3},{3,2},{4,5},{5,4},{6,7},{7,6},{8,9},{9,8},{10,11... | collective-permute-start | bytes 589832 | tf_op jit(solution)/shard_map/ppermute | solution.py:548
  721.4 16.4 %copy-start.11 = (bf16[6,1024,64]{2,1,0:T(8,128)(2,1)S(1)}, bf16[6,1024,64]{2,1,0:T(8,128)(2,1)}, u32[]{:S(2)}) copy-start(bf16[6,1024,64]{2,1,0:T(8,128)(2,1)} %copy-done.10) | copy-start | bytes 2359300
  721.4 37.1 %copy-start.58 = (bf16[8,4,48,640]{3,2,1,0:T(8,128)(2,1)S(1)}, bf16[8,4,48,640]{3,2,1,0:T(8,128)(2,1)}, u32[]{:S(2)}) copy-start(bf16[8,4,48,640]{3,2,1,0:T(8,128)(2,1)} %get-tuple-element.104) | copy-start | bytes 5898244
  722.7 7.9 collective-permute-start.1
  730.6 7.1 collective-permute-start.2
  761.5 5.7 copy-start.57
  761.5 106.0 %collective-permute-start.3 = (bf16[2,256,1536]{2,1,0:T(8,128)(2,1)S(1)}, bf16[2,256,1536]{2,1,0:T(8,128)(2,1)S(1)}, u32[]{:S(2)}, u32[]{:S(2)}) collective-permute-start(bf16[2,256,1536]{2,1,0:T(8,128)(2,1)S(1)} %dynamic-slice_bitcast_fusion), channel_id=1, source_target_pairs={{0,1},{1,0},{2,3},{3,2},{4,5},{5,4},{6,7},{7,6},{8,9},{9,8},{10,11... | collective-permute-start | bytes 4718600 | tf_op jit(solution)/shard_map/ppermute | solution.py:548
  765.0 106.1 %collective-permute-start.18 = (bf16[5,32,4608]{2,1,0:T(8,128)(2,1)S(1)}, bf16[5,32,4608]{2,1,0:T(8,128)(2,1)S(1)}, u32[]{:S(2)}, u32[]{:S(2)}) collective-permute-start(bf16[5,32,4608]{2,1,0:T(8,128)(2,1)S(1)} %fusion.28), channel_id=1, source_target_pairs={{0,24},{8,16},{16,8},{24,0},{1,25},{9,17},{17,9},{25,1},{2,26},{10... | collective-permute-start | bytes 4423688 | tf_op jit(solution)/shard_map/ppermute | solution.py:548
  867.4 5.3 copy-start.25
  867.5 42.0 %collective-permute-start.7 = (bf16[48,640]{1,0:T(8,128)(2,1)S(1)}, bf16[48,640]{1,0:T(8,128)(2,1)S(1)}, u32[]{:S(2)}, u32[]{:S(2)}) collective-permute-start(bf16[48,640]{1,0:T(8,128)(2,1)S(1)} %get-tuple-element.361), channel_id=1, source_target_pairs={{0,3},{1,2},{2,1},{3,0},{4,7},{5,6},{6,5},{7,4},{8,11},{9,10},{10,... | collective-permute-start | bytes 184328 | tf_op jit(solution)/shard_map/ppermute | solution.py:548
  867.6 6.9 copy-start.1
  868.0 6.5 copy-start.28
  868.0 6.5 copy-start
  869.0 40.7 %collective-permute-start.6 = (bf16[48,640]{1,0:T(8,128)(2,1)S(1)}, bf16[48,640]{1,0:T(8,128)(2,1)S(1)}, u32[]{:S(2)}, u32[]{:S(2)}) collective-permute-start(bf16[48,640]{1,0:T(8,128)(2,1)S(1)} %get-tuple-element.362), channel_id=1, source_target_pairs={{0,2},{1,3},{2,0},{3,1},{4,6},{5,7},{6,4},{7,5},{8,10},{9,11},{10,... | collective-permute-start | bytes 184328 | tf_op jit(solution)/shard_map/ppermute | solution.py:548
  870.9 38.9 %collective-permute-start.5 = (bf16[48,640]{1,0:T(8,128)(2,1)S(1)}, bf16[48,640]{1,0:T(8,128)(2,1)S(1)}, u32[]{:S(2)}, u32[]{:S(2)}) collective-permute-start(bf16[48,640]{1,0:T(8,128)(2,1)S(1)} %get-tuple-element.363), channel_id=1, source_target_pairs={{0,1},{1,0},{2,3},{3,2},{4,5},{5,4},{6,7},{7,6},{8,9},{9,8},{10,11... | collective-permute-start | bytes 184328 | tf_op jit(solution)/shard_map/ppermute | solution.py:548
  871.1 49.4 %collective-permute-start.4 = (bf16[1,256,1536]{2,1,0:T(8,128)(2,1)}, bf16[1,256,1536]{2,1,0:T(8,128)(2,1)S(1)}, u32[]{:S(2)}, u32[]{:S(2)}) collective-permute-start(bf16[1,256,1536]{2,1,0:T(8,128)(2,1)} %constant_dynamic-slice_fusion), channel_id=1, source_target_pairs={{0,2},{1,3},{2,0},{3,1},{4,6},{5,7},{6,4},{7,5},{8,10},{9,11},{10,... | collective-permute-start | bytes 2359304 | tf_op jit(solution)/shard_map/ppermute | solution.py:548
  901.0 15.2 %copy-start.49 = (f32[48]{0:T(128)S(1)}, f32[48]{0:T(128)}, u32[]{:S(2)}) copy-start(f32[48]{0:T(128)} %copy-done.48) | copy-start | bytes 580
  909.4 6.8 copy-start.38
  909.5 9.7 %copy-start.54 = (bf16[48]{0:T(256)(128)(2,1)S(1)}, bf16[48]{0:T(256)(128)(2,1)}, u32[]{:S(2)}) copy-start(bf16[48]{0:T(256)(128)(2,1)} %param.29) | copy-start | bytes 292
  909.5 10.9 %copy-start.23 = (bf16[256,1536]{1,0:T(8,128)(2,1)S(1)}, bf16[256,1536]{1,0:T(8,128)(2,1)}, u32[]{:S(2)}) copy-start(bf16[256,1536]{1,0:T(8,128)(2,1)} %param.25) | copy-start | bytes 2359300
  916.2 5.9 copy-start.22
  916.2 5.9 copy-start.29
  919.2 4.6 copy-start.50
  922.1 4.2 copy-start.45
  922.1 4.2 copy-start.46
  922.1 4.2 copy-start.47
  922.1 6.3 copy-start.51
  922.1 6.3 copy-start.55
  922.1 6.3 copy-start.56
  922.1 6.9 copy-start.41
  926.3 4.8 copy-start.52
  (16 other events, 24.2 us)
Sparse Core Ops, SparseCore 0:
  548.5 118.8 reduce-scatter.4
  721.5 142.6 reduce-scatter.6

commit v2 on v1

--- a/solution.py
+++ b/solution.py
@@ -1,3 +1,5 @@
+import functools
+
 import jax
 import jax.numpy as jnp
 from jax import lax
@@ -168,7 +170,7 @@
     )
 
 
-def attend_back_kernel(rows_ref, query_ref, keys_ref, values_ref, grad_ref, out_ref, flipped, grad_keys, grad_values):
+def attend_back(rows_ref, query_ref, keys_ref, values_ref, grad_ref, out_ref, flipped, grad_keys, grad_values):
     block = 256
     blocks = rows_ref.shape[0] // block
     heads, groups = query_ref.shape[0], keys_ref.shape[0]
@@ -187,7 +189,7 @@
         for head in range(heads):
             group = head // repeat
             query = query_ref[head, span, :]
-            grad = grad_ref[span, head * HD : (head + 1) * HD]
+            grad = grad_ref[index, :, head * HD : (head + 1) * HD]
             scores = scores_of(keys_ref[group, :length, :], query, index * block, length)
             peak = jnp.max(scores, axis=0, keepdims=True)
             raised = jnp.exp(scores - peak)
@@ -244,7 +246,7 @@
     heads, length = query.shape[:2]
     groups = keys.shape[0]
     return pl.pallas_call(
-        attend_back_kernel,
+        attend_back,
         out_shape=jax.ShapeDtypeStruct((length, (heads + 2 * groups) * HD), jnp.bfloat16),
         scratch_shapes=[
             pltpu.VMEM((groups * HD, length), jnp.bfloat16),
@@ -320,7 +322,7 @@
             jax.ShapeDtypeStruct((count, sources * CAP, D), jnp.bfloat16),
             jax.ShapeDtypeStruct((sources, count * CAP, tokens), jnp.bfloat16),
         ),
-        compiler_params=pltpu.CompilerParams(vmem_limit_bytes=40 * 1024 * 1024),
+        compiler_params=pltpu.CompilerParams(vmem_limit_bytes=62 * 1024 * 1024),
         cost_estimate=pl.CostEstimate(flops=1, bytes_accessed=1, transcendentals=0),
     )(first, rows, grads)
 
@@ -344,7 +346,7 @@
         ],
         out_specs=pl.BlockSpec((1, tokens, wide), lambda s: (s, 0, 0)),
         out_shape=jax.ShapeDtypeStruct((sources, tokens, wide), jnp.bfloat16),
-        compiler_params=pltpu.CompilerParams(vmem_limit_bytes=40 * 1024 * 1024),
+        compiler_params=pltpu.CompilerParams(vmem_limit_bytes=62 * 1024 * 1024),
         cost_estimate=pl.CostEstimate(flops=1, bytes_accessed=1, transcendentals=0),
     )(pick, rows)
 
@@ -356,23 +358,15 @@
 
     @pl.when(pl.program_id(1) == 0)
     def assemble():
-        if len(pieces) == 2:
+        if len(pieces[0].shape) == 3:
             whole_in[...] = pieces[0][0]
             whole_out[...] = pieces[1][0]
             return
-        (folded,) = pieces
-        deep = folded.shape[2]
-        wide = whole_in.shape[1]
-        folds = (folded.shape[3] - D) // wide
-        for index in range(folded.shape[0]):
+        for index in range(pieces[0].shape[0]):
             block = order_ref[index]
-            for fold in range(folds):
-                start = pl.multiple_of((block * folds + fold) * deep, deep)
-                whole_in[pl.ds(start, deep), :] = folded[
-                    index, 0, :, fold * wide : (fold + 1) * wide
-                ]
-            start = pl.multiple_of(block * deep, deep)
-            whole_out[pl.ds(start, deep), :] = folded[index, 0, :, folds * wide :]
+            for piece, whole in zip(pieces, (whole_in, whole_out)):
+                deep = piece.shape[2]
+                whole[pl.ds(pl.multiple_of(block * deep, deep), deep), :] = piece[index, 0]
 
     tail = rows_ref[0, :, D:].astype(jnp.float32)
     lane = lax.broadcasted_iota(jnp.int32, tail.shape, 1)
@@ -420,9 +414,11 @@
     count, slots, wide = rows.shape
     chunk = min(512, slots)
     by_chunk = lambda e, c, *_: (e, c, 0)
-    if len(pieces) == 1:
-        folded = pieces[0].shape
-        piece_specs = [pl.BlockSpec((folded[0], 1) + folded[2:], lambda e, c, *_: (0, e, 0, 0))]
+    if len(pieces[0].shape) == 4:
+        piece_specs = [
+            pl.BlockSpec((piece.shape[0], 1) + piece.shape[2:], lambda e, c, *_: (0, e, 0, 0))
+            for piece in pieces
+        ]
     else:
         piece_specs = [
             pl.BlockSpec((1,) + piece.shape[1:], lambda e, c, *_: (e, 0, 0)) for piece in pieces
@@ -454,7 +450,7 @@
             jax.ShapeDtypeStruct((count, slots, 2 * hidden), jnp.bfloat16),
             jax.ShapeDtypeStruct((count, slots, hidden), jnp.bfloat16),
         ),
-        compiler_params=pltpu.CompilerParams(vmem_limit_bytes=56 * 1024 * 1024),
+        compiler_params=pltpu.CompilerParams(vmem_limit_bytes=62 * 1024 * 1024),
         cost_estimate=pl.CostEstimate(flops=1, bytes_accessed=1, transcendentals=0),
     )(first, order, rows, grads, *pieces)
 
@@ -538,7 +534,7 @@
             ],
         ),
         out_shape=tuple(jax.ShapeDtypeStruct(s, jnp.bfloat16) for s in shapes),
-        compiler_params=pltpu.CompilerParams(vmem_limit_bytes=56 * 1024 * 1024),
+        compiler_params=pltpu.CompilerParams(vmem_limit_bytes=62 * 1024 * 1024),
         cost_estimate=pl.CostEstimate(flops=1, bytes_accessed=1, transcendentals=0),
     )(order, rows, grads, grad_hidden, gated)
 
@@ -686,138 +682,548 @@
             copy.wait_recv()
 
 
-def gather_kernel(rows_ref, out_ref, sends, receives, local):
-    greet([("dp", 1), ("dp", 3), ("expert", 1)])
-    own = 2 * lax.axis_index("dp") + lax.axis_index("expert")
-    keep = pltpu.make_async_copy(rows_ref, out_ref.at[own], local)
-    keep.start()
-    line = Line(rows_ref, out_ref, sends, receives)
-    line.start()
-    line.first()
-    line.second()
-    line.third()
-    line.finish()
-    keep.wait()
-
-
-def gather_owners(rows, number):
-    return pl.pallas_call(
-        gather_kernel,
-        out_shape=jax.ShapeDtypeStruct((8,) + rows.shape, rows.dtype),
-        in_specs=[pl.BlockSpec(memory_space=pl.ANY)],
-        out_specs=pl.BlockSpec(memory_space=pl.ANY),
-        scratch_shapes=[
-            pltpu.SemaphoreType.DMA((9,)),
-            pltpu.SemaphoreType.DMA((8,)),
-            pltpu.SemaphoreType.DMA,
-        ],
-        compiler_params=pltpu.CompilerParams(collective_id=number, has_side_effects=True),
-    )(rows)
-
-
-def scatter_kernel(blocks_ref, out_ref, over, sums, parts, sends, receives):
-    greet([("dp", 1), ("dp", 3), ("expert", 1)])
-    z, y = lax.axis_index("dp"), lax.axis_index("expert")
-    inner = z * (3 - z) > 0
-
-    def slot(flip, plane):
-        return 2 * (near(z, "dp", flip) if flip else z) + plane
-
-    def hand(number, source, target, flip, axis="dp"):
-        return pltpu.make_async_remote_copy(
-            src_ref=source,
-            dst_ref=target,
-            send_sem=sends.at[number],
-            recv_sem=receives.at[number],
-            device_id={axis: near(lax.axis_index(axis), axis, flip)},
-            device_id_type=pl.DeviceIdType.MESH,
-        )
-
-    across = [
-        hand(flip, blocks_ref.at[slot(flip, 1 - y)], over.at[flip], 1, "expert") for flip in range(4)
+class Fold:
+    def __init__(self, blocks_ref, out_ref, over, sums, parts, sends, receives):
+        z, y = lax.axis_index("dp"), lax.axis_index("expert")
+        self.inner = z * (3 - z) > 0
+        self.outer = z * (3 - z) < 1
+        self.blocks, self.out, self.over, self.sums, self.parts = blocks_ref, out_ref, over, sums, parts
+        self.y = y
+
+        def slot(flip, plane):
+            return 2 * (near(z, "dp", flip) if flip else z) + plane
+
+        def hand(number, source, target, flip, axis="dp"):
+            return pltpu.make_async_remote_copy(
+                src_ref=source,
+                dst_ref=target,
+                send_sem=sends.at[number],
+                recv_sem=receives.at[number],
+                device_id={axis: near(lax.axis_index(axis), axis, flip)},
+                device_id_type=pl.DeviceIdType.MESH,
+            )
+
+        self.slot = slot
+        self.across = [
+            hand(flip, blocks_ref.at[slot(flip, 1 - y)], over.at[flip], 1, "expert")
+            for flip in range(4)
+        ]
+        self.to_line = [hand(4 + k, sums.at[3 - k], parts.at[k], 1) for k in range(3)]
+        self.to_middle = [hand(7 + k, sums.at[2 + k], parts.at[3 + k], 3) for k in range(2)]
+        self.to_end = hand(9, sums.at[1], parts.at[5], 1)
+
+    def own(self, flip):
+        self.across[flip].wait_recv()
+        return self.blocks[self.slot(flip, self.y)].astype(jnp.float32) + self.over[flip].astype(
+            jnp.float32
+        )
+
+    def part(self, number):
+        return self.parts[number].astype(jnp.float32)
+
+    def start(self):
+        @pl.when(self.inner)
+        def inner():
+            for flip in (2, 3, 1, 0):
+                self.across[flip].start()
+
+        @pl.when(self.outer)
+        def outer():
+            for flip in (3, 2, 1, 0):
+                self.across[flip].start()
+
+    def early(self, k):
+        @pl.when(self.inner)
+        def inner():
+            total = self.own(2 + k)
+            self.to_line[k].wait_recv()
+            self.sums[2 + k] = (total + self.part(k)).astype(jnp.bfloat16)
+            self.to_middle[k].start()
+
+        @pl.when(self.outer)
+        def outer():
+            self.sums[3 - k] = self.own(3 - k).astype(jnp.bfloat16)
+            self.to_line[k].start()
+
+    def late(self):
+        @pl.when(self.inner)
+        def inner():
+            total = self.own(1)
+            self.to_middle[0].wait_recv()
+            self.sums[1] = (total + self.part(3)).astype(jnp.bfloat16)
+            self.to_end.start()
+
+        @pl.when(self.outer)
+        def outer():
+            self.sums[1] = self.own(1).astype(jnp.bfloat16)
+            self.to_line[2].start()
+
+    def last(self):
+        @pl.when(self.inner)
+        def inner():
+            total = self.own(0)
+            self.to_line[2].wait_recv()
+            self.to_middle[1].wait_recv()
+            self.out[...] = (total + self.part(2) + self.part(4)).astype(self.out.dtype)
+
+        @pl.when(self.outer)
+        def outer():
+            total = self.own(0)
+            self.to_end.wait_recv()
+            self.out[...] = (total + self.part(5)).astype(self.out.dtype)
+
+    def finish(self):
+        @pl.when(self.inner)
+        def inner():
+            for copy in self.to_middle + [self.to_end]:
+                copy.wait_send()
+
+        @pl.when(self.outer)
+        def outer():
+            for copy in self.to_line:
+                copy.wait_send()
+
+        for copy in self.across:
+            copy.wait_send()
+
+
+def fold_scratch(shape):
+    return [
+        pltpu.VMEM((4,) + shape, jnp.bfloat16),
+        pltpu.VMEM((4,) + shape, jnp.bfloat16),
+        pltpu.VMEM((6,) + shape, jnp.bfloat16),
+        pltpu.SemaphoreType.DMA((10,)),
+        pltpu.SemaphoreType.DMA((10,)),
     ]
-    to_line = [hand(4 + k, sums.at[3 - k], parts.at[k], 1) for k in range(3)]
-    to_middle = [hand(7 + k, sums.at[2 + k], parts.at[3 + k], 3) for k in range(2)]
-    to_end = hand(9, sums.at[1], parts.at[5], 1)
-
-    def fold(flip):
-        across[flip].wait_recv()
-        return blocks_ref[slot(flip, y)].astype(jnp.float32) + over[flip].astype(jnp.float32)
-
-    def part(number):
-        return parts[number].astype(jnp.float32)
-
-    @pl.when(inner)
-    def middle():
-        for flip in (2, 3, 1, 0):
-            across[flip].start()
-        second = fold(2)
-        to_line[0].wait_recv()
-        sums[2] = (second + part(0)).astype(jnp.bfloat16)
-        to_middle[0].start()
-        third = fold(3)
-        to_line[1].wait_recv()
-        sums[3] = (third + part(1)).astype(jnp.bfloat16)
-        to_middle[1].start()
-        first = fold(1)
-        to_middle[0].wait_recv()
-        sums[1] = (first + part(3)).astype(jnp.bfloat16)
-        to_end.start()
-        own = fold(0)
-        to_line[2].wait_recv()
-        to_middle[1].wait_recv()
-        out_ref[...] = own + part(2) + part(4)
-        to_middle[0].wait_send()
-        to_middle[1].wait_send()
-        to_end.wait_send()
-
-    @pl.when(jnp.logical_not(inner))
-    def ends():
-        for flip in (3, 2, 1, 0):
-            across[flip].start()
-        for k in range(3):
-            sums[3 - k] = fold(3 - k).astype(jnp.bfloat16)
-            to_line[k].start()
-        own = fold(0)
-        to_end.wait_recv()
-        out_ref[...] = own + part(5)
-        for k in range(3):
-            to_line[k].wait_send()
-
-    for flip in range(4):
-        across[flip].wait_send()
-
-
-def scatter_owners(blocks, number):
+
+
+def add_into(target, sources):
+    def body(item, carry):
+        total = sources[0][item].astype(jnp.float32)
+        for source in sources[1:]:
+            total = total + source[item].astype(jnp.float32)
+        target[item] = total.astype(jnp.bfloat16)
+        return carry
+
+    lax.fori_loop(0, target.shape[0], body, 0)
+
+
+def fetch(pairs, local):
+    copies = [
+        pltpu.make_async_copy(source, target, local.at[number])
+        for number, (source, target) in enumerate(pairs)
+    ]
+    for copy in copies:
+        copy.start()
+    for copy in copies:
+        copy.wait()
+
+
+EVERYONE = [("dp", 1), ("dp", 2), ("dp", 3), ("expert", 1), ("ctx", 1), ("ctx", 2), ("ctx", 3)]
+
+
+def returning_kernel(
+    blocks_ref, give3, keep3, give2, keep2, give1, keep1, give0,
+    after_ref, input_ref, gates_ref, grad_ref, gain_ref, pack_ref, attended_ref,
+    grad_after_ref, seq_grad_ref, grad_pack_ref, arrived, done3, ready2, ready1,
+    routed, over, sums, parts, fold_sends, fold_receives,
+    sent, crossed, stage, outgoing, sends, receives, local,
+):
+    z, c = lax.axis_index("dp"), lax.axis_index("ctx")
+    greet(EVERYONE)
+    link = Link(sends, receives)
+    fold = Fold(blocks_ref, routed, over, sums, parts, fold_sends, fold_receives)
+    gives = {3: give3, 2: give2, 1: give1, 0: give0}
+    keeps = {3: keep3, 2: keep2, 1: keep1}
+    core = {step: link.push(gives[step], arrived.at[step], "ctx", 1) for step in (3, 2, 1, 0)}
+    fold.start()
+    pair = {}
+    count = stage.shape[1]
+
+    def cross(step, cut):
+        core[step].wait_recv()
+        fetch([(keeps[step].at[1], stage.at[0]), (arrived.at[step, 1], stage.at[1])], local)
+        add_into(sent.at[step - 1], [stage.at[0], stage.at[1]])
+        source, target = sent.at[step - 1], crossed.at[step - 1]
+        if cut:
+            pair[step] = [
+                link.push(source.at[item], target.at[item], "ctx", 2) for item in range(count)
+            ]
+        else:
+            pair[step] = [link.push(source, target, "ctx", 2)]
+
+    def close(step):
+        fetch([(keeps[step].at[0], stage.at[2]), (arrived.at[step, 0], stage.at[3])], local)
+        for copy in pair[step]:
+            copy.wait_recv()
+            copy.wait_send()
+        add_into(sent.at[step - 1], [stage.at[2], stage.at[3], crossed.at[step - 1]])
+
+    line = []
+
+    def close_one(item):
+        pair[3][item].wait_recv()
+        pair[3][item].wait_send()
+        sent[2, item] = (
+            stage[2, item].astype(jnp.float32)
+            + stage[3, item].astype(jnp.float32)
+            + crossed[2, item].astype(jnp.float32)
+        ).astype(jnp.bfloat16)
+        line.append(link.push(sent.at[2, item], done3.at[item], "dp", 3))
+
+    cross(3, True)
+    fetch([(keep3.at[0], stage.at[2]), (arrived.at[3, 0], stage.at[3])], local)
+    close_one(0)
+    fold.early(0)
+    close_one(1)
+    cross(2, False)
+    close_one(2)
+    fold.early(1)
+    for item in range(3, count):
+        close_one(item)
+    cross(1, False)
+    fold.late()
+    fold.last()
+
+    gates = gates_ref[...]
+    high = routed[:, D:]
+    lane = lax.broadcasted_iota(jnp.int32, high.shape, 1)
+    grad_gates = jnp.where(lane < EXPERTS, high + pltpu.roll(high, 128 - EXPERTS, 1), 0.0)
+    grad_picked = gates * (grad_gates - jnp.sum(gates * grad_gates, axis=-1, keepdims=True))
+    grad_logits = grad_picked.astype(jnp.bfloat16)
+    grad_input = routed[:, :D] + lax.dot_general(
+        grad_logits,
+        pack_ref[:, D:],
+        (((1,), (1,)), ((), ())),
+        preferred_element_type=jnp.float32,
+    )
+    normed, factor = normalize(after_ref[...])
+    grad_after = grad_ref[...].astype(jnp.float32) + norm_back(
+        grad_input * gain_ref[...], normed, factor
+    )
+    grad_after_ref[...] = grad_after
+    grad_branch = (RESIDUAL_SCALE * grad_after).astype(jnp.bfloat16)
+    wide = outgoing.shape[2]
+    for index in range(outgoing.shape[0]):
+        outgoing[index] = lax.dot_general(
+            grad_branch,
+            pack_ref[index * wide : (index + 1) * wide, :D],
+            (((1,), (1,)), ((), ())),
+            preferred_element_type=jnp.float32,
+        ).astype(jnp.bfloat16)
+    seq_grad_ref[c] = outgoing[c]
+    spread = [
+        link.push(outgoing.at[near(c, "ctx", flip)], seq_grad_ref.at[c], "ctx", flip)
+        for flip in (1, 2, 3)
+    ]
+    close(2)
+    keep_ready = [pltpu.make_async_copy(sent.at[1], ready2, local.at[0])]
+    keep_ready[0].start()
+    turned = (((0,), (0,)), ((), ()))
+    column = (lane == EXPERTS).astype(jnp.bfloat16)
+    small = lax.dot_general(
+        input_ref[...], grad_logits, turned, preferred_element_type=jnp.float32
+    ) + lax.dot_general(
+        (grad_input * normed).astype(jnp.bfloat16),
+        column,
+        turned,
+        preferred_element_type=jnp.float32,
+    )
+    small = small.astype(jnp.bfloat16).reshape(grad_pack_ref.shape[:3] + (128,))
+    grad_pack_ref[..., D:] = small
+    some = grad_pack_ref.shape[0] // outgoing.shape[0]
+    for index in range(outgoing.shape[0]):
+        part = lax.dot_general(
+            attended_ref[index], grad_branch, turned, preferred_element_type=jnp.float32
+        ).astype(jnp.bfloat16)
+        grad_pack_ref[index * some : (index + 1) * some, :, :, :D] = part.reshape(
+            (some,) + grad_pack_ref.shape[1:3] + (D,)
+        )
+    keep_ready[0].wait()
+    close(1)
+    fetch([(sent.at[0], ready1)], local)
+    for copy in spread + line + [core[0]]:
+        copy.wait_recv()
+    fold.finish()
+    for copy in list(core.values()) + spread + line:
+        copy.wait_send()
+
+
+def returning(blocks, parts, after, expert_input, gates, grads, gain, pack, attended, number):
+    kind = jnp.bfloat16
+    far = pl.BlockSpec(memory_space=pl.ANY)
+    held = pl.BlockSpec(memory_space=pltpu.VMEM)
+    give3, keep3, give2, keep2, give1, keep1, give0, _ = parts
+    piece = give3.shape[1:]
+    ctx, tokens, wide = attended.shape
     shape = blocks.shape[1:]
     return pl.pallas_call(
-        scatter_kernel,
-        out_shape=jax.ShapeDtypeStruct(shape, jnp.float32),
-        scratch_shapes=[
-            pltpu.VMEM((4,) + shape, jnp.bfloat16),
-            pltpu.VMEM((4,) + shape, jnp.bfloat16),
-            pltpu.VMEM((6,) + shape, jnp.bfloat16),
-            pltpu.SemaphoreType.DMA((10,)),
-            pltpu.SemaphoreType.DMA((10,)),
+        returning_kernel,
+        out_shape=(
+            jax.ShapeDtypeStruct((tokens, D), jnp.float32),
+            jax.ShapeDtypeStruct(attended.shape, kind),
+            jax.ShapeDtypeStruct((8, ctx, D // (8 * ctx), shape[1]), kind),
+            jax.ShapeDtypeStruct((4,) + give3.shape, kind),
+            jax.ShapeDtypeStruct(piece, kind),
+            jax.ShapeDtypeStruct(piece, kind),
+            jax.ShapeDtypeStruct(piece, kind),
+        ),
+        in_specs=[held] + [far] * 7 + [held] * 7,
+        out_specs=(held, held, held, far, far, far, far),
+        scratch_shapes=[pltpu.VMEM(shape, jnp.float32)]
+        + fold_scratch(shape)
+        + [
+            pltpu.VMEM((3,) + piece, kind),
+            pltpu.VMEM((3,) + piece, kind),
+            pltpu.VMEM((4,) + piece, kind),
+            pltpu.VMEM(attended.shape, kind),
+            pltpu.SemaphoreType.DMA((9 + 2 * piece[0],)),
+            pltpu.SemaphoreType.DMA((9 + 2 * piece[0],)),
+            pltpu.SemaphoreType.DMA((2,)),
         ],
         compiler_params=pltpu.CompilerParams(
-            collective_id=number, has_side_effects=True, vmem_limit_bytes=48 * 1024 * 1024
+            collective_id=number, has_side_effects=True, vmem_limit_bytes=62 * 1024 * 1024
         ),
-    )(blocks)
+    )(
+        blocks, give3, keep3, give2, keep2, give1, keep1, give0,
+        after, expert_input, gates, grads, gain, pack, attended,
+    )
+
+
+def closing_kernel(
+    ready2, ready1, keep0, arrived, table_ref, query_ref, keys_ref, values_ref, seq_grad_ref,
+    normed_ref, columns_ref, grad_pack_ref, rows_ref, grad_after_ref,
+    done2, done1, done0, input_grad_ref, shard_columns_ref, shard_pack_ref,
+    sent, crossed, stage, mixed, flipped, grad_keys, grad_values,
+    pack_core, pack_pair, pack_sent, pack_blocks, pack_over, pack_sums, pack_parts, pack_sends, pack_receives,
+    scaled, scaled_core, scaled_pair, scaled_sent,
+    part_blocks, part_out, part_over, part_sums, part_parts, part_sends, part_receives,
+    sends, receives, local,
+):
+    z, c = lax.axis_index("dp"), lax.axis_index("ctx")
+    greet(EVERYONE)
+    link = Link(sends, receives)
+
+    def c_at(flip):
+        return near(c, "ctx", flip) if flip else c
+
+    to_core = [
+        link.push(grad_pack_ref.at[:, c_at(flip)], pack_core.at[number], "ctx", 1)
+        for number, flip in enumerate((3, 1))
+    ]
+    line = [link.push(ready2, done2, "dp", 2), link.push(ready1, done1, "dp", 1)]
+    zones = grad_pack_ref.shape[0]
+    to_core[0].wait_recv()
+    for zone in range(zones):
+        pack_sent[zone] = (
+            grad_pack_ref[zone, c_at(2)].astype(jnp.float32)
+            + pack_core[0, zone].astype(jnp.float32)
+        ).astype(jnp.bfloat16)
+    pack_over_pair = link.push(pack_sent, pack_pair, "ctx", 2)
+    fetch([(keep0.at[1], stage.at[0]), (arrived.at[0, 1], stage.at[1])], local)
+    add_into(sent, [stage.at[0], stage.at[1]])
+    pair = link.push(sent, crossed, "ctx", 2)
+    attend_back(
+        table_ref, query_ref, keys_ref, values_ref, seq_grad_ref, mixed, flipped, grad_keys, grad_values
+    )
+    blocks, block = scaled.shape[:2]
+    for index in range(blocks):
+        scaled[index] = lax.dot_general(
+            mixed[index * block : (index + 1) * block, :],
+            columns_ref[...],
+            (((1,), (1,)), ((), ())),
+            preferred_element_type=jnp.float32,
+        ).astype(jnp.bfloat16)
+    scaled_to_core = [
+        link.push(scaled.at[c_at(flip)], scaled_core.at[number], "ctx", 1)
+        for number, flip in enumerate((3, 1))
+    ]
+    wide = normed_ref.shape[1] // blocks
+    some = zones // blocks
+    for index in range(blocks):
+        part = lax.dot_general(
+            normed_ref[:, index * wide : (index + 1) * wide],
+            mixed[...],
+            (((0,), (0,)), ((), ())),
+            preferred_element_type=jnp.float32,
+        ).astype(jnp.bfloat16)
+        part_blocks[index * some : (index + 1) * some] = part.reshape(
+            (some,) + part_blocks.shape[1:]
+        )
+    part_fold = Fold(
+        part_blocks, part_out, part_over, part_sums, part_parts, part_sends, part_receives
+    )
+    part_fold.start()
+    scaled_to_core[0].wait_recv()
+    scaled_sent[...] = (
+        scaled[c_at(2)].astype(jnp.float32) + scaled_core[0].astype(jnp.float32)
+    ).astype(jnp.bfloat16)
+    scaled_over_pair = link.push(scaled_sent, scaled_pair, "ctx", 2)
+    to_core[1].wait_recv()
+    pack_over_pair.wait_recv()
+    for zone in range(zones):
+        pack_blocks[zone] = (
+            grad_pack_ref[zone, c].astype(jnp.float32)
+            + pack_core[1, zone].astype(jnp.float32)
+            + pack_pair[zone].astype(jnp.float32)
+        ).astype(jnp.bfloat16)
+    pack_fold = Fold(
+        pack_blocks, shard_pack_ref, pack_over, pack_sums, pack_parts, pack_sends, pack_receives
+    )
+    pack_fold.start()
+    part_fold.early(0)
+    part_fold.early(1)
+    pack_fold.early(0)
+    pack_fold.early(1)
+    part_fold.late()
+    part_fold.last()
+    apart = [
+        link.push(part_out.at[c_at(flip)], shard_columns_ref.at[c], "ctx", flip)
+        for flip in (1, 2, 3)
+    ]
+    shard_columns_ref[c] = part_out[c]
+    scaled_to_core[1].wait_recv()
+    scaled_over_pair.wait_recv()
+    grad_normed = (
+        scaled[c].astype(jnp.float32)
+        + scaled_core[1].astype(jnp.float32)
+        + scaled_pair[...].astype(jnp.float32)
+    )
+    normed, factor = normalize(rows_ref[...].astype(jnp.float32))
+    input_grad_ref[...] = grad_after_ref[...] + norm_back(grad_normed, normed, factor)
+    pack_fold.late()
+    pack_fold.last()
+    fetch([(keep0.at[0], stage.at[0]), (arrived.at[0, 0], stage.at[1])], local)
+    pair.wait_recv()
+    pair.wait_send()
+    add_into(sent, [stage.at[0], stage.at[1], crossed])
+    fetch([(sent, done0)], local)
+    for copy in apart + line:
+        copy.wait_recv()
+    part_fold.finish()
+    pack_fold.finish()
+    for copy in link.started:
+        if copy is not pair:
+            copy.wait_send()
+
+
+def closing(
+    ready2, ready1, keep0, arrived, table, query, keys, values, seq_grad, normed, columns,
+    grad_pack, rows, grad_after, number,
+):
+    kind = jnp.bfloat16
+    far = pl.BlockSpec(memory_space=pl.ANY)
+    held = pl.BlockSpec(memory_space=pltpu.VMEM)
+    piece = ready2.shape
+    heads, length = query.shape[:2]
+    groups = keys.shape[0]
+    zones, ctx, share, wide = grad_pack.shape
+    width = columns.shape[1]
+    pack = (zones, share, wide)
+    block = (length // ctx, D)
+    part = (ctx, share, width)
+    return pl.pallas_call(
+        closing_kernel,
+        out_shape=(
+            jax.ShapeDtypeStruct(piece, kind),
+            jax.ShapeDtypeStruct(piece, kind),
+            jax.ShapeDtypeStruct(piece, kind),
+            jax.ShapeDtypeStruct(rows.shape, jnp.float32),
+            jax.ShapeDtypeStruct(part, kind),
+            jax.ShapeDtypeStruct((share, wide), jnp.float32),
+        ),
+        in_specs=[far] * 4 + [held] * 10,
+        out_specs=(far, far, far, held, held, held),
+        scratch_shapes=[
+            pltpu.VMEM(piece, kind),
+            pltpu.VMEM(piece, kind),
+            pltpu.VMEM((2,) + piece, kind),
+            pltpu.VMEM((length, width), kind),
+            pltpu.VMEM((groups * HD, length), kind),
+            pltpu.VMEM((groups, length, HD), jnp.float32),
+            pltpu.VMEM((groups, length, HD), jnp.float32),
+            pltpu.VMEM((2,) + pack, kind),
+            pltpu.VMEM(pack, kind),
+            pltpu.VMEM(pack, kind),
+            pltpu.VMEM(pack, kind),
+        ]
+        + fold_scratch(pack[1:])
+        + [
+            pltpu.VMEM((ctx,) + block, kind),
+            pltpu.VMEM((2,) + block, kind),
+            pltpu.VMEM(block, kind),
+            pltpu.VMEM(block, kind),
+            pltpu.VMEM((zones,) + part, kind),
+            pltpu.VMEM(part, kind),
+        ]
+        + fold_scratch(part)
+        + [
+            pltpu.SemaphoreType.DMA((12,)),
+            pltpu.SemaphoreType.DMA((12,)),
+            pltpu.SemaphoreType.DMA((2,)),
+        ],
+        compiler_params=pltpu.CompilerParams(
+            collective_id=number, has_side_effects=True, vmem_limit_bytes=62 * 1024 * 1024
+        ),
+    )(
+        ready2, ready1, keep0, arrived, table, query, keys, values, seq_grad, normed, columns,
+        grad_pack, rows, grad_after,
+    )
+
+
+def route_rows(rows, pack_ref, attended_ref, routes_ref, after_ref, gates_ref, gain_ref, packed):
+    quarters = attended_ref.shape[0]
+    wide = pack_ref.shape[-1]
+    branch = jnp.zeros((rows.shape[0], D), jnp.float32)
+    tails = []
+    for index in range(quarters):
+        pack = pack_ref[index].reshape(-1, wide)
+        branch += jnp.dot(attended_ref[index], pack[:, :D], preferred_element_type=jnp.float32)
+        tails.append(pack[:, D:])
+    tail = jnp.concatenate(tails, 0)
+    after = rows.astype(jnp.float32) + RESIDUAL_SCALE * branch
+    after_ref[...] = after
+    normed, _ = normalize(after)
+    single = lax.broadcasted_iota(jnp.int32, (8, 128), 1) == EXPERTS
+    gain = lax.dot_general(
+        single.astype(jnp.bfloat16),
+        tail,
+        (((1,), (1,)), ((), ())),
+        preferred_element_type=jnp.float32,
+    )[:1]
+    gain_ref[...] = gain
+    expert_input = (normed * gain).astype(jnp.bfloat16)
+    logits = jnp.dot(expert_input, tail, preferred_element_type=jnp.float32)
+    lane = lax.broadcasted_iota(jnp.int32, logits.shape, 1)
+    marks = jnp.zeros(logits.shape, jnp.float32)
+    for index in range(TOP):
+        marks = jnp.where(lane == routes_ref[:, index : index + 1], 1.0, marks)
+    chosen = marks > 0.0
+    peak = jnp.max(jnp.where(chosen, logits, -3e38), axis=-1, keepdims=True)
+    raised = jnp.where(chosen, jnp.exp(jnp.where(chosen, logits - peak, 0.0)), 0.0)
+    gates = raised / jnp.sum(raised, axis=-1, keepdims=True)
+    gates_ref[...] = gates
+    high = gates.astype(jnp.bfloat16).astype(jnp.float32)
+    packed[:, :D] = expert_input
+    packed[:, D:] = (
+        high + pltpu.roll(gates - high, EXPERTS, 1) + pltpu.roll(marks, 2 * EXPERTS, 1)
+    ).astype(jnp.bfloat16)
 
 
 def opening_kernel(
-    rows_ref, columns_ref, pack_ref, weights_ref, grads_ref,
-    all_rows, all_columns, all_pack, pieces, all_grads,
+    rows_ref, columns_ref, pack_ref, weights_in, weights_out, grads_ref, routes_ref,
+    all_rows, all_columns, all_pack, pieces_in, pieces_out, all_grads, all_packed,
+    after_ref, gates_ref, gain_ref, packed,
     normed_ref, query_ref, keys_ref, values_ref, attended_ref,
-    outgoing, flipped, sends, receives, line_sends, line_receives, locals_,
+    outgoing, flipped, sends, receives, line_sends, line_receives, token_sends, token_receives, locals_,
 ):
     z, y, c = lax.axis_index("dp"), lax.axis_index("expert"), lax.axis_index("ctx")
-    greet([("dp", 1), ("dp", 2), ("dp", 3), ("expert", 1), ("ctx", 1), ("ctx", 2), ("ctx", 3)])
+    greet(EVERYONE)
     link = Link(sends, receives)
     line = Line(grads_ref, all_grads, line_sends, line_receives)
+    token_line = Line(packed, all_packed, token_sends, token_receives)
     own = 2 * z + y
-    count = weights_ref.shape[1]
+    count = weights_in.shape[1]
 
     def z_at(flip):
         return near(z, "dp", flip) if flip else z
@@ -825,70 +1231,77 @@
     def c_at(flip):
         return near(c, "ctx", flip) if flip else c
 
-    keeps = [
-        pltpu.make_async_copy(source, target, locals_.at[number])
-        for number, (source, target) in enumerate(
-            [
-                (columns_ref.at[c], all_columns.at[own, c]),
-                (rows_ref, all_rows.at[c]),
-                (pack_ref, all_pack.at[z, y, c]),
-                (grads_ref, all_grads.at[own]),
-                (weights_ref.at[z], pieces.at[0, 0]),
-            ]
-        )
+    def keep(number, source, target):
+        copy = pltpu.make_async_copy(source, target, locals_.at[number])
+        copy.start()
+        return copy
+
+    def both(target, source, axis, flip):
+        return [link.push(source(ref), target(ref), axis, flip) for ref in (pieces_in, pieces_out)]
+
+    def share(*place):
+        step, rest = place[0], place[1:]
+        source = lambda ref: ref.at[(step, 0) + rest]
+        over = both(lambda ref: ref.at[(step, 2) + rest], source, "ctx", 2)
+        core = both(lambda ref: ref.at[(step, 1) + rest], source, "ctx", 1)
+        return over, core
+
+    def hand_on(*place):
+        step, rest = place[0], place[1:]
+        return both(
+            lambda ref: ref.at[(step, 3) + rest], lambda ref: ref.at[(step, 2) + rest], "ctx", 1
+        )
+
+    def move(step, *rest):
+        return [
+            link.push(weights.at[(z_at(step),) + rest], ref.at[(step, 0) + rest], "dp", step)
+            for weights, ref in ((weights_in, pieces_in), (weights_out, pieces_out))
+        ]
+
+    def arrive(copies):
+        for copy in copies:
+            copy.wait_recv()
+
+    kept = [
+        keep(0, columns_ref.at[c], all_columns.at[own, c]),
+        keep(1, weights_in.at[z], pieces_in.at[0, 0]),
+        keep(2, weights_out.at[z], pieces_out.at[0, 0]),
+        keep(3, rows_ref, all_rows.at[c]),
+        keep(4, pack_ref, all_pack.at[z, y, c]),
+        keep(5, grads_ref, all_grads.at[own]),
     ]
-    for keep in keeps:
-        keep.start()
     cut = [
         link.push(columns_ref.at[c_at(flip)], all_columns.at[own, c], "ctx", flip)
         for flip in (1, 2, 3)
     ]
-
-    def share(*place):
-        step, rest = place[0], place[1:]
-        source = pieces.at[(step, 0) + rest]
-        over = link.push(source, pieces.at[(step, 2) + rest], "ctx", 2)
-        core = link.push(source, pieces.at[(step, 1) + rest], "ctx", 1)
-        return over, core
-
-    def hand_on(*place):
-        step, rest = place[0], place[1:]
-        return link.push(pieces.at[(step, 2) + rest], pieces.at[(step, 3) + rest], "ctx", 1)
-
-    moved = {
-        step: link.push(weights_ref.at[z_at(step)], pieces.at[step, 0], "dp", step)
-        for step in (1, 2)
-    }
-    line.start()
-    keeps[4].wait()
-    shared = [share(0)]
-    keeps[0].wait()
-    for copy in cut:
-        copy.wait_recv()
+    rows_over = link.push(rows_ref, all_rows.at[c], "ctx", 2)
+    rows_core = link.push(rows_ref, all_rows.at[c], "ctx", 1)
+    pack_line = [link.push(pack_ref, all_pack.at[z, y, c], "dp", flip) for flip in (1, 2, 3)]
+    kept[0].wait()
+    arrive(cut)
     column_line = [
         link.push(all_columns.at[own], all_columns.at[own], "dp", flip) for flip in (1, 2, 3)
     ]
     column_over = [link.push(all_columns.at[own], all_columns.at[own], "expert", 1)]
-    rows_over = link.push(rows_ref, all_rows.at[c], "ctx", 2)
-    rows_core = link.push(rows_ref, all_rows.at[c], "ctx", 1)
-    pack_line = [link.push(pack_ref, all_pack.at[z, y, c], "dp", flip) for flip in (1, 2, 3)]
-    line.first()
+    kept[1].wait()
+    kept[2].wait()
+    rows_over.wait_recv()
+    rows_pass = link.push(all_rows.at[c_at(2)], all_rows.at[c_at(2)], "ctx", 1)
+    shared = [share(0)]
+    arrive(pack_line)
+    kept[4].wait()
+    pack_over = link.push(all_pack.at[:, y, c], all_pack.at[:, y, c], "expert", 1)
     for flip in (1, 2, 3):
         column_line[flip - 1].wait_recv()
         block = all_columns.at[2 * z_at(flip) + y]
         column_over.append(link.push(block, block, "expert", 1))
-    rows_over.wait_recv()
-    rows_pass = link.push(all_rows.at[c_at(2)], all_rows.at[c_at(2)], "ctx", 1)
-    moved[1].wait_recv()
-    shared.append(share(1))
-    line.second()
-    for copy in pack_line:
-        copy.wait_recv()
-    keeps[2].wait()
-    pack_over = link.push(all_pack.at[:, y, c], all_pack.at[:, y, c], "expert", 1)
-    for copy in [rows_core, rows_pass] + column_over:
-        copy.wait_recv()
-    keeps[1].wait()
+    moved = {1: move(1), 2: move(2)}
+    line.start()
+    arrive([pack_over])
+    pack_pair = link.push(all_pack.at[:, :, c], all_pack.at[:, :, c], "ctx", 2)
+    pack_core = link.push(all_pack.at[:, :, c], all_pack.at[:, :, c], "ctx", 1)
+    arrive([rows_core, rows_pass] + column_over)
+    kept[3].wait()
     project_rows(
         all_rows,
         all_columns[...].reshape(D, all_columns.shape[-1]),
@@ -898,53 +1311,65 @@
         values_ref,
         flipped,
     )
-    line.third()
-    pack_over.wait_recv()
-    pack_pair = link.push(all_pack.at[:, :, c], all_pack.at[:, :, c], "ctx", 2)
-    pack_core = link.push(all_pack.at[:, :, c], all_pack.at[:, :, c], "ctx", 1)
-    shared[0][0].wait_recv()
-    passed = [hand_on(0)]
-    moved[2].wait_recv()
-    shared.append(share(2))
-
-    def last_piece(item):
-        return link.push(weights_ref.at[z_at(3), item], pieces.at[3, 0, item], "dp", 3)
-
-    last = [last_piece(0), last_piece(1)]
     for index in range(all_rows.shape[0]):
         attend_rows(index, all_rows.shape[1], query_ref, keys_ref, outgoing, flipped)
     attended = [
         link.push(outgoing.at[c_at(flip)], attended_ref.at[c], "ctx", flip) for flip in (1, 2, 3)
     ]
     attended_ref[c] = outgoing[c]
-    shared[1][0].wait_recv()
-    passed.append(hand_on(1))
+    line.first()
+    arrive([pack_pair])
+    pack_last = link.push(all_pack.at[:, :, c_at(2)], all_pack.at[:, :, c_at(2)], "ctx", 1)
+    arrive(shared[0][0])
+    passed = hand_on(0)
+    arrive([pack_core, pack_last] + attended)
+    route_rows(
+        all_rows[c, :, :D], all_pack, attended_ref, routes_ref, after_ref, gates_ref, gain_ref, packed
+    )
+    token_line.start()
+    kept.append(keep(6, packed, all_packed.at[own]))
+    arrive(moved[1])
+    shared.append(share(1))
+    line.second()
+    token_line.first()
+    line.third()
+    token_line.second()
+    arrive(moved[2])
+    shared.append(share(2))
+    last = [move(3, 0), move(3, 1)]
+    token_line.third()
+    arrive(shared[1][0])
+    passed += hand_on(1)
+
+    def next_piece(item):
+        arrive(last[item])
+        if item + 2 < count:
+            last.append(move(3, item + 2))
+        shared.append(share(3, item))
+
     for item in range(count):
-        last[item].wait_recv()
-        if item + 2 < count:
-            last.append(last_piece(item + 2))
-        shared.append(share(3, item))
-    pack_pair.wait_recv()
-    pack_last = link.push(all_pack.at[:, :, c_at(2)], all_pack.at[:, :, c_at(2)], "ctx", 1)
-    shared[2][0].wait_recv()
-    passed.append(hand_on(2))
+        next_piece(item)
+    arrive(shared[2][0])
+    passed += hand_on(2)
     for item in range(count):
-        shared[3 + item][0].wait_recv()
-        passed.append(hand_on(3, item))
-    keeps[3].wait()
-    for copy in attended + [pack_core, pack_last] + passed:
-        copy.wait_recv()
+        arrive(shared[3 + item][0])
+        passed += hand_on(3, item)
+    kept[5].wait()
+    kept[6].wait()
+    arrive(passed)
     for over, core in shared:
-        core.wait_recv()
+        arrive(core)
     line.finish()
+    token_line.finish()
     link.finish()
 
 
-def opening(rows, columns, pack, weights, grads, heads, groups, number):
+def opening(rows, columns, pack, weights_in, weights_out, grads, routes, heads, groups, number):
     ctx = columns.shape[0]
-    shards, count = weights.shape[:2]
+    shards, count = weights_in.shape[:2]
+    tokens = rows.shape[0]
     kind = jnp.bfloat16
-    copies = 24 + 10 + 4 * count
+    copies = 24 + 2 * (2 + 3 * 3 + 5 * count)
     far = pl.BlockSpec(memory_space=pl.ANY)
     held = pl.BlockSpec(memory_space=pltpu.VMEM)
     all_rows = (ctx,) + rows.shape
@@ -954,12 +1379,18 @@
             jax.ShapeDtypeStruct(all_rows, kind),
             jax.ShapeDtypeStruct((8,) + columns.shape, kind),
             jax.ShapeDtypeStruct((shards, 2, ctx) + pack.shape, kind),
-            jax.ShapeDtypeStruct((shards, ctx) + weights.shape[1:], kind),
+            jax.ShapeDtypeStruct((shards, ctx) + weights_in.shape[1:], kind),
+            jax.ShapeDtypeStruct((shards, ctx) + weights_out.shape[1:], kind),
             jax.ShapeDtypeStruct((8,) + grads.shape, kind),
+            jax.ShapeDtypeStruct((8,) + rows.shape, kind),
+            jax.ShapeDtypeStruct((tokens, D), jnp.float32),
+            jax.ShapeDtypeStruct((tokens, 128), jnp.float32),
+            jax.ShapeDtypeStruct((1, D), jnp.float32),
+            jax.ShapeDtypeStruct(rows.shape, kind),
         )
         + attend_shapes(all_rows, heads, groups),
-        in_specs=[far] * 5,
-        out_specs=(held, held, far, far, far) + (held,) * 5,
+        in_specs=[far] * 6 + [held],
+        out_specs=(held, held, held, far, far, far, far) + (held,) * 9,
         scratch_shapes=[
             pltpu.VMEM((ctx, rows.shape[0], heads * HD), kind),
             pltpu.VMEM((groups * HD, ctx * rows.shape[0]), kind),
@@ -967,12 +1398,14 @@
             pltpu.SemaphoreType.DMA((copies,)),
             pltpu.SemaphoreType.DMA((9,)),
             pltpu.SemaphoreType.DMA((8,)),
-            pltpu.SemaphoreType.DMA((5,)),
+            pltpu.SemaphoreType.DMA((9,)),
+            pltpu.SemaphoreType.DMA((8,)),
+            pltpu.SemaphoreType.DMA((7,)),
         ],
         compiler_params=pltpu.CompilerParams(
-            collective_id=number, has_side_effects=True, vmem_limit_bytes=48 * 1024 * 1024
+            collective_id=number, has_side_effects=True, vmem_limit_bytes=56 * 1024 * 1024
         ),
-    )(rows, columns, pack, weights, grads)
+    )(rows, columns, pack, weights_in, weights_out, grads, routes)
 
 
 def split_high_low(values):
@@ -1070,33 +1503,22 @@
     return [all_in.reshape(count, -1, 2 * part), all_out]
 
 
-def collect_weights(order, rows, grads, grad_hidden, gated, expert_in, expert_out, close):
+def piece_grads(order, rows, grads, grad_hidden, gated, pieces_in, pieces_out):
+    _, _, shards, ctx = block_order()
+    count, deep = pieces_out.shape[1:3]
+    folds = pieces_in.shape[2] // deep
+    shape = (ctx // 2, count, deep, folds * pieces_in.shape[3] + pieces_out.shape[3])
+    slots = []
+    for step in reversed(range(shards)):
+        for bit in (1, 0):
+            slots += [step * ctx + turn for turn in range(bit, ctx, 2)]
+    order = jnp.stack([order[slot] for slot in slots])
+    return weight_grads(order, rows, grads, grad_hidden, gated, [shape] * (2 * shards))
+
+
+def collect_weights(order, rows, grads, grad_hidden, gated, expert_in, expert_out):
     place, column, shards, ctx = block_order()
     depth_in, depth_out = expert_in.shape[1], expert_out.shape[1]
-    if close:
-        count = expert_in.shape[0] // shards
-        folds = depth_in // depth_out
-        sent, slots = [], []
-        for step in reversed(range(shards)):
-            for bit in (1, 0):
-                sent.append((ctx // 2, count, depth_out, folds * 2 * FFE + D))
-                slots += [step * ctx + turn for turn in range(bit, ctx, 2)]
-        order = jnp.stack([order[slot] for slot in slots])
-        parts = weight_grads(order, rows, grads, grad_hidden, gated, sent)
-        received = []
-        for number, step in enumerate(reversed(range(shards))):
-            give, keep = parts[2 * number], parts[2 * number + 1]
-            flip = 1
-            while True:
-                total = keep.astype(jnp.float32) + swap(give, "ctx", flip).astype(jnp.float32)
-                total = total.astype(jnp.bfloat16)
-                flip *= 2
-                if flip == ctx:
-                    break
-                keep, give = total[0::2], total[1::2]
-            piece = swap(total[0], "dp", step) if step else total[0]
-            received.append((place ^ step, piece))
-        return received
     count = expert_in.shape[0]
     part = FFE // shards
     blocks = shards * ctx
@@ -1113,46 +1535,63 @@
     return [(0, fold_weights(own_in, own_out))]
 
 
-def expert_step_kernel(first_ref, grad_ref, *refs):
-    states, outs = refs[:6], refs[-8:]
+def expert_step_kernel(places_ref, *refs):
+    states, outs = refs[-14:-8], refs[-8:]
+    grads = refs[:-14]
+    number = pl.program_id(0)
     wide = states[0].shape[2]
     deep = states[3].shape[1]
     folds = states[0].shape[1] // deep
     rates = learn_rates()
-    for fold in range(folds):
-        span = pl.ds(fold * deep, deep)
-        grad = grad_ref[0, :, fold * wide : (fold + 1) * wide].astype(jnp.float32)
-        news = adam_step(
-            states[0][0, span, :], states[1][0, span, :], states[2][0, span, :], grad, DECAY_RATE, rates[5]
-        )
-        for out, new in zip(outs[:4], news):
-            out[0, span, :] = new
-    grad = grad_ref[0, :, folds * wide :].astype(jnp.float32)
-    news = adam_step(states[3][0], states[4][0], states[5][0], grad, DECAY_RATE, rates[6])
-    for out, new in zip(outs[4:], news):
-        out[0] = new
-
-
-def expert_step(first, folded, states, outs):
+
+    def update(grad_ref):
+        for fold in range(folds):
+            span = pl.ds(fold * deep, deep)
+            grad = grad_ref[0, :, fold * wide : (fold + 1) * wide].astype(jnp.float32)
+            news = adam_step(
+                states[0][0, span, :],
+                states[1][0, span, :],
+                states[2][0, span, :],
+                grad,
+                DECAY_RATE,
+                rates[5],
+            )
+            for out, new in zip(outs[:4], news):
+                out[0, span, :] = new
+        grad = grad_ref[0, :, folds * wide :].astype(jnp.float32)
+        news = adam_step(states[3][0], states[4][0], states[5][0], grad, DECAY_RATE, rates[6])
+        for out, new in zip(outs[4:], news):
+            out[0] = new
+
+    count = pl.num_programs(0) // len(grads)
+    for index, grad_ref in enumerate(grads):
+        pl.when(number // count == index)(functools.partial(update, grad_ref))
+
+
+def expert_step(places, grads, states):
+    count = grads[0].shape[0]
     shapes = [states[1].shape] * 4 + [states[4].shape] * 4
-    moved = lambda e, f: (f[0] + e, 0, 0)
+    moved = lambda e, p: (p[e // count] * count + e % count, 0, 0)
     block = lambda shape: pl.BlockSpec((1,) + shape[1:], moved)
-    begun = [] if outs is None else list(outs)
+
+    def grad_spec(index):
+        return pl.BlockSpec(
+            (1,) + grads[0].shape[1:], lambda e, p: (jnp.clip(e - index * count, 0, count - 1), 0, 0)
+        )
+
     return pl.pallas_call(
         expert_step_kernel,
         grid_spec=pltpu.PrefetchScalarGridSpec(
             num_scalar_prefetch=1,
-            grid=(folded.shape[0],),
-            in_specs=[pl.BlockSpec((1,) + folded.shape[1:], lambda e, f: (e, 0, 0))]
-            + [block(state.shape) for state in states]
-            + [pl.BlockSpec(memory_space=pl.ANY) for _ in begun],
+            grid=(count * len(grads),),
+            in_specs=[grad_spec(index) for index in range(len(grads))]
+            + [block(state.shape) for state in states],
             out_specs=tuple(block(shape) for shape in shapes),
         ),
         out_shape=tuple(jax.ShapeDtypeStruct(shape, jnp.float32) for shape in shapes),
-        input_output_aliases={8 + index: index for index in range(len(begun))},
-        compiler_params=pltpu.CompilerParams(vmem_limit_bytes=40 * 1024 * 1024),
+        compiler_params=pltpu.CompilerParams(vmem_limit_bytes=62 * 1024 * 1024),
         cost_estimate=pl.CostEstimate(flops=1, bytes_accessed=1, transcendentals=0),
-    )(first, folded, *states, *begun)
+    )(places, *grads, *states)
 
 
 def local(
@@ -1206,13 +1645,17 @@
     )
     order = piece_order()
     if close:
-        folded = fold_weights(expert_in, expert_out)
-        folded = folded.reshape((shards, -1) + folded.shape[1:])
+        parted = lambda array: array.reshape((shards, -1) + array.shape[1:])
         (
-            seq_rows, own_in, full_pack_out, pieces, all_grads,
-            seq_normed, query, keys, values, attended,
-        ) = opening(rows, columns, pack_out, folded, cotangent, heads, groups, 1)
-        pieces = [pieces.reshape((-1,) + pieces.shape[2:])]
+            seq_rows, own_in, full_pack_out, all_in, all_out, all_grads, all_packed,
+            after, gates_wide, gain_two, packed,
+            seq_normed, query, keys, values, attended_heads,
+        ) = opening(
+            rows, columns, pack_out, parted(expert_in), parted(expert_out), cotangent, routes,
+            heads, groups, 1,
+        )
+        expert_input = packed[:, :D]
+        pieces = [array.reshape((-1,) + array.shape[2:]) for array in (all_in, all_out)]
     else:
         seq_rows = gather_ctx(rows)
         own_in = lax.all_gather(exchange_ctx(columns), owners, axis=0, tiled=False)
@@ -1222,33 +1665,30 @@
         seq_normed, query, keys, values, seq_attended = attend_forward(
             seq_rows, own_in.reshape(D, -1), heads, groups
         )
-        attended = exchange_ctx(seq_attended)
+        attended_heads = exchange_ctx(seq_attended)
     seq_rows = seq_rows.reshape(-1, D + 128)
     own_in = own_in.reshape(D, -1)
     full_pack_out = full_pack_out.reshape(H * HD, -1)
-    full_out = full_pack_out[:, :D]
-    full_router = full_pack_out[:, D : D + EXPERTS]
-    gain_two = full_pack_out[:, D + EXPERTS].astype(jnp.float32)
-
-    attended = attended.transpose(1, 0, 2).reshape(rows_local, H * HD)
-    branch = jnp.dot(attended, full_out, preferred_element_type=jnp.float32)
-    after = hidden_in + RESIDUAL_SCALE * branch
-    normed_two, factor_two = normalize(after)
-    expert_input = (normed_two * gain_two).astype(jnp.bfloat16)
-    logits = jnp.dot(expert_input, full_router, preferred_element_type=jnp.float32)
-    chosen = jnp.any(routes[:, :, None] == jnp.arange(EXPERTS, dtype=jnp.int32), axis=1)
-    peak = jnp.max(jnp.where(chosen, logits, -3e38), axis=-1, keepdims=True)
-    raised = jnp.where(chosen, jnp.exp(jnp.where(chosen, logits - peak, 0.0)), 0.0)
-    gates = raised / jnp.sum(raised, axis=-1, keepdims=True)
-    packed = jnp.concatenate(
-        (expert_input,)
-        + split_high_low(gates)
-        + (chosen.astype(jnp.bfloat16), pad_columns(expert_input, 128 - 3 * EXPERTS)),
-        1,
-    )
-    if close:
-        all_packed = gather_owners(packed, 2)
-    else:
+    if not close:
+        full_out = full_pack_out[:, :D]
+        full_router = full_pack_out[:, D : D + EXPERTS]
+        gain_two = full_pack_out[:, D + EXPERTS].astype(jnp.float32)[None]
+        attended = attended_heads.transpose(1, 0, 2).reshape(rows_local, H * HD)
+        branch = jnp.dot(attended, full_out, preferred_element_type=jnp.float32)
+        after = hidden_in + RESIDUAL_SCALE * branch
+        normed_two, factor_two = normalize(after)
+        expert_input = (normed_two * gain_two).astype(jnp.bfloat16)
+        logits = jnp.dot(expert_input, full_router, preferred_element_type=jnp.float32)
+        chosen = jnp.any(routes[:, :, None] == jnp.arange(EXPERTS, dtype=jnp.int32), axis=1)
+        peak = jnp.max(jnp.where(chosen, logits, -3e38), axis=-1, keepdims=True)
+        raised = jnp.where(chosen, jnp.exp(jnp.where(chosen, logits - peak, 0.0)), 0.0)
+        gates = raised / jnp.sum(raised, axis=-1, keepdims=True)
+        packed = jnp.concatenate(
+            (expert_input,)
+            + split_high_low(gates)
+            + (chosen.astype(jnp.bfloat16), pad_columns(expert_input, 128 - 3 * EXPERTS)),
+            1,
+        )
         all_packed = lax.all_gather(packed, owners, axis=0, tiled=False)
 
     first = lax.axis_index("expert") * local_count
@@ -1264,80 +1704,107 @@
         first, order, slot_rows, slot_grads, pieces, hidden
     )
     shared_grads = combine(pick, grad_rows)
+    shared = combine(pick, produced)
+    gated, shared = lax.optimization_barrier((gated, shared))
+    moe = lax.psum_scatter(shared, owners, scatter_dimension=0, tiled=False).astype(jnp.float32)
     if close:
-        grad_routed = scatter_owners(shared_grads, 3)
+        place = lax.axis_index("dp")
+        parts = piece_grads(order, slot_rows, slot_grads, grad_hidden, gated, *pieces)
+        grad_after, seq_grad, grad_pack_out, arrived, done3, ready2, ready1 = returning(
+            shared_grads,
+            parts,
+            after,
+            expert_input,
+            gates_wide,
+            cotangent,
+            gain_two,
+            full_pack_out,
+            attended_heads,
+            3,
+        )
+        done2, done1, done0, input_grad, shard_columns, shard_pack_out = closing(
+            ready2,
+            ready1,
+            parts[7],
+            arrived,
+            seq_rows[:, D:],
+            query,
+            keys,
+            values,
+            seq_grad,
+            seq_normed,
+            own_in,
+            grad_pack_out,
+            tokens,
+            grad_after,
+            4,
+        )
+        expert_grads = [
+            (near(place, "dp", 3), done3),
+            (near(place, "dp", 2), done2),
+            (near(place, "dp", 1), done1),
+            (place, done0),
+        ]
     else:
         grad_routed = lax.psum_scatter(
             shared_grads, owners, scatter_dimension=0, tiled=False
         ).astype(jnp.float32)
-    expert_grads = collect_weights(
-        order, slot_rows, slot_grads, grad_hidden, gated, expert_in, expert_out, close
-    )
-    produced, grad_routed = lax.optimization_barrier((produced, grad_routed))
-    moe = lax.psum_scatter(
-        combine(pick, produced), owners, scatter_dimension=0, tiled=False
-    ).astype(jnp.float32)
+        expert_grads = collect_weights(
+            order, slot_rows, slot_grads, grad_hidden, gated, expert_in, expert_out
+        )
+        grad_final = cotangent.astype(jnp.float32)
+        grad_gates = grad_routed[:, D : D + EXPERTS] + grad_routed[:, D + EXPERTS : D + 2 * EXPERTS]
+        grad_picked = gates * (grad_gates - jnp.sum(gates * grad_gates, axis=-1, keepdims=True))
+        grad_logits = grad_picked.astype(jnp.bfloat16)
+        grad_from_router = jnp.einsum(
+            "te,de->td", grad_logits, full_router, preferred_element_type=jnp.float32
+        )
+        grad_input = grad_from_router + grad_routed[:, :D]
+        grad_after = grad_final + norm_back(grad_input * gain_two, normed_two, factor_two)
+        grad_branch = (RESIDUAL_SCALE * grad_after).astype(jnp.bfloat16)
+        grad_attended = jnp.einsum(
+            "td,cd->tc", grad_branch, full_out, preferred_element_type=jnp.float32
+        ).astype(jnp.bfloat16)
+        seq_grad = exchange_ctx(
+            grad_attended.reshape(rows_local, ctx, heads * HD).transpose(1, 0, 2)
+        )
+        grad_mixed = attend_backward(seq_rows[:, D:], query, keys, values, seq_grad)
+        grad_in_part = jnp.einsum(
+            "td,tc->dc", seq_normed, grad_mixed, preferred_element_type=jnp.float32
+        ).astype(jnp.bfloat16)
+        grad_in_part = grad_in_part.reshape(shards * planes, -1, grad_in_part.shape[1])
+        shard_columns = lax.psum_scatter(grad_in_part, owners, scatter_dimension=0, tiled=False)
+        shard_columns = exchange_ctx(shard_columns.reshape(ctx, -1, shard_columns.shape[-1]))
+        grad_scaled = jnp.einsum(
+            "tc,dc->td", grad_mixed, own_in, preferred_element_type=jnp.float32
+        ).astype(jnp.bfloat16)
+        grad_normed = scatter_ctx(grad_scaled.reshape(ctx, rows_local, D))
+        normed_one, factor_one = normalize(hidden_in)
+        input_grad = grad_after + norm_back(grad_normed, normed_one, factor_one)
+        grad_project_out = jnp.einsum(
+            "tc,td->cd", attended, grad_branch, preferred_element_type=jnp.float32
+        ).astype(jnp.bfloat16)
+        ones = jnp.where(jnp.arange(128) == EXPERTS, 1.0, 0.0).astype(jnp.bfloat16)
+        grad_small = jnp.einsum(
+            "td,te->de",
+            jnp.concatenate([expert_input, (grad_input * normed_two).astype(jnp.bfloat16)], 0),
+            jnp.concatenate(
+                [
+                    jnp.pad(grad_logits, ((0, 0), (0, 128 - EXPERTS))),
+                    jnp.broadcast_to(ones, (rows_local, 128)),
+                ],
+                0,
+            ),
+            preferred_element_type=jnp.float32,
+        ).astype(jnp.bfloat16)
+        grad_pack_out = jnp.concatenate([grad_project_out, grad_small], 1)
+        shard_pack_out = lax.psum_scatter(
+            grad_pack_out, everywhere, scatter_dimension=0, tiled=True
+        ).astype(jnp.float32)
     block_output = (after + RESIDUAL_SCALE * moe).astype(jnp.bfloat16)
-
-    grad_final = cotangent.astype(jnp.float32)
-    grad_gates = grad_routed[:, D : D + EXPERTS] + grad_routed[:, D + EXPERTS : D + 2 * EXPERTS]
-    grad_picked = gates * (grad_gates - jnp.sum(gates * grad_gates, axis=-1, keepdims=True))
-    grad_logits = grad_picked.astype(jnp.bfloat16)
-    grad_from_router = jnp.einsum(
-        "te,de->td", grad_logits, full_router, preferred_element_type=jnp.float32
-    )
-    grad_input = grad_from_router + grad_routed[:, :D]
-    grad_after = grad_final + norm_back(grad_input * gain_two, normed_two, factor_two)
-    grad_branch = (RESIDUAL_SCALE * grad_after).astype(jnp.bfloat16)
-    grad_attended = jnp.einsum(
-        "td,cd->tc", grad_branch, full_out, preferred_element_type=jnp.float32
-    ).astype(jnp.bfloat16)
-    seq_grad = exchange_ctx(
-        grad_attended.reshape(rows_local, ctx, heads * HD).transpose(1, 0, 2)
-    ).reshape(ctx * rows_local, heads * HD)
-    grad_mixed = attend_backward(seq_rows[:, D:], query, keys, values, seq_grad)
-    grad_in_part = jnp.einsum(
-        "td,tc->dc", seq_normed, grad_mixed, preferred_element_type=jnp.float32
-    ).astype(jnp.bfloat16)
-    grad_in_part = grad_in_part.reshape(shards * planes, -1, grad_in_part.shape[1])
-    if close:
-        shard_columns = scatter_owners(grad_in_part, 4).astype(jnp.bfloat16)
-    else:
-        shard_columns = lax.psum_scatter(
-            grad_in_part, owners, scatter_dimension=0, tiled=False
-        )
-    shard_scaled = ungroup_columns(
-        exchange_ctx(shard_columns.reshape(ctx, -1, shard_columns.shape[-1]))
-    ).astype(jnp.float32)
+    shard_scaled = ungroup_columns(shard_columns).astype(jnp.float32)
     shard_in = gain_attend_wide * shard_scaled
     shard_attend = jnp.sum(shard_scaled * project_in.astype(jnp.float32), axis=1)
-    grad_scaled = jnp.einsum(
-        "tc,dc->td", grad_mixed, own_in, preferred_element_type=jnp.float32
-    ).astype(jnp.bfloat16)
-    grad_normed = scatter_ctx(grad_scaled.reshape(ctx, rows_local, D))
-    normed_one, factor_one = normalize(hidden_in)
-    input_grad = grad_after + norm_back(grad_normed, normed_one, factor_one)
-
-    grad_project_out = jnp.einsum(
-        "tc,td->cd", attended, grad_branch, preferred_element_type=jnp.float32
-    ).astype(jnp.bfloat16)
-    ones = jnp.where(jnp.arange(128) == EXPERTS, 1.0, 0.0).astype(jnp.bfloat16)
-    grad_small = jnp.einsum(
-        "td,te->de",
-        jnp.concatenate([expert_input, (grad_input * normed_two).astype(jnp.bfloat16)], 0),
-        jnp.concatenate(
-            [
-                jnp.pad(grad_logits, ((0, 0), (0, 128 - EXPERTS))),
-                jnp.broadcast_to(ones, (rows_local, 128)),
-            ],
-            0,
-        ),
-        preferred_element_type=jnp.float32,
-    ).astype(jnp.bfloat16)
-    grad_pack_out = jnp.concatenate([grad_project_out, grad_small], 1)
-    shard_pack_out = lax.psum_scatter(
-        grad_pack_out, everywhere, scatter_dimension=0, tiled=True
-    ).astype(jnp.float32)
     shard_out = shard_pack_out[:, :D]
     shard_router = shard_pack_out[:, D : D + EXPERTS]
     shard_expert = shard_pack_out[:, D + EXPERTS]
@@ -1368,10 +1835,8 @@
         )
     )
     states = (expert_in, expert_in_mean, expert_in_square, expert_out, expert_out_mean, expert_out_square)
-    expert_outs = None
-    for place, folded in expert_grads:
-        base = jnp.asarray(place * folded.shape[0], jnp.int32).reshape(1)
-        expert_outs = expert_step(base, folded, states, expert_outs)
+    places = jnp.stack([jnp.asarray(place, jnp.int32) for place, _ in expert_grads])
+    expert_outs = expert_step(places, [folded for _, folded in expert_grads], states)
     results.extend(expert_outs)
     return tuple(results)
 

time: 951 us -> 757 us (0.80)
  waiting for transfers between devices: 89.7 us -> 0.02 us
  local copies, waits for them, and re-layouts: 71.1 us -> 15.7 us
  other arithmetic: 50.8 us -> 13.4 us
  Pallas kernels: 666 us -> 702 us
  matrix products: 23.7 us -> 0 us
  starting transfers between devices: 21.2 us -> 0.04 us
    ppermute x19 -> x0, waiting for transfers between devices: 89.7 us -> none  [swap(): return lax.ppermute(rows, axis, [(i, i ^ flip) for i in range(size)])]
    unnamed x134 -> x46, local copies, waits for them, and re-layouts: 39.2 us -> 7.35 us
    dot_general x8 -> x0, matrix products: 23.7 us -> none  [the longest x1 5.26 us: local(): jnp.einsum('td,cd->tc', grad_branch, full_out, preferred_element_type=jnp...]
    ppermute x19 -> x0, starting transfers between devices: 21.2 us -> none  [swap(): return lax.ppermute(rows, axis, [(i, i ^ flip) for i in range(size)])]
    convert_element_type x13 -> x1, other arithmetic: 18.4 us -> 2.21 us  [local(): block_output = (after + RESIDUAL_SCALE * moe).astype(jnp.bfloat16)]
    pallas_call x1, Pallas kernels: 273 us -> 288 us  [opening(): pl.pallas_call(opening_kernel, out_shape=(jax.ShapeDtypeStruct(all_rows,...]
    pallas_call x4 -> x2, Pallas kernels: 274 us -> 281 us  [the longest x1 153 us: returning(): pl.pallas_call(returning_kernel, out_shape=(jax.ShapeDtypeStruct((tokens,...]
    pallas_call x4 -> x1, Pallas kernels: 34.9 us -> 38.2 us  [expert_step(): pl.pallas_call(expert_step_kernel, grid_spec=pltpu.PrefetchScalarGridSpec...]
  transfers between devices with their start and end apart: 21 -> 1, of which waited for: 4 -> 0; matrix products, arithmetic and copies ran while one was open for 9% -> 2% of each run, Pallas kernels for 18% -> 47%
where the time goes in v2:
time: 757 us; the launch traced here: 746 us
  Pallas kernels  702 us (93%)
  local copies, waits for them, and re-layouts  15.7 us (2%)
  between operations  14.8 us (2%)
  other arithmetic  13.4 us (2%)
    pallas_call x1, Pallas kernels, opening(): pl.pallas_call(opening_kernel, out_shape=(jax.ShapeDtypeStruct(all_rows,...  288 us
    pallas_call x1, Pallas kernels, returning(): pl.pallas_call(returning_kernel, out_shape=(jax.ShapeDtypeStruct((tokens,...  153 us
    pallas_call x1, Pallas kernels, closing(): pl.pallas_call(closing_kernel, out_shape=(jax.ShapeDtypeStruct(piece, kin...  128 us
    pallas_call x1, Pallas kernels, expert_step(): pl.pallas_call(expert_step_kernel, grid_spec=pltpu.PrefetchScalarGridSpec...  38.2 us
    pallas_call x1, Pallas kernels, run_experts(): pl.pallas_call(expert_kernel, grid_spec=pltpu.PrefetchScalarGridSpec(num_...  34.3 us
    pallas_call x1, Pallas kernels, weight_grads(): pl.pallas_call(weight_grad_kernel, grid_spec=pltpu.PrefetchScalarGridSpec...  23.5 us
    pallas_call x2, Pallas kernels, combine(): pl.pallas_call(combine_kernel, grid=(sources,), in_specs=[pl.BlockSpec((1...  21 us
    pallas_call x1, Pallas kernels, dispatch(): pl.pallas_call(dispatch_kernel, grid_spec=pltpu.PrefetchScalarGridSpec(nu...  15.5 us
  transfers between devices with their start and end apart: 1, of which 0 were waited for; matrix products, arithmetic and copies ran while one was open for 2% of the time, Pallas kernels for 47%

profile of v2, /device:TPU:0, one launch (start us, length us, event | category | flops | bytes accessed | tf_op | source)
XLA Modules:
  0.0 745.6 jit_solution(5146094673361349088)
XLA Ops:
  7.2 0.0 copy-start.1
  7.2 0.0 reduce-scatter.2.cloned.1.call-start
  7.3 0.7 convert_element_type.59
  8.0 1.1 fusion.2
  9.1 0.7 convert_element_type.52
  9.8 0.8 copy.85
  10.6 0.8 copy.86
  11.3 1.5 copy.87.routes_ref
  12.9 0.6 fusion.13
  13.5 0.7 maximum_bitcast_fusion.columns_ref
  14.2 1.7 concatenate.14.pack_ref
  15.8 0.0 copy-done.1
  15.9 1.1 concatenate.12.rows_ref
  16.9 288.0 %shard_map.472 = (bf16[4,256,1664]{2,1,0:T(8,128)(2,1)}, bf16[8,4,48,640]{3,2,1,0:T(8,128)(2,1)}, bf16[4,2,4,48,1664]{4,3,2,1,0:T(8,128)(2,1)}, bf16[4,4,5,96,10...) custom-call(bf16[256,1664]{1,0:T(8,128)(2,1)} %concatenate.12.rows_r, ...), custom_call_target="tpu_custom_call" | custom-call | tf_op jit(solution)/shard_map/pallas_call | solution.py:1376
  305.0 15.5 %shard_map.473 = (bf16[5,512,1664]{2,1,0:T(8,128)(2,1)}, bf16[5,512,1536]{2,1,0:T(8,128)(2,1)}, bf16[8,320,256]{2,1,0:T(8,128)(2,1)}) custom-call(s32[1]{0:T(128)} %bitcast.4.first_ref, bf16[8,256,1664]{2,1,0:T(8,128)(2,1)} %get-tuple-element.85.rows_ref, bf16[8,256,1536]{2,1,0:T(8,128)(2,1)} %get-tuple-element.86.grads_ref), custom_call_target="tpu_custom_call" | custom-call | flops 1 | bytes 1 | tf_op jit(solution)/shard_map/pallas_call | solution.py:305
  320.5 0.6 stack.85.order_ref
  321.1 34.3 %shard_map.474 = (bf16[5,512,1536]{2,1,0:T(8,128)(2,1)}, bf16[5,512,1664]{2,1,0:T(8,128)(2,1)}, bf16[5,512,1024]{2,1,0:T(8,128)(2,1)}, bf16[5,512,512]{2,1,0:T(8,128)(2,1)}) custom-call(s32[1]{0:T(128)} %bitcast.4.first_ref, s32[16]{0:T(128)} %stack.85.order_ref, bf16[5,512,1664]{2,1,0:T(8,128)(2,1)} %get-tuple-element.87.rows_ref, ...), custom_call_target="tpu_custom_call" | custom-call | flops 1 | bytes 1 | tf_op jit(solution)/shard_map/pallas_call | solution.py:426
  355.4 10.1 %shard_map.475 = bf16[8,256,1536]{2,1,0:T(8,128)(2,1)} custom-call(bf16[8,320,256]{2,1,0:T(8,128)(2,1)} %get-tuple-element.92.pick_ref, bf16[5,512,1536]{2,1,0:T(8,128)(2,1)} %get-tuple-element.93.rows_ref), custom_call_target="tpu_custom_call" | custom-call | flops 1 | bytes 1 | tf_op jit(solution)/shard_map/pallas_call | solution.py:340
  365.5 0.0 reduce-scatter.2.cloned.1.call-update
  365.5 10.9 %shard_map.476.blocks_ref = bf16[8,256,1664]{2,1,0:T(8,128)(2,1)} custom-call(bf16[8,320,256]{2,1,0:T(8,128)(2,1)} %get-tuple-element.92.pick_ref, bf16[5,512,1664]{2,1,0:T(8,128)(2,1)} %get-tuple-element.95.rows_ref), custom_call_target="tpu_custom_call" | custom-call | flops 1 | bytes 1 | tf_op jit(solution)/shard_map/pallas_call | solution.py:340
  376.4 0.6 stack.86.order_ref
  377.0 23.5 %shard_map.477 = (bf16[2,5,32,4608]{3,2,1,0:T(8,128)(2,1)}, bf16[2,5,32,4608]{3,2,1,0:T(8,128)(2,1)}, bf16[2,5,32,4608]{3,2,1,0:T(8,128)(2,1)}, bf16[2,5,32,4608...) custom-call(s32[16]{0:T(128)} %stack.86.order_ref, ...), custom_call_target="tpu_custom_call" | custom-call | flops 1 | bytes 1 | tf_op jit(solution)/shard_map/pallas_call | solution.py:519
  400.5 1.7 slice.47.table_ref
  402.2 0.0 copy-done.4
  402.2 0.9 slice.36.input_ref
  403.1 153.1 %shard_map.478 = (f32[256,1536]{1,0:T(8,128)}, bf16[4,256,384]{2,1,0:T(8,128)(2,1)}, bf16[8,4,48,1664]{3,2,1,0:T(8,128)(2,1)}, bf16[4,2,5,32,4608]{4,3,2,1,0:T(8...) custom-call(bf16[8,256,1664]{2,1,0:T(8,128)(2,1)} %shard_map.476.blocks_ref, ...), custom_call_target="tpu_custom_call" | custom-call | tf_op jit(solution)/shard_map/pallas_call | solution.py:960
  556.2 128.0 %shard_map.479 = (bf16[5,32,4608]{2,1,0:T(8,128)(2,1)}, bf16[5,32,4608]{2,1,0:T(8,128)(2,1)}, bf16[5,32,4608]{2,1,0:T(8,128)(2,1)}, f32[256,1536]{1,0:T(8,128)},...) custom-call(bf16[5,32,4608]{2,1,0:T(8,128)(2,1)} %get-tuple-element.110.ready2, ...), custom_call_target="tpu_custom_call" | custom-call | tf_op jit(solution)/shard_map/pallas_call | solution.py:1125
  684.2 0.6 pad_add_fusion.places_ref
  684.8 0.0 copy-start.12
  684.8 0.0 copy-start.13
  684.8 0.0 copy-start.3
  684.8 38.2 %shard_map.480 = (f32[20,96,1024]{2,1,0:T(8,128)}, f32[20,96,1024]{2,1,0:T(8,128)}, f32[20,96,1024]{2,1,0:T(8,128)}, f32[20,96,1024]{2,1,0:T(8,128)}, f32[20,32,...) custom-call(s32[4]{0:T(128)} %pad_add_fusion.places_ref, ...), custom_call_target="tpu_custom_call" | custom-call | flops 1 | bytes 1 | tf_op jit(solution)/shard_map/pallas_call | solution.py:1582
  723.1 0.0 copy-done.7
  723.1 0.0 copy-start.14
  723.1 0.0 copy-start.15
  723.1 0.0 copy-start.16
  723.1 0.0 copy-start.5
  723.1 0.1 copy.91
  723.2 0.0 copy-done.8
  723.2 0.1 copy.92
  723.3 0.8 convert_subtract_fusion.2
  724.1 0.7 copy.97
  724.8 0.7 copy.96
  725.4 0.7 copy.95
  726.1 0.7 copy.94
  726.8 0.0 copy-done.6
  726.8 0.0 copy-start
  726.9 0.9 slice_bitcast_fusion.4
  727.8 0.9 slice_reduce_fusion
  728.8 0.0 copy-done.10
  728.8 0.0 copy-done.12
  728.8 0.0 copy-done.13
  728.8 0.0 copy-start.11
  728.8 0.5 multiply_subtract_fusion
  729.3 0.0 copy-done.3
  729.3 2.8 convert_subtract_fusion
  732.2 0.0 copy-start.9
  732.2 0.0 copy-start.2
  732.2 0.0 copy-done.14
  732.2 0.5 multiply_subtract_fusion.1
  732.7 2.2 convert_subtract_fusion.1
  735.0 2.2 fusion
  737.2 0.0 copy-done.11
  737.2 1.1 copy.113
  (22 shorter events, 0.1 us)
Async XLA Ops:
  7.2 8.6 %copy-start.1 = (bf16[256,1536]{1,0:T(8,128)(2,1)S(1)}, bf16[256,1536]{1,0:T(8,128)(2,1)}, u32[]{:S(2)}) copy-start(bf16[256,1536]{1,0:T(8,128)(2,1)} %rows_ref.1) | copy-start | bytes 2359300
  7.2 727.7 %reduce-scatter.2.cloned.1.call-start = ((), (), s32[]{:S(2)}) async-start(), calls=%async_computation.1 | async-start | bytes 7077888 | tf_op jit(solution)/shard_map/reduce_scatter | solution.py:1709
  377.0 25.2 %copy-start.4 = (bf16[256,1664]{1,0:T(8,128)(2,1)S(1)}, bf16[256,1664]{1,0:T(8,128)(2,1)}, u32[]{:S(2)}) copy-start(bf16[256,1664]{1,0:T(8,128)(2,1)} %get-tuple-element.105) | copy-start | bytes 2555908
  684.8 38.3 %copy-start.7 = (f32[48,40]{0,1:T(8,128)S(1)}, f32[48,40]{0,1:T(8,128)}, u32[]{:S(2)}) copy-start(f32[48,40]{0,1:T(8,128)} %param.42) | copy-start | bytes 23044
  684.8 38.4 %copy-start.8 = (f32[48,40]{0,1:T(8,128)S(1)}, f32[48,40]{0,1:T(8,128)}, u32[]{:S(2)}) copy-start(f32[48,40]{0,1:T(8,128)} %param.43) | copy-start | bytes 23044
  684.8 42.0 %copy-start.6 = (bf16[4,48,640]{2,1,0:T(8,128)(2,1)S(1)}, bf16[4,48,640]{2,1,0:T(8,128)(2,1)}, u32[]{:S(2)}) copy-start(bf16[4,48,640]{2,1,0:T(8,128)(2,1)} %get-tuple-element.124) | copy-start | bytes 737284
  684.8 44.0 %copy-start.10 = (bf16[48]{0:T(256)(128)(2,1)S(1)}, bf16[48]{0:T(256)(128)(2,1)}, u32[]{:S(2)}) copy-start(bf16[48]{0:T(256)(128)(2,1)} %param.38) | copy-start | bytes 292
  684.8 44.0 %copy-start.12 = (f32[48]{0:T(128)S(1)}, f32[48]{0:T(128)}, u32[]{:S(2)}) copy-start(f32[48]{0:T(128)} %param.40) | copy-start | bytes 580
  684.8 44.0 %copy-start.13 = (f32[48]{0:T(128)S(1)}, f32[48]{0:T(128)}, u32[]{:S(2)}) copy-start(f32[48]{0:T(128)} %param.39) | copy-start | bytes 580
  684.8 44.5 %copy-start.3 = (bf16[48,2560]{1,0:T(8,128)(2,1)S(1)}, bf16[48,2560]{1,0:T(8,128)(2,1)}, u32[]{:S(2)}) copy-start(bf16[48,2560]{1,0:T(8,128)(2,1)} %param.32) | copy-start | bytes 737284
  723.1 9.1 %copy-start.14 = (bf16[48]{0:T(256)(128)(2,1)S(1)}, bf16[48]{0:T(256)(128)(2,1)}, u32[]{:S(2)}) copy-start(bf16[48]{0:T(256)(128)(2,1)} %param.29) | copy-start | bytes 292
  723.1 9.1 %copy-start.15 = (f32[48]{0:T(128)S(1)}, f32[48]{0:T(128)}, u32[]{:S(2)}) copy-start(f32[48]{0:T(128)} %param.31) | copy-start | bytes 580
  723.1 9.1 %copy-start.16 = (f32[48]{0:T(128)S(1)}, f32[48]{0:T(128)}, u32[]{:S(2)}) copy-start(f32[48]{0:T(128)} %param.30) | copy-start | bytes 580
  723.1 9.6 %copy-start.5 = (bf16[48,1536]{1,0:T(8,128)(2,1)S(1)}, bf16[48,1536]{1,0:T(8,128)(2,1)}, u32[]{:S(2)}) copy-start(bf16[48,1536]{1,0:T(8,128)(2,1)} %param.35) | copy-start | bytes 442372
  726.8 8.1 %copy-start = (f32[256,1536]{1,0:T(8,128)S(1)}, f32[256,1536]{1,0:T(8,128)}, u32[]{:S(2)}) copy-start(f32[256,1536]{1,0:T(8,128)} %get-tuple-element.84.after_ref) | copy-start | bytes 4718596
  728.8 8.4 %copy-start.11 = (f32[48]{0:T(128)}, f32[48]{0:T(128)S(1)}, u32[]{:S(2)}) copy-start(f32[48]{0:T(128)S(1)} %slice_reduce_fusion) | copy-start | bytes 580
  732.2 6.2 copy-start.9
  732.2 5.0 copy-start.2
Sparse Core Ops, SparseCore 0:
  365.6 157.9 reduce-scatter.1

commit v3 on v2

--- a/solution.py
+++ b/solution.py
@@ -52,10 +52,8 @@
 def adam_step(weight, first, second, grad, decay, rate):
     new_first = BETA_ONE * first + (1.0 - BETA_ONE) * grad
     new_second = BETA_TWO * second + (1.0 - BETA_TWO) * grad * grad
-    corrected = (
-        new_first
-        / (1.0 - BETA_ONE**STEP)
-        / (jnp.sqrt(new_second / (1.0 - BETA_TWO**STEP)) + ADAM_EPS)
+    corrected = (new_first * (1.0 / (1.0 - BETA_ONE**STEP))) / (
+        jnp.sqrt(new_second * (1.0 / (1.0 - BETA_TWO**STEP))) + ADAM_EPS
     )
     old = weight.astype(jnp.float32)
     return (grad, new_first, new_second, old - rate * (corrected + decay * old))
@@ -96,17 +94,17 @@
     return jnp.where(rows <= columns, scores, -1e30)
 
 
-def project_rows(rows_ref, weight, normed_ref, query_ref, keys_ref, values_ref, flipped):
+def project_rows(rows_ref, table_ref, weight, normed_ref, query_ref, keys_ref, values_ref, flipped):
     blocks, block = rows_ref.shape[:2]
     heads, groups = query_ref.shape[0], keys_ref.shape[0]
     wide = heads * HD
     for index in range(blocks):
         span = pl.ds(index * block, block)
-        rows = rows_ref[index, :, :D].astype(jnp.float32)
+        rows = rows_ref[index].astype(jnp.float32)
         factor = lax.rsqrt(jnp.mean(rows * rows, axis=-1, keepdims=True) + EPS_NORM)
         normed = (rows * factor).astype(jnp.bfloat16)
         normed_ref[span, :] = normed
-        tables = lane_tables(rows_ref[index, :, D : D + 128])
+        tables = lane_tables(table_ref[index])
         mixed = jnp.dot(normed, weight, preferred_element_type=jnp.float32)
         for column in range(0, wide + 2 * groups * HD, 128):
             part = mixed[:, column : column + 128]
@@ -152,8 +150,8 @@
     out_ref[index] = jnp.concatenate(outputs, 0).T.astype(jnp.bfloat16)
 
 
-def attend_kernel(rows_ref, weight_ref, normed_ref, query_ref, keys_ref, values_ref, out_ref, flipped):
-    project_rows(rows_ref, weight_ref[...], normed_ref, query_ref, keys_ref, values_ref, flipped)
+def attend_kernel(rows_ref, table_ref, weight_ref, normed_ref, query_ref, keys_ref, values_ref, out_ref, flipped):
+    project_rows(rows_ref, table_ref, weight_ref[...], normed_ref, query_ref, keys_ref, values_ref, flipped)
     for index in range(rows_ref.shape[0]):
         attend_rows(index, rows_ref.shape[1], query_ref, keys_ref, out_ref, flipped)
 
@@ -232,14 +230,14 @@
         out_ref[span, wide + groups * HD :] = values.astype(jnp.bfloat16)
 
 
-def attend_forward(rows, weight, heads, groups):
+def attend_forward(rows, table, weight, heads, groups):
     return pl.pallas_call(
         attend_kernel,
         out_shape=attend_shapes(rows.shape, heads, groups),
         scratch_shapes=[pltpu.VMEM((groups * HD, rows.shape[0] * rows.shape[1]), jnp.bfloat16)],
         compiler_params=pltpu.CompilerParams(vmem_limit_bytes=48 * 1024 * 1024),
         cost_estimate=pl.CostEstimate(flops=1, bytes_accessed=1, transcendentals=0),
-    )(rows, weight)
+    )(rows, table, weight)
 
 
 def attend_backward(table, query, keys, values, grad):
@@ -351,14 +349,16 @@
     )(pick, rows)
 
 
-def expert_kernel(first_ref, order_ref, rows_ref, grads_ref, *refs):
-    produced_ref, grad_rows_ref, grad_hidden_ref, gated_ref, whole_in, whole_out = refs[-6:]
-    pieces = refs[:-6]
+def expert_kernel(first_ref, order_ref, slots_ref, rows_ref, grads_ref, *refs):
+    whole_in, whole_out, total_in, total_out = refs[-4:]
+    pieces, (produced_ref, grad_rows_ref), outs = refs[:2], refs[2:4], refs[4:-4]
     expert = first_ref[0] + pl.program_id(0)
-
-    @pl.when(pl.program_id(1) == 0)
+    chunk = pl.program_id(1)
+    parted = len(pieces[0].shape) == 4
+
+    @pl.when(chunk == 0)
     def assemble():
-        if len(pieces[0].shape) == 3:
+        if not parted:
             whole_in[...] = pieces[0][0]
             whole_out[...] = pieces[1][0]
             return
@@ -380,7 +380,6 @@
     activated = gate_half * sigma
     middle = activated * up_half
     gated = (gate * middle).astype(jnp.bfloat16)
-    gated_ref[0] = gated
     produced_ref[0] = jnp.dot(gated, whole_out[...], preferred_element_type=jnp.float32).astype(
         jnp.bfloat16
     )
@@ -396,7 +395,6 @@
     grad_hidden = jnp.concatenate(
         [grad_middle * up_half * slope, grad_middle * activated], -1
     ).astype(jnp.bfloat16)
-    grad_hidden_ref[0] = grad_hidden
     grad_rows_ref[0, :, :D] = lax.dot_general(
         grad_hidden,
         whole_in[...],
@@ -409,66 +407,12 @@
     )
     grad_rows_ref[0, :, D:] = spread.astype(jnp.bfloat16)
 
-
-def run_experts(first, order, rows, grads, pieces, hidden):
-    count, slots, wide = rows.shape
-    chunk = min(512, slots)
-    by_chunk = lambda e, c, *_: (e, c, 0)
-    if len(pieces[0].shape) == 4:
-        piece_specs = [
-            pl.BlockSpec((piece.shape[0], 1) + piece.shape[2:], lambda e, c, *_: (0, e, 0, 0))
-            for piece in pieces
-        ]
-    else:
-        piece_specs = [
-            pl.BlockSpec((1,) + piece.shape[1:], lambda e, c, *_: (e, 0, 0)) for piece in pieces
-        ]
-    return pl.pallas_call(
-        expert_kernel,
-        grid_spec=pltpu.PrefetchScalarGridSpec(
-            num_scalar_prefetch=2,
-            grid=(count, slots // chunk),
-            in_specs=[
-                pl.BlockSpec((1, chunk, wide), by_chunk),
-                pl.BlockSpec((1, chunk, D), by_chunk),
-            ]
-            + piece_specs,
-            out_specs=(
-                pl.BlockSpec((1, chunk, D), by_chunk),
-                pl.BlockSpec((1, chunk, wide), by_chunk),
-                pl.BlockSpec((1, chunk, 2 * hidden), by_chunk),
-                pl.BlockSpec((1, chunk, hidden), by_chunk),
-            ),
-            scratch_shapes=[
-                pltpu.VMEM((D, 2 * hidden), jnp.bfloat16),
-                pltpu.VMEM((hidden, D), jnp.bfloat16),
-            ],
-        ),
-        out_shape=(
-            jax.ShapeDtypeStruct((count, slots, D), jnp.bfloat16),
-            jax.ShapeDtypeStruct((count, slots, wide), jnp.bfloat16),
-            jax.ShapeDtypeStruct((count, slots, 2 * hidden), jnp.bfloat16),
-            jax.ShapeDtypeStruct((count, slots, hidden), jnp.bfloat16),
-        ),
-        compiler_params=pltpu.CompilerParams(vmem_limit_bytes=62 * 1024 * 1024),
-        cost_estimate=pl.CostEstimate(flops=1, bytes_accessed=1, transcendentals=0),
-    )(first, order, rows, grads, *pieces)
-
-
-def weight_grad_kernel(order_ref, rows_ref, grads_ref, hidden_ref, gated_ref, *refs):
-    outs, total_in, total_out = refs[:-2], refs[-2], refs[-1]
-    chunk = pl.program_id(1)
+    turned = (((0,), (0,)), ((), ()))
     part_in = lax.dot_general(
-        rows_ref[0, :, :D],
-        hidden_ref[0],
-        (((0,), (0,)), ((), ())),
-        preferred_element_type=jnp.float32,
+        rows_ref[0, :, :D], grad_hidden, turned, preferred_element_type=jnp.float32
     )
     part_out = RESIDUAL_SCALE * lax.dot_general(
-        gated_ref[0],
-        grads_ref[0],
-        (((0,), (0,)), ((), ())),
-        preferred_element_type=jnp.float32,
+        gated, grads_ref[0], turned, preferred_element_type=jnp.float32
     )
 
     @pl.when(chunk == 0)
@@ -483,7 +427,7 @@
 
     @pl.when(chunk == pl.num_programs(1) - 1)
     def finish():
-        if len(outs) == 2:
+        if not parted:
             outs[0][0] = total_in[...].astype(jnp.bfloat16)
             outs[1][0] = total_out[...].astype(jnp.bfloat16)
             return
@@ -493,7 +437,7 @@
         folds = (outs[0].shape[3] - D) // wide
         for number, out in enumerate(outs):
             for turn in range(turns):
-                block = order_ref[number * turns + turn]
+                block = slots_ref[number * turns + turn]
                 for fold in range(folds):
                     start = pl.multiple_of((block * folds + fold) * deep, deep)
                     out[turn, 0, :, fold * wide : (fold + 1) * wide] = total_in[
@@ -505,38 +449,58 @@
                 )
 
 
-def weight_grads(order, rows, grads, grad_hidden, gated, shapes):
+def run_experts(first, order, rows, grads, pieces, hidden, parted):
     count, slots, wide = rows.shape
-    hidden = gated.shape[2]
     chunk = min(512, slots)
     by_chunk = lambda e, c, *_: (e, c, 0)
-    if len(shapes) == 2:
-        out_specs = tuple(pl.BlockSpec((1,) + s[1:], lambda e, c, *_: (e, 0, 0)) for s in shapes)
+    by_expert = lambda e, c, *_: (e, 0, 0)
+    by_turn = lambda e, c, *_: (0, e, 0, 0)
+    if parted:
+        _, _, shards, ctx = block_order()
+        places = []
+        for step in reversed(range(shards)):
+            for bit in (1, 0):
+                places += [step * ctx + turn for turn in range(bit, ctx, 2)]
+        places = jnp.stack([order[place] for place in places])
+        deep = pieces[1].shape[2]
+        folds = pieces[0].shape[2] // deep
+        shapes = [(ctx // 2, count, deep, folds * 2 * hidden + D)] * (2 * shards)
+        block = lambda shape: pl.BlockSpec((shape[0], 1) + shape[2:], by_turn)
     else:
-        out_specs = tuple(
-            pl.BlockSpec((s[0], 1) + s[2:], lambda e, c, *_: (0, e, 0, 0)) for s in shapes
-        )
-    return pl.pallas_call(
-        weight_grad_kernel,
+        places = order
+        shapes = [(count, D, 2 * hidden), (count, hidden, D)]
+        block = lambda shape: pl.BlockSpec((1,) + shape[1:], by_expert)
+    outs = pl.pallas_call(
+        expert_kernel,
         grid_spec=pltpu.PrefetchScalarGridSpec(
-            num_scalar_prefetch=1,
+            num_scalar_prefetch=3,
             grid=(count, slots // chunk),
             in_specs=[
                 pl.BlockSpec((1, chunk, wide), by_chunk),
                 pl.BlockSpec((1, chunk, D), by_chunk),
-                pl.BlockSpec((1, chunk, 2 * hidden), by_chunk),
-                pl.BlockSpec((1, chunk, hidden), by_chunk),
-            ],
-            out_specs=out_specs,
+            ]
+            + [block(piece.shape) for piece in pieces],
+            out_specs=(
+                pl.BlockSpec((1, chunk, D), by_chunk),
+                pl.BlockSpec((1, chunk, wide), by_chunk),
+            )
+            + tuple(block(shape) for shape in shapes),
             scratch_shapes=[
+                pltpu.VMEM((D, 2 * hidden), jnp.bfloat16),
+                pltpu.VMEM((hidden, D), jnp.bfloat16),
                 pltpu.VMEM((D, 2 * hidden), jnp.float32),
                 pltpu.VMEM((hidden, D), jnp.float32),
             ],
         ),
-        out_shape=tuple(jax.ShapeDtypeStruct(s, jnp.bfloat16) for s in shapes),
+        out_shape=(
+            jax.ShapeDtypeStruct((count, slots, D), jnp.bfloat16),
+            jax.ShapeDtypeStruct((count, slots, wide), jnp.bfloat16),
+        )
+        + tuple(jax.ShapeDtypeStruct(shape, jnp.bfloat16) for shape in shapes),
         compiler_params=pltpu.CompilerParams(vmem_limit_bytes=62 * 1024 * 1024),
         cost_estimate=pl.CostEstimate(flops=1, bytes_accessed=1, transcendentals=0),
-    )(order, rows, grads, grad_hidden, gated)
+    )(first, order, places, rows, grads, *pieces)
+    return outs[0], outs[1], outs[2:]
 
 
 def swap(rows, axis, flip):
@@ -683,7 +647,7 @@
 
 
 class Fold:
-    def __init__(self, blocks_ref, out_ref, over, sums, parts, sends, receives):
+    def __init__(self, blocks_ref, out_ref, over, sums, parts, sends, receives, local=None):
         z, y = lax.axis_index("dp"), lax.axis_index("expert")
         self.inner = z * (3 - z) > 0
         self.outer = z * (3 - z) < 1
@@ -704,6 +668,10 @@
             )
 
         self.slot = slot
+        self.staged = [
+            pltpu.make_async_copy(blocks_ref.at[slot(flip, y)], sums.at[flip], local.at[flip])
+            for flip in range(4 if local is not None else 0)
+        ]
         self.across = [
             hand(flip, blocks_ref.at[slot(flip, 1 - y)], over.at[flip], 1, "expert")
             for flip in range(4)
@@ -714,9 +682,12 @@
 
     def own(self, flip):
         self.across[flip].wait_recv()
-        return self.blocks[self.slot(flip, self.y)].astype(jnp.float32) + self.over[flip].astype(
-            jnp.float32
-        )
+        if self.staged:
+            self.staged[flip].wait()
+            held = self.sums[flip]
+        else:
+            held = self.blocks[self.slot(flip, self.y)]
+        return held.astype(jnp.float32) + self.over[flip].astype(jnp.float32)
 
     def part(self, number):
         return self.parts[number].astype(jnp.float32)
@@ -732,18 +703,25 @@
             for flip in (3, 2, 1, 0):
                 self.across[flip].start()
 
-    def early(self, k):
-        @pl.when(self.inner)
-        def inner():
-            total = self.own(2 + k)
-            self.to_line[k].wait_recv()
-            self.sums[2 + k] = (total + self.part(k)).astype(jnp.bfloat16)
-            self.to_middle[k].start()
-
-        @pl.when(self.outer)
-        def outer():
-            self.sums[3 - k] = self.own(3 - k).astype(jnp.bfloat16)
-            self.to_line[k].start()
+        for copy in self.staged:
+            copy.start()
+
+    def early(self, k, ends=True, middle=True):
+        if middle:
+
+            @pl.when(self.inner)
+            def inner():
+                total = self.own(2 + k)
+                self.to_line[k].wait_recv()
+                self.sums[2 + k] = (total + self.part(k)).astype(jnp.bfloat16)
+                self.to_middle[k].start()
+
+        if ends:
+
+            @pl.when(self.outer)
+            def outer():
+                self.sums[3 - k] = self.own(3 - k).astype(jnp.bfloat16)
+                self.to_line[k].start()
 
     def late(self):
         @pl.when(self.inner)
@@ -823,16 +801,20 @@
 
 
 def returning_kernel(
-    blocks_ref, give3, keep3, give2, keep2, give1, keep1, give0,
+    blocks_ref, moe_blocks, give3, keep3, give2, keep2, give1, keep1, give0,
     after_ref, input_ref, gates_ref, grad_ref, gain_ref, pack_ref, attended_ref,
-    grad_after_ref, seq_grad_ref, grad_pack_ref, arrived, done3, ready2, ready1,
-    routed, over, sums, parts, fold_sends, fold_receives,
+    grad_after_ref, seq_grad_ref, grad_pack_ref, output_ref, arrived, done3, ready2, ready1,
+    routed, over, sums, parts, fold_sends, fold_receives, fold_local,
+    moe_over, moe_sums, moe_parts, moe_sends, moe_receives, moe_local,
     sent, crossed, stage, outgoing, sends, receives, local,
 ):
     z, c = lax.axis_index("dp"), lax.axis_index("ctx")
     greet(EVERYONE)
     link = Link(sends, receives)
-    fold = Fold(blocks_ref, routed, over, sums, parts, fold_sends, fold_receives)
+    fold = Fold(blocks_ref, routed, over, sums, parts, fold_sends, fold_receives, fold_local)
+    moe_fold = Fold(
+        moe_blocks, routed.at[:, :D], moe_over, moe_sums, moe_parts, moe_sends, moe_receives, moe_local
+    )
     gives = {3: give3, 2: give2, 1: give1, 0: give0}
     keeps = {3: keep3, 2: keep2, 1: keep1}
     core = {step: link.push(gives[step], arrived.at[step], "ctx", 1) for step in (3, 2, 1, 0)}
@@ -883,7 +865,9 @@
         close_one(item)
     cross(1, False)
     fold.late()
+    moe_fold.start()
     fold.last()
+    moe_fold.early(0, middle=False)
 
     gates = gates_ref[...]
     high = routed[:, D:]
@@ -916,13 +900,15 @@
         link.push(outgoing.at[near(c, "ctx", flip)], seq_grad_ref.at[c], "ctx", flip)
         for flip in (1, 2, 3)
     ]
+    moe_fold.early(0, ends=False)
+    moe_fold.early(1, middle=False)
     close(2)
     keep_ready = [pltpu.make_async_copy(sent.at[1], ready2, local.at[0])]
     keep_ready[0].start()
     turned = (((0,), (0,)), ((), ()))
     column = (lane == EXPERTS).astype(jnp.bfloat16)
     small = lax.dot_general(
-        input_ref[...], grad_logits, turned, preferred_element_type=jnp.float32
+        input_ref[:, :D], grad_logits, turned, preferred_element_type=jnp.float32
     ) + lax.dot_general(
         (grad_input * normed).astype(jnp.bfloat16),
         column,
@@ -931,6 +917,7 @@
     )
     small = small.astype(jnp.bfloat16).reshape(grad_pack_ref.shape[:3] + (128,))
     grad_pack_ref[..., D:] = small
+    moe_fold.early(1, ends=False)
     some = grad_pack_ref.shape[0] // outgoing.shape[0]
     for index in range(outgoing.shape[0]):
         part = lax.dot_general(
@@ -940,8 +927,12 @@
             (some,) + grad_pack_ref.shape[1:3] + (D,)
         )
     keep_ready[0].wait()
+    moe_fold.late()
     close(1)
     fetch([(sent.at[0], ready1)], local)
+    moe_fold.last()
+    output_ref[...] = (after_ref[...] + RESIDUAL_SCALE * routed[:, :D]).astype(jnp.bfloat16)
+    moe_fold.finish()
     for copy in spread + line + [core[0]]:
         copy.wait_recv()
     fold.finish()
@@ -949,7 +940,7 @@
         copy.wait_send()
 
 
-def returning(blocks, parts, after, expert_input, gates, grads, gain, pack, attended, number):
+def returning(blocks, moe_blocks, parts, after, expert_input, gates, grads, gain, pack, attended, number):
     kind = jnp.bfloat16
     far = pl.BlockSpec(memory_space=pl.ANY)
     held = pl.BlockSpec(memory_space=pltpu.VMEM)
@@ -963,16 +954,20 @@
             jax.ShapeDtypeStruct((tokens, D), jnp.float32),
             jax.ShapeDtypeStruct(attended.shape, kind),
             jax.ShapeDtypeStruct((8, ctx, D // (8 * ctx), shape[1]), kind),
+            jax.ShapeDtypeStruct((tokens, D), kind),
             jax.ShapeDtypeStruct((4,) + give3.shape, kind),
             jax.ShapeDtypeStruct(piece, kind),
             jax.ShapeDtypeStruct(piece, kind),
             jax.ShapeDtypeStruct(piece, kind),
         ),
-        in_specs=[held] + [far] * 7 + [held] * 7,
-        out_specs=(held, held, held, far, far, far, far),
+        in_specs=[far] * 9 + [held] * 7,
+        out_specs=(held, held, held, held, far, far, far, far),
         scratch_shapes=[pltpu.VMEM(shape, jnp.float32)]
         + fold_scratch(shape)
+        + [pltpu.SemaphoreType.DMA((4,))]
+        + fold_scratch((tokens, D))
         + [
+            pltpu.SemaphoreType.DMA((4,)),
             pltpu.VMEM((3,) + piece, kind),
             pltpu.VMEM((3,) + piece, kind),
             pltpu.VMEM((4,) + piece, kind),
@@ -982,10 +977,10 @@
             pltpu.SemaphoreType.DMA((2,)),
         ],
         compiler_params=pltpu.CompilerParams(
-            collective_id=number, has_side_effects=True, vmem_limit_bytes=62 * 1024 * 1024
+            collective_id=number, has_side_effects=True, vmem_limit_bytes=63 * 1024 * 1024
         ),
     )(
-        blocks, give3, keep3, give2, keep2, give1, keep1, give0,
+        blocks, moe_blocks, give3, keep3, give2, keep2, give1, keep1, give0,
         after, expert_input, gates, grads, gain, pack, attended,
     )
 
@@ -1211,8 +1206,8 @@
 
 
 def opening_kernel(
-    rows_ref, columns_ref, pack_ref, weights_in, weights_out, grads_ref, routes_ref,
-    all_rows, all_columns, all_pack, pieces_in, pieces_out, all_grads, all_packed,
+    rows_ref, table_ref, columns_ref, pack_ref, weights_in, weights_out, grads_ref, routes_ref,
+    all_rows, all_table, all_columns, all_pack, pieces_in, pieces_out, all_grads, all_packed,
     after_ref, gates_ref, gain_ref, packed,
     normed_ref, query_ref, keys_ref, values_ref, attended_ref,
     outgoing, flipped, sends, receives, line_sends, line_receives, token_sends, token_receives, locals_,
@@ -1269,11 +1264,13 @@
         keep(3, rows_ref, all_rows.at[c]),
         keep(4, pack_ref, all_pack.at[z, y, c]),
         keep(5, grads_ref, all_grads.at[own]),
+        keep(7, table_ref, all_table.at[c]),
     ]
     cut = [
         link.push(columns_ref.at[c_at(flip)], all_columns.at[own, c], "ctx", flip)
         for flip in (1, 2, 3)
     ]
+    table_all = [link.push(table_ref, all_table.at[c], "ctx", flip) for flip in (1, 2, 3)]
     rows_over = link.push(rows_ref, all_rows.at[c], "ctx", 2)
     rows_core = link.push(rows_ref, all_rows.at[c], "ctx", 1)
     pack_line = [link.push(pack_ref, all_pack.at[z, y, c], "dp", flip) for flip in (1, 2, 3)]
@@ -1300,10 +1297,12 @@
     arrive([pack_over])
     pack_pair = link.push(all_pack.at[:, :, c], all_pack.at[:, :, c], "ctx", 2)
     pack_core = link.push(all_pack.at[:, :, c], all_pack.at[:, :, c], "ctx", 1)
-    arrive([rows_core, rows_pass] + column_over)
+    arrive([rows_core, rows_pass] + column_over + table_all)
     kept[3].wait()
+    kept[6].wait()
     project_rows(
         all_rows,
+        all_table,
         all_columns[...].reshape(D, all_columns.shape[-1]),
         normed_ref,
         query_ref,
@@ -1317,17 +1316,17 @@
         link.push(outgoing.at[c_at(flip)], attended_ref.at[c], "ctx", flip) for flip in (1, 2, 3)
     ]
     attended_ref[c] = outgoing[c]
-    line.first()
     arrive([pack_pair])
     pack_last = link.push(all_pack.at[:, :, c_at(2)], all_pack.at[:, :, c_at(2)], "ctx", 1)
+    arrive([pack_core, pack_last] + attended)
+    route_rows(
+        all_rows[c], all_pack, attended_ref, routes_ref, after_ref, gates_ref, gain_ref, packed
+    )
+    token_line.start()
+    kept.append(keep(6, packed, all_packed.at[own]))
+    line.first()
     arrive(shared[0][0])
     passed = hand_on(0)
-    arrive([pack_core, pack_last] + attended)
-    route_rows(
-        all_rows[c, :, :D], all_pack, attended_ref, routes_ref, after_ref, gates_ref, gain_ref, packed
-    )
-    token_line.start()
-    kept.append(keep(6, packed, all_packed.at[own]))
     arrive(moved[1])
     shared.append(share(1))
     line.second()
@@ -1355,7 +1354,7 @@
         arrive(shared[3 + item][0])
         passed += hand_on(3, item)
     kept[5].wait()
-    kept[6].wait()
+    kept[7].wait()
     arrive(passed)
     for over, core in shared:
         arrive(core)
@@ -1364,12 +1363,12 @@
     link.finish()
 
 
-def opening(rows, columns, pack, weights_in, weights_out, grads, routes, heads, groups, number):
+def opening(rows, table, columns, pack, weights_in, weights_out, grads, routes, heads, groups, number):
     ctx = columns.shape[0]
     shards, count = weights_in.shape[:2]
     tokens = rows.shape[0]
     kind = jnp.bfloat16
-    copies = 24 + 2 * (2 + 3 * 3 + 5 * count)
+    copies = 27 + 2 * (2 + 3 * 3 + 5 * count)
     far = pl.BlockSpec(memory_space=pl.ANY)
     held = pl.BlockSpec(memory_space=pltpu.VMEM)
     all_rows = (ctx,) + rows.shape
@@ -1377,20 +1376,21 @@
         opening_kernel,
         out_shape=(
             jax.ShapeDtypeStruct(all_rows, kind),
+            jax.ShapeDtypeStruct((ctx,) + table.shape, kind),
             jax.ShapeDtypeStruct((8,) + columns.shape, kind),
             jax.ShapeDtypeStruct((shards, 2, ctx) + pack.shape, kind),
             jax.ShapeDtypeStruct((shards, ctx) + weights_in.shape[1:], kind),
             jax.ShapeDtypeStruct((shards, ctx) + weights_out.shape[1:], kind),
             jax.ShapeDtypeStruct((8,) + grads.shape, kind),
-            jax.ShapeDtypeStruct((8,) + rows.shape, kind),
+            jax.ShapeDtypeStruct((8, tokens, D + 128), kind),
             jax.ShapeDtypeStruct((tokens, D), jnp.float32),
             jax.ShapeDtypeStruct((tokens, 128), jnp.float32),
             jax.ShapeDtypeStruct((1, D), jnp.float32),
-            jax.ShapeDtypeStruct(rows.shape, kind),
+            jax.ShapeDtypeStruct((tokens, D + 128), kind),
         )
         + attend_shapes(all_rows, heads, groups),
-        in_specs=[far] * 6 + [held],
-        out_specs=(held, held, held, far, far, far, far) + (held,) * 9,
+        in_specs=[far] * 7 + [held],
+        out_specs=(held, held, held, held, far, far, far, far) + (held,) * 9,
         scratch_shapes=[
             pltpu.VMEM((ctx, rows.shape[0], heads * HD), kind),
             pltpu.VMEM((groups * HD, ctx * rows.shape[0]), kind),
@@ -1400,12 +1400,12 @@
             pltpu.SemaphoreType.DMA((8,)),
             pltpu.SemaphoreType.DMA((9,)),
             pltpu.SemaphoreType.DMA((8,)),
-            pltpu.SemaphoreType.DMA((7,)),
+            pltpu.SemaphoreType.DMA((8,)),
         ],
         compiler_params=pltpu.CompilerParams(
             collective_id=number, has_side_effects=True, vmem_limit_bytes=56 * 1024 * 1024
         ),
-    )(rows, columns, pack, weights_in, weights_out, grads, routes)
+    )(rows, table, columns, pack, weights_in, weights_out, grads, routes)
 
 
 def split_high_low(values):
@@ -1503,27 +1503,10 @@
     return [all_in.reshape(count, -1, 2 * part), all_out]
 
 
-def piece_grads(order, rows, grads, grad_hidden, gated, pieces_in, pieces_out):
-    _, _, shards, ctx = block_order()
-    count, deep = pieces_out.shape[1:3]
-    folds = pieces_in.shape[2] // deep
-    shape = (ctx // 2, count, deep, folds * pieces_in.shape[3] + pieces_out.shape[3])
-    slots = []
-    for step in reversed(range(shards)):
-        for bit in (1, 0):
-            slots += [step * ctx + turn for turn in range(bit, ctx, 2)]
-    order = jnp.stack([order[slot] for slot in slots])
-    return weight_grads(order, rows, grads, grad_hidden, gated, [shape] * (2 * shards))
-
-
-def collect_weights(order, rows, grads, grad_hidden, gated, expert_in, expert_out):
-    place, column, shards, ctx = block_order()
-    depth_in, depth_out = expert_in.shape[1], expert_out.shape[1]
-    count = expert_in.shape[0]
+def collect_weights(grad_in, grad_out):
+    shards = lax.axis_size("dp")
+    count = grad_in.shape[0]
     part = FFE // shards
-    blocks = shards * ctx
-    shapes = ((count, blocks * depth_in, 2 * part), (count, part, D))
-    grad_in, grad_out = weight_grads(order, rows, grads, grad_hidden, gated, shapes)
     part_in = lax.psum_scatter(
         grad_in.reshape(count, shards, -1, 2, part), "ctx", scatter_dimension=2, tiled=True
     )
@@ -1638,7 +1621,6 @@
     table = jnp.concatenate(split_high_low(jnp.cos(angles)) + split_high_low(jnp.sin(angles)), 1)
     gain_attend_wide = gain_attend.astype(jnp.float32)[:, None]
     scaled_in = (gain_attend_wide * project_in.astype(jnp.float32)).astype(jnp.bfloat16)
-    rows = jnp.concatenate([tokens, table], 1)
     columns = group_columns(scaled_in, ctx)
     pack_out = jnp.concatenate(
         [project_out, router_weight, gain_expert[:, None], pad_columns(project_out, 87)], 1
@@ -1647,26 +1629,25 @@
     if close:
         parted = lambda array: array.reshape((shards, -1) + array.shape[1:])
         (
-            seq_rows, own_in, full_pack_out, all_in, all_out, all_grads, all_packed,
+            _, seq_table, own_in, full_pack_out, all_in, all_out, all_grads, all_packed,
             after, gates_wide, gain_two, packed,
             seq_normed, query, keys, values, attended_heads,
         ) = opening(
-            rows, columns, pack_out, parted(expert_in), parted(expert_out), cotangent, routes,
+            tokens, table, columns, pack_out, parted(expert_in), parted(expert_out), cotangent, routes,
             heads, groups, 1,
         )
-        expert_input = packed[:, :D]
         pieces = [array.reshape((-1,) + array.shape[2:]) for array in (all_in, all_out)]
     else:
-        seq_rows = gather_ctx(rows)
+        seq_rows, seq_table = gather_ctx(tokens), gather_ctx(table)
         own_in = lax.all_gather(exchange_ctx(columns), owners, axis=0, tiled=False)
         full_pack_out = lax.all_gather(pack_out, everywhere, axis=0, tiled=True)
         all_grads = lax.all_gather(cotangent, owners, axis=0, tiled=False)
         pieces = spread_weights(expert_in, expert_out)
         seq_normed, query, keys, values, seq_attended = attend_forward(
-            seq_rows, own_in.reshape(D, -1), heads, groups
+            seq_rows, seq_table, own_in.reshape(D, -1), heads, groups
         )
         attended_heads = exchange_ctx(seq_attended)
-    seq_rows = seq_rows.reshape(-1, D + 128)
+    seq_table = seq_table.reshape(-1, 128)
     own_in = own_in.reshape(D, -1)
     full_pack_out = full_pack_out.reshape(H * HD, -1)
     if not close:
@@ -1700,21 +1681,21 @@
         first = first + lax.axis_index("dp") * count
     first = first.astype(jnp.int32).reshape(1)
     slot_rows, slot_grads, pick = dispatch(first, all_packed, all_grads, count)
-    produced, grad_rows, grad_hidden, gated = run_experts(
-        first, order, slot_rows, slot_grads, pieces, hidden
+    produced, grad_rows, parts = run_experts(
+        first, order, slot_rows, slot_grads, pieces, hidden, close
     )
     shared_grads = combine(pick, grad_rows)
     shared = combine(pick, produced)
-    gated, shared = lax.optimization_barrier((gated, shared))
-    moe = lax.psum_scatter(shared, owners, scatter_dimension=0, tiled=False).astype(jnp.float32)
     if close:
         place = lax.axis_index("dp")
-        parts = piece_grads(order, slot_rows, slot_grads, grad_hidden, gated, *pieces)
-        grad_after, seq_grad, grad_pack_out, arrived, done3, ready2, ready1 = returning(
+        (
+            grad_after, seq_grad, grad_pack_out, block_output, arrived, done3, ready2, ready1,
+        ) = returning(
             shared_grads,
+            shared,
             parts,
             after,
-            expert_input,
+            packed,
             gates_wide,
             cotangent,
             gain_two,
@@ -1727,7 +1708,7 @@
             ready1,
             parts[7],
             arrived,
-            seq_rows[:, D:],
+            seq_table,
             query,
             keys,
             values,
@@ -1749,9 +1730,9 @@
         grad_routed = lax.psum_scatter(
             shared_grads, owners, scatter_dimension=0, tiled=False
         ).astype(jnp.float32)
-        expert_grads = collect_weights(
-            order, slot_rows, slot_grads, grad_hidden, gated, expert_in, expert_out
-        )
+        moe = lax.psum_scatter(shared, owners, scatter_dimension=0, tiled=False)
+        block_output = (after + RESIDUAL_SCALE * moe.astype(jnp.float32)).astype(jnp.bfloat16)
+        expert_grads = collect_weights(*parts)
         grad_final = cotangent.astype(jnp.float32)
         grad_gates = grad_routed[:, D : D + EXPERTS] + grad_routed[:, D + EXPERTS : D + 2 * EXPERTS]
         grad_picked = gates * (grad_gates - jnp.sum(gates * grad_gates, axis=-1, keepdims=True))
@@ -1768,7 +1749,7 @@
         seq_grad = exchange_ctx(
             grad_attended.reshape(rows_local, ctx, heads * HD).transpose(1, 0, 2)
         )
-        grad_mixed = attend_backward(seq_rows[:, D:], query, keys, values, seq_grad)
+        grad_mixed = attend_backward(seq_table, query, keys, values, seq_grad)
         grad_in_part = jnp.einsum(
             "td,tc->dc", seq_normed, grad_mixed, preferred_element_type=jnp.float32
         ).astype(jnp.bfloat16)
@@ -1801,7 +1782,6 @@
         shard_pack_out = lax.psum_scatter(
             grad_pack_out, everywhere, scatter_dimension=0, tiled=True
         ).astype(jnp.float32)
-    block_output = (after + RESIDUAL_SCALE * moe).astype(jnp.bfloat16)
     shard_scaled = ungroup_columns(shard_columns).astype(jnp.float32)
     shard_in = gain_attend_wide * shard_scaled
     shard_attend = jnp.sum(shard_scaled * project_in.astype(jnp.float32), axis=1)

time: 757 us -> 722 us (0.954)
  Pallas kernels: 702 us -> 688 us
  between operations: 14.8 us -> 1.22 us
    pallas_call x1, Pallas kernels: 153 us -> 177 us  [returning(): pl.pallas_call(returning_kernel, out_shape=(jax.ShapeDtypeStruct((tokens,...]
    pallas_call x1 -> x0, Pallas kernels: 23.5 us -> none  [weight_grads(): pl.pallas_call(weight_grad_kernel, grid_spec=pltpu.PrefetchScalarGridSpec...]
    pallas_call x1, Pallas kernels: 128 us -> 105 us  [closing(): pl.pallas_call(closing_kernel, out_shape=(jax.ShapeDtypeStruct(piece, kin...]
    pallas_call x1, Pallas kernels: 34.3 us -> 51 us  [run_experts(): pl.pallas_call(expert_kernel, grid_spec=pltpu.PrefetchScalarGridSpec(num_...]
    pallas_call x1, Pallas kernels: 288 us -> 280 us  [opening(): pl.pallas_call(opening_kernel, out_shape=(jax.ShapeDtypeStruct(all_rows,...]
  transfers between devices with their start and end apart: 1 -> 0, of which waited for: 0 -> 0; matrix products, arithmetic and copies ran while one was open for 2% -> 0% of each run, Pallas kernels for 47% -> 0%
where the time goes in v3:
time: 722 us; the launch traced here: 712 us
  Pallas kernels  688 us (95%)
  local copies, waits for them, and re-layouts  14.2 us (2%)
  other arithmetic  8.94 us (1%)
    pallas_call x1, Pallas kernels, opening(): pl.pallas_call(opening_kernel, out_shape=(jax.ShapeDtypeStruct(all_rows,...  280 us
    pallas_call x1, Pallas kernels, returning(): pl.pallas_call(returning_kernel, out_shape=(jax.ShapeDtypeStruct((tokens,...  177 us
    pallas_call x1, Pallas kernels, closing(): pl.pallas_call(closing_kernel, out_shape=(jax.ShapeDtypeStruct(piece, kin...  105 us
    pallas_call x1, Pallas kernels, run_experts(): pl.pallas_call(expert_kernel, grid_spec=pltpu.PrefetchScalarGridSpec(num_...  51 us
    pallas_call x1, Pallas kernels, expert_step(): pl.pallas_call(expert_step_kernel, grid_spec=pltpu.PrefetchScalarGridSpec...  38.2 us
    pallas_call x2, Pallas kernels, combine(): pl.pallas_call(combine_kernel, grid=(sources,), in_specs=[pl.BlockSpec((1...  20.7 us
    pallas_call x1, Pallas kernels, dispatch(): pl.pallas_call(dispatch_kernel, grid_spec=pltpu.PrefetchScalarGridSpec(nu...  15.5 us

profile of v3, /device:TPU:0, one launch (start us, length us, event | category | flops | bytes accessed | tf_op | source)
XLA Modules:
  0.0 712.3 jit_solution(202203351603982148)
XLA Ops:
  0.7 0.7 convert_element_type.45
  1.4 0.6 fusion.9
  1.9 0.8 pad_maximum_fusion.1.table_ref
  2.7 0.7 convert_element_type.52
  3.4 1.1 fusion.1
  4.5 0.7 maximum_bitcast_fusion.columns_ref
  5.2 0.8 copy.85
  6.0 0.8 copy.86
  6.8 1.7 concatenate.14.pack_ref
  8.4 1.5 copy.87.routes_ref
  9.9 280.2 %shard_map.472 = (bf16[4,256,1536]{2,1,0:T(8,128)(2,1)}, bf16[4,256,128]{2,1,0:T(8,128)(2,1)}, bf16[8,4,48,640]{3,2,1,0:T(8,128)(2,1)}, bf16[4,2,4,48,1664]{4,3,...) custom-call(bf16[256,1536]{1,0:T(8,128)(2,1)} %rows_ref.3, ...), custom_call_target="tpu_custom_call" | custom-call | tf_op jit(solution)/shard_map/pallas_call | solution.py:1375
  290.2 15.5 %shard_map.473 = (bf16[5,512,1664]{2,1,0:T(8,128)(2,1)}, bf16[5,512,1536]{2,1,0:T(8,128)(2,1)}, bf16[8,320,256]{2,1,0:T(8,128)(2,1)}) custom-call(s32[1]{0:T(128)} %bitcast.first_ref, bf16[8,256,1664]{2,1,0:T(8,128)(2,1)} %get-tuple-element.81.rows_ref, bf16[8,256,1536]{2,1,0:T(8,128)(2,1)} %get-tuple-element.82.grads_ref), custom_call_target="tpu_custom_call" | custom-call | flops 1 | bytes 1 | tf_op jit(solution)/shard_map/pallas_call | solution.py:303
  305.7 0.6 stack.85.order_ref
  306.3 0.6 stack.86.slots_ref
  306.9 51.0 %shard_map.474 = (bf16[5,512,1536]{2,1,0:T(8,128)(2,1)}, bf16[5,512,1664]{2,1,0:T(8,128)(2,1)}, bf16[2,5,32,4608]{3,2,1,0:T(8,128)(2,1)}, bf16[2,5,32,4608]{3,2,...) custom-call(s32[1]{0:T(128)} %bitcast.first_ref, ...), custom_call_target="tpu_custom_call" | custom-call | flops 1 | bytes 1 | tf_op jit(solution)/shard_map/pallas_call | solution.py:473
  358.0 10.6 %shard_map.475.blocks_ref = bf16[8,256,1664]{2,1,0:T(8,128)(2,1)} custom-call(bf16[8,320,256]{2,1,0:T(8,128)(2,1)} %get-tuple-element.83.pick_ref, bf16[5,512,1664]{2,1,0:T(8,128)(2,1)} %get-tuple-element.88.rows_ref), custom_call_target="tpu_custom_call" | custom-call | flops 1 | bytes 1 | tf_op jit(solution)/shard_map/pallas_call | solution.py:338
  368.6 10.1 %shard_map.476.moe_blocks = bf16[8,256,1536]{2,1,0:T(8,128)(2,1)} custom-call(bf16[8,320,256]{2,1,0:T(8,128)(2,1)} %get-tuple-element.83.pick_ref, bf16[5,512,1536]{2,1,0:T(8,128)(2,1)} %get-tuple-element.89.rows_ref), custom_call_target="tpu_custom_call" | custom-call | flops 1 | bytes 1 | tf_op jit(solution)/shard_map/pallas_call | solution.py:338
  378.7 177.0 %shard_map.477 = (f32[256,1536]{1,0:T(8,128)}, bf16[4,256,384]{2,1,0:T(8,128)(2,1)}, bf16[8,4,48,1664]{3,2,1,0:T(8,128)(2,1)}, bf16[256,1536]{1,0:T(8,128)(2,1)}...) custom-call(bf16[8,256,1664]{2,1,0:T(8,128)(2,1)} %shard_map.475.blo, ...), custom_call_target="tpu_custom_call" | custom-call | tf_op jit(solution)/shard_map/pallas_call | solution.py:951
  555.7 0.0 copy-start.1
  555.7 0.0 copy-start.3
  555.7 0.0 copy-start.4
  555.8 105.1 %shard_map.478 = (bf16[5,32,4608]{2,1,0:T(8,128)(2,1)}, bf16[5,32,4608]{2,1,0:T(8,128)(2,1)}, bf16[5,32,4608]{2,1,0:T(8,128)(2,1)}, f32[256,1536]{1,0:T(8,128)},...) custom-call(bf16[5,32,4608]{2,1,0:T(8,128)(2,1)} %get-tuple-element.104.ready2, ...), custom_call_target="tpu_custom_call" | custom-call | tf_op jit(solution)/shard_map/pallas_call | solution.py:1120
  660.9 0.0 copy-start.13
  660.9 0.0 copy-start.14
  660.9 0.0 copy-start.15
  660.9 0.0 copy-start.2
  660.9 0.0 copy-start.5
  660.9 0.0 copy-start.6
  660.9 0.0 copy-start.7
  660.9 0.0 copy-start.11
  661.0 0.0 copy-start.16
  661.0 0.0 copy-start.17
  661.0 0.0 copy-start.8
  661.0 0.0 copy-start.9
  661.0 0.9 slice_bitcast_fusion.4
  662.0 0.9 slice_bitcast_fusion
  662.9 0.0 copy-done.1
  662.9 0.0 copy-done.3
  662.9 0.0 copy-done.4
  662.9 1.6 convert_subtract_fusion
  664.6 0.0 copy-start.10
  664.6 0.0 copy-done.13
  664.6 0.0 copy-done.14
  664.6 0.0 copy-done.15
  664.6 0.5 multiply_subtract_fusion.1
  665.2 0.0 copy-done.2
  665.2 0.0 copy-done.5
  665.2 1.1 convert_subtract_fusion.1
  666.3 0.2 slice_reduce_fusion
  666.5 0.0 copy-start.12
  666.5 0.5 multiply_subtract_fusion
  667.0 0.0 copy-done.8
  667.0 0.1 copy.92
  667.1 0.0 copy-done.9
  667.1 0.1 copy.91
  667.2 0.7 copy.94
  667.9 0.7 copy.95
  668.6 0.7 copy.96
  669.3 0.7 copy.97
  670.0 0.7 pad_add_fusion.places_ref
  670.6 38.2 %shard_map.479 = (f32[20,96,1024]{2,1,0:T(8,128)}, f32[20,96,1024]{2,1,0:T(8,128)}, f32[20,96,1024]{2,1,0:T(8,128)}, f32[20,96,1024]{2,1,0:T(8,128)}, f32[20,32,...) custom-call(s32[4]{0:T(128)} %pad_add_fusion.places_ref, ...), custom_call_target="tpu_custom_call" | custom-call | flops 1 | bytes 1 | tf_op jit(solution)/shard_map/pallas_call | solution.py:1565
  708.9 2.1 copy.114
  710.9 0.0 copy-done
  710.9 1.1 copy.115
  (18 shorter events, 0.2 us)
Async XLA Ops:
  555.7 107.2 %copy-start.1 = (bf16[48,2560]{1,0:T(8,128)(2,1)S(1)}, bf16[48,2560]{1,0:T(8,128)(2,1)}, u32[]{:S(2)}) copy-start(bf16[48,2560]{1,0:T(8,128)(2,1)} %param.32) | copy-start | bytes 737284
  555.7 107.2 %copy-start.3 = (f32[48,2560]{1,0:T(8,128)S(1)}, f32[48,2560]{1,0:T(8,128)}, u32[]{:S(2)}) copy-start(f32[48,2560]{1,0:T(8,128)} %param.34) | copy-start | bytes 1474564
  555.7 107.2 %copy-start.4 = (f32[48,2560]{1,0:T(8,128)S(1)}, f32[48,2560]{1,0:T(8,128)}, u32[]{:S(2)}) copy-start(f32[48,2560]{1,0:T(8,128)} %param.33) | copy-start | bytes 1474564
  660.9 3.7 copy-start.13
  660.9 3.7 copy-start.14
  660.9 3.7 copy-start.15
  660.9 4.3 copy-start.2
  660.9 4.3 copy-start.5
  660.9 4.2 copy-start.6
  660.9 4.2 copy-start.7
  660.9 5.5 copy-start.11
  661.0 5.5 copy-start.16
  661.0 5.5 copy-start.17
  661.0 6.0 copy-start.8
  661.0 6.1 copy-start.9
  664.6 44.3 %copy-start.10 = (f32[48]{0:T(128)}, f32[48]{0:T(128)S(1)}, u32[]{:S(2)}) copy-start(f32[48]{0:T(128)S(1)} %get-tuple-element.283) | copy-start | bytes 580
  666.5 42.4 %copy-start.12 = (f32[48]{0:T(128)}, f32[48]{0:T(128)S(1)}, u32[]{:S(2)}) copy-start(f32[48]{0:T(128)S(1)} %slice_reduce_fusion) | copy-start | bytes 580
  670.6 40.3 %copy-start = (f32[256,1536]{1,0:T(8,128)S(1)}, f32[256,1536]{1,0:T(8,128)}, u32[]{:S(2)}) copy-start(f32[256,1536]{1,0:T(8,128)} %get-tuple-element.282) | copy-start | bytes 4718596

commit v4 on v3

--- a/solution.py
+++ b/solution.py
@@ -168,7 +168,7 @@
     )
 
 
-def attend_back(rows_ref, query_ref, keys_ref, values_ref, grad_ref, out_ref, flipped, grad_keys, grad_values):
+def attend_back(rows_ref, query_ref, keys_ref, values_ref, grad_ref, out_ref, flipped, grad_keys, grad_values, between=None):
     block = 256
     blocks = rows_ref.shape[0] // block
     heads, groups = query_ref.shape[0], keys_ref.shape[0]
@@ -220,6 +220,8 @@
             out_ref[span, column : column + 128] = turn_lanes(
                 stacked[:, column : column + 128], tables, -1.0
             ).astype(jnp.bfloat16)
+        if between is not None and index == 1:
+            between()
     for index in range(blocks):
         span = pl.ds(index * block, block)
         tables = lane_tables(rows_ref[span, :])
@@ -325,28 +327,33 @@
     )(first, rows, grads)
 
 
-def combine_kernel(pick_ref, rows_ref, out_ref):
-    rows = jnp.concatenate([rows_ref[item] for item in range(rows_ref.shape[0])], 0)
-    out_ref[0] = lax.dot_general(
-        pick_ref[0], rows, (((0,), (0,)), ((), ())), preferred_element_type=jnp.float32
-    ).astype(jnp.bfloat16)
-
-
-def combine(pick, rows):
+def combine_kernel(pick_ref, *refs):
+    half = len(refs) // 2
+    for rows_ref, out_ref in zip(refs[:half], refs[half:]):
+        rows = jnp.concatenate([rows_ref[item] for item in range(rows_ref.shape[0])], 0)
+        out_ref[0] = lax.dot_general(
+            pick_ref[0], rows, (((0,), (0,)), ((), ())), preferred_element_type=jnp.float32
+        ).astype(jnp.bfloat16)
+
+
+def combine(pick, arrays):
     sources, slots, tokens = pick.shape
-    count, _, wide = rows.shape
+    count = arrays[0].shape[0]
     return pl.pallas_call(
         combine_kernel,
         grid=(sources,),
-        in_specs=[
-            pl.BlockSpec((1, slots, tokens), lambda s: (s, 0, 0)),
-            pl.BlockSpec((count, CAP, wide), lambda s: (0, s, 0)),
-        ],
-        out_specs=pl.BlockSpec((1, tokens, wide), lambda s: (s, 0, 0)),
-        out_shape=jax.ShapeDtypeStruct((sources, tokens, wide), jnp.bfloat16),
+        in_specs=[pl.BlockSpec((1, slots, tokens), lambda s: (s, 0, 0))]
+        + [pl.BlockSpec((count, CAP, rows.shape[2]), lambda s: (0, s, 0)) for rows in arrays],
+        out_specs=tuple(
+            pl.BlockSpec((1, tokens, rows.shape[2]), lambda s: (s, 0, 0)) for rows in arrays
+        ),
+        out_shape=tuple(
+            jax.ShapeDtypeStruct((sources, tokens, rows.shape[2]), jnp.bfloat16)
+            for rows in arrays
+        ),
         compiler_params=pltpu.CompilerParams(vmem_limit_bytes=62 * 1024 * 1024),
         cost_estimate=pl.CostEstimate(flops=1, bytes_accessed=1, transcendentals=0),
-    )(pick, rows)
+    )(pick, *arrays)
 
 
 def expert_kernel(first_ref, order_ref, slots_ref, rows_ref, grads_ref, *refs):
@@ -1008,18 +1015,31 @@
     ]
     line = [link.push(ready2, done2, "dp", 2), link.push(ready1, done1, "dp", 1)]
     zones = grad_pack_ref.shape[0]
-    to_core[0].wait_recv()
-    for zone in range(zones):
-        pack_sent[zone] = (
-            grad_pack_ref[zone, c_at(2)].astype(jnp.float32)
-            + pack_core[0, zone].astype(jnp.float32)
-        ).astype(jnp.bfloat16)
-    pack_over_pair = link.push(pack_sent, pack_pair, "ctx", 2)
+    held = []
+
+    def pack_step():
+        to_core[0].wait_recv()
+        for zone in range(zones):
+            pack_sent[zone] = (
+                grad_pack_ref[zone, c_at(2)].astype(jnp.float32)
+                + pack_core[0, zone].astype(jnp.float32)
+            ).astype(jnp.bfloat16)
+        held.append(link.push(pack_sent, pack_pair, "ctx", 2))
+
     fetch([(keep0.at[1], stage.at[0]), (arrived.at[0, 1], stage.at[1])], local)
     add_into(sent, [stage.at[0], stage.at[1]])
     pair = link.push(sent, crossed, "ctx", 2)
     attend_back(
-        table_ref, query_ref, keys_ref, values_ref, seq_grad_ref, mixed, flipped, grad_keys, grad_values
+        table_ref,
+        query_ref,
+        keys_ref,
+        values_ref,
+        seq_grad_ref,
+        mixed,
+        flipped,
+        grad_keys,
+        grad_values,
+        pack_step,
     )
     blocks, block = scaled.shape[:2]
     for index in range(blocks):
@@ -1055,7 +1075,7 @@
     ).astype(jnp.bfloat16)
     scaled_over_pair = link.push(scaled_sent, scaled_pair, "ctx", 2)
     to_core[1].wait_recv()
-    pack_over_pair.wait_recv()
+    held[0].wait_recv()
     for zone in range(zones):
         pack_blocks[zone] = (
             grad_pack_ref[zone, c].astype(jnp.float32)
@@ -1292,7 +1312,7 @@
         column_line[flip - 1].wait_recv()
         block = all_columns.at[2 * z_at(flip) + y]
         column_over.append(link.push(block, block, "expert", 1))
-    moved = {1: move(1), 2: move(2)}
+    moved = {2: move(2), 1: move(1)}
     line.start()
     arrive([pack_over])
     pack_pair = link.push(all_pack.at[:, :, c], all_pack.at[:, :, c], "ctx", 2)
@@ -1684,8 +1704,7 @@
     produced, grad_rows, parts = run_experts(
         first, order, slot_rows, slot_grads, pieces, hidden, close
     )
-    shared_grads = combine(pick, grad_rows)
-    shared = combine(pick, produced)
+    shared_grads, shared = combine(pick, (grad_rows, produced))
     if close:
         place = lax.axis_index("dp")
         (

time: 722 us -> 716 us (level)
  Pallas kernels: 688 us -> 680 us
    pallas_call x2 -> x1, Pallas kernels: 20.7 us -> 15.3 us  [combine(): pl.pallas_call(combine_kernel, grid=(sources,), in_specs=[pl.BlockSpec((1...]
where the time goes in v4:
time: 716 us; the launch traced here: 704 us
  Pallas kernels  680 us (95%)
  local copies, waits for them, and re-layouts  14.2 us (2%)
  other arithmetic  8.88 us (1%)
    pallas_call x1, Pallas kernels, opening(): pl.pallas_call(opening_kernel, out_shape=(jax.ShapeDtypeStruct(all_rows,...  278 us
    pallas_call x1, Pallas kernels, returning(): pl.pallas_call(returning_kernel, out_shape=(jax.ShapeDtypeStruct((tokens,...  176 us
    pallas_call x1, Pallas kernels, closing(): pl.pallas_call(closing_kernel, out_shape=(jax.ShapeDtypeStruct(piece, kin...  106 us
    pallas_call x1, Pallas kernels, run_experts(): pl.pallas_call(expert_kernel, grid_spec=pltpu.PrefetchScalarGridSpec(num_...  51 us
    pallas_call x1, Pallas kernels, expert_step(): pl.pallas_call(expert_step_kernel, grid_spec=pltpu.PrefetchScalarGridSpec...  38.2 us
    pallas_call x1, Pallas kernels, dispatch(): pl.pallas_call(dispatch_kernel, grid_spec=pltpu.PrefetchScalarGridSpec(nu...  15.5 us
    pallas_call x1, Pallas kernels, combine(): pl.pallas_call(combine_kernel, grid=(sources,), in_specs=[pl.BlockSpec((1...  15.3 us

profile of v4, /device:TPU:0, one launch (start us, length us, event | category | flops | bytes accessed | tf_op | source)
XLA Modules:
  0.0 704.1 jit_solution(6378440270168647998)
XLA Ops:
  0.7 0.7 convert_element_type.45
  1.4 0.6 fusion.9
  1.9 0.8 pad_maximum_fusion.1.table_ref
  2.7 0.7 convert_element_type.52
  3.4 1.1 fusion.1
  4.5 0.7 maximum_bitcast_fusion.columns_ref
  5.2 0.8 copy.85
  6.0 0.8 copy.86
  6.8 1.7 concatenate.14.pack_ref
  8.4 1.5 copy.87.routes_ref
  9.9 277.6 %shard_map.472 = (bf16[4,256,1536]{2,1,0:T(8,128)(2,1)}, bf16[4,256,128]{2,1,0:T(8,128)(2,1)}, bf16[8,4,48,640]{3,2,1,0:T(8,128)(2,1)}, bf16[4,2,4,48,1664]{4,3,...) custom-call(bf16[256,1536]{1,0:T(8,128)(2,1)} %rows_ref.3, ...), custom_call_target="tpu_custom_call" | custom-call | tf_op jit(solution)/shard_map/pallas_call | solution.py:1395
  287.6 15.5 %shard_map.473 = (bf16[5,512,1664]{2,1,0:T(8,128)(2,1)}, bf16[5,512,1536]{2,1,0:T(8,128)(2,1)}, bf16[8,320,256]{2,1,0:T(8,128)(2,1)}) custom-call(s32[1]{0:T(128)} %bitcast.first_ref, bf16[8,256,1664]{2,1,0:T(8,128)(2,1)} %get-tuple-element.83.rows_ref, bf16[8,256,1536]{2,1,0:T(8,128)(2,1)} %get-tuple-element.84.grads_ref), custom_call_target="tpu_custom_call" | custom-call | flops 1 | bytes 1 | tf_op jit(solution)/shard_map/pallas_call | solution.py:305
  303.1 0.6 stack.85.order_ref
  303.7 0.6 stack.86.slots_ref
  304.3 51.0 %shard_map.474 = (bf16[5,512,1536]{2,1,0:T(8,128)(2,1)}, bf16[5,512,1664]{2,1,0:T(8,128)(2,1)}, bf16[2,5,32,4608]{3,2,1,0:T(8,128)(2,1)}, bf16[2,5,32,4608]{3,2,...) custom-call(s32[1]{0:T(128)} %bitcast.first_ref, ...), custom_call_target="tpu_custom_call" | custom-call | flops 1 | bytes 1 | tf_op jit(solution)/shard_map/pallas_call | solution.py:480
  355.3 15.3 %shard_map.475 = (bf16[8,256,1664]{2,1,0:T(8,128)(2,1)}, bf16[8,256,1536]{2,1,0:T(8,128)(2,1)}) custom-call(bf16[8,320,256]{2,1,0:T(8,128)(2,1)} %get-tuple-element.85.pick_ref, bf16[5,512,1664]{2,1,0:T(8,128)(2,1)} %get-tuple-element.90.refs_0_, bf16[5,512,1536]{2,1,0:T(8,128)(2,1)} %get-tuple-element.91.refs_1_), custom_call_target="tpu_custom_call" | custom-call | flops 1 | bytes 1 | tf_op jit(solution)/shard_map/pallas_call | solution.py:342
  370.7 176.0 %shard_map.476 = (f32[256,1536]{1,0:T(8,128)}, bf16[4,256,384]{2,1,0:T(8,128)(2,1)}, bf16[8,4,48,1664]{3,2,1,0:T(8,128)(2,1)}, bf16[256,1536]{1,0:T(8,128)(2,1)}...) custom-call(bf16[8,256,1664]{2,1,0:T(8,128)(2,1)} %get-tuple-element, ...), custom_call_target="tpu_custom_call" | custom-call | tf_op jit(solution)/shard_map/pallas_call | solution.py:958
  546.7 0.0 copy-start.1
  546.7 0.0 copy-start.3
  546.7 0.0 copy-start.4
  546.7 106.1 %shard_map.477 = (bf16[5,32,4608]{2,1,0:T(8,128)(2,1)}, bf16[5,32,4608]{2,1,0:T(8,128)(2,1)}, bf16[5,32,4608]{2,1,0:T(8,128)(2,1)}, f32[256,1536]{1,0:T(8,128)},...) custom-call(bf16[5,32,4608]{2,1,0:T(8,128)(2,1)} %get-tuple-element.108.ready2, ...), custom_call_target="tpu_custom_call" | custom-call | tf_op jit(solution)/shard_map/pallas_call | solution.py:1140
  652.8 0.0 copy-start.13
  652.8 0.0 copy-start.14
  652.8 0.0 copy-start.15
  652.8 0.0 copy-start.2
  652.8 0.0 copy-start.5
  652.8 0.0 copy-start.6
  652.9 0.0 copy-start.7
  652.9 0.0 copy-start.11
  652.9 0.0 copy-start.16
  652.9 0.0 copy-start.17
  652.9 0.0 copy-start.8
  652.9 0.0 copy-start.9
  652.9 0.9 slice_bitcast_fusion.4
  653.9 0.9 slice_bitcast_fusion
  654.8 0.0 copy-done.1
  654.9 0.0 copy-done.3
  654.9 0.0 copy-done.4
  654.9 1.6 convert_subtract_fusion
  656.5 0.0 copy-start.10
  656.5 0.0 copy-done.13
  656.5 0.0 copy-done.14
  656.5 0.0 copy-done.15
  656.5 0.5 multiply_subtract_fusion.1
  657.1 0.0 copy-done.2
  657.1 0.0 copy-done.5
  657.1 0.0 copy-done.6
  657.1 1.1 convert_subtract_fusion.1
  658.2 0.2 slice_reduce_fusion
  658.4 0.0 copy-start.12
  658.4 0.5 multiply_subtract_fusion
  659.0 0.0 copy-done.8
  659.0 0.1 copy.92
  659.0 0.1 copy.91
  659.2 0.7 copy.94
  659.8 0.7 copy.95
  660.5 0.7 copy.96
  661.2 0.7 copy.97
  661.9 0.6 pad_add_fusion.places_ref
  662.5 38.2 %shard_map.478 = (f32[20,96,1024]{2,1,0:T(8,128)}, f32[20,96,1024]{2,1,0:T(8,128)}, f32[20,96,1024]{2,1,0:T(8,128)}, f32[20,96,1024]{2,1,0:T(8,128)}, f32[20,32,...) custom-call(s32[4]{0:T(128)} %pad_add_fusion.places_ref, ...), custom_call_target="tpu_custom_call" | custom-call | flops 1 | bytes 1 | tf_op jit(solution)/shard_map/pallas_call | solution.py:1585
  700.7 0.0 copy-done.10
  700.7 0.0 copy-done.12
  700.7 2.1 copy.114
  702.8 1.1 copy.115
  (17 shorter events, 0.2 us)
Async XLA Ops:
  546.7 108.2 %copy-start.1 = (bf16[48,2560]{1,0:T(8,128)(2,1)S(1)}, bf16[48,2560]{1,0:T(8,128)(2,1)}, u32[]{:S(2)}) copy-start(bf16[48,2560]{1,0:T(8,128)(2,1)} %param.32) | copy-start | bytes 737284
  546.7 108.2 %copy-start.3 = (f32[48,2560]{1,0:T(8,128)S(1)}, f32[48,2560]{1,0:T(8,128)}, u32[]{:S(2)}) copy-start(f32[48,2560]{1,0:T(8,128)} %param.34) | copy-start | bytes 1474564
  546.7 108.2 %copy-start.4 = (f32[48,2560]{1,0:T(8,128)S(1)}, f32[48,2560]{1,0:T(8,128)}, u32[]{:S(2)}) copy-start(f32[48,2560]{1,0:T(8,128)} %param.33) | copy-start | bytes 1474564
  652.8 3.7 copy-start.13
  652.8 3.7 copy-start.14
  652.8 3.7 copy-start.15
  652.8 4.3 copy-start.2
  652.8 4.3 copy-start.5
  652.8 4.2 copy-start.6
  652.9 4.2 copy-start.7
  652.9 5.5 copy-start.11
  652.9 5.5 copy-start.16
  652.9 5.5 copy-start.17
  652.9 6.0 copy-start.8
  652.9 6.1 copy-start.9
  656.5 44.2 %copy-start.10 = (f32[48]{0:T(128)}, f32[48]{0:T(128)S(1)}, u32[]{:S(2)}) copy-start(f32[48]{0:T(128)S(1)} %get-tuple-element.287) | copy-start | bytes 580
  658.4 42.3 %copy-start.12 = (f32[48]{0:T(128)}, f32[48]{0:T(128)S(1)}, u32[]{:S(2)}) copy-start(f32[48]{0:T(128)S(1)} %slice_reduce_fusion) | copy-start | bytes 580
  662.5 40.3 %copy-start = (f32[256,1536]{1,0:T(8,128)S(1)}, f32[256,1536]{1,0:T(8,128)}, u32[]{:S(2)}) copy-start(f32[256,1536]{1,0:T(8,128)} %get-tuple-element.286) | copy-start | bytes 4718596

commit v5 on v4

--- a/solution.py
+++ b/solution.py
@@ -1042,6 +1042,22 @@
         pack_step,
     )
     blocks, block = scaled.shape[:2]
+    wide = normed_ref.shape[1] // blocks
+    some = zones // blocks
+    for index in range(blocks):
+        part = lax.dot_general(
+            normed_ref[:, index * wide : (index + 1) * wide],
+            mixed[...],
+            (((0,), (0,)), ((), ())),
+            preferred_element_type=jnp.float32,
+        ).astype(jnp.bfloat16)
+        part_blocks[index * some : (index + 1) * some] = part.reshape(
+            (some,) + part_blocks.shape[1:]
+        )
+    part_fold = Fold(
+        part_blocks, part_out, part_over, part_sums, part_parts, part_sends, part_receives
+    )
+    part_fold.start()
     for index in range(blocks):
         scaled[index] = lax.dot_general(
             mixed[index * block : (index + 1) * block, :],
@@ -1053,27 +1069,12 @@
         link.push(scaled.at[c_at(flip)], scaled_core.at[number], "ctx", 1)
         for number, flip in enumerate((3, 1))
     ]
-    wide = normed_ref.shape[1] // blocks
-    some = zones // blocks
-    for index in range(blocks):
-        part = lax.dot_general(
-            normed_ref[:, index * wide : (index + 1) * wide],
-            mixed[...],
-            (((0,), (0,)), ((), ())),
-            preferred_element_type=jnp.float32,
-        ).astype(jnp.bfloat16)
-        part_blocks[index * some : (index + 1) * some] = part.reshape(
-            (some,) + part_blocks.shape[1:]
-        )
-    part_fold = Fold(
-        part_blocks, part_out, part_over, part_sums, part_parts, part_sends, part_receives
-    )
-    part_fold.start()
     scaled_to_core[0].wait_recv()
     scaled_sent[...] = (
         scaled[c_at(2)].astype(jnp.float32) + scaled_core[0].astype(jnp.float32)
     ).astype(jnp.bfloat16)
     scaled_over_pair = link.push(scaled_sent, scaled_pair, "ctx", 2)
+    part_fold.early(0)
     to_core[1].wait_recv()
     held[0].wait_recv()
     for zone in range(zones):
@@ -1086,7 +1087,6 @@
         pack_blocks, shard_pack_ref, pack_over, pack_sums, pack_parts, pack_sends, pack_receives
     )
     pack_fold.start()
-    part_fold.early(0)
     part_fold.early(1)
     pack_fold.early(0)
     pack_fold.early(1)

time: 716 us -> 713 us (level)
  no operation moved by 1% of the time
where the time goes in v5:
time: 713 us; the launch traced here: 703 us
  Pallas kernels  679 us (95%)
  local copies, waits for them, and re-layouts  14.2 us (2%)
  other arithmetic  8.88 us (1%)
    pallas_call x1, Pallas kernels, opening(): pl.pallas_call(opening_kernel, out_shape=(jax.ShapeDtypeStruct(all_rows,...  278 us
    pallas_call x1, Pallas kernels, returning(): pl.pallas_call(returning_kernel, out_shape=(jax.ShapeDtypeStruct((tokens,...  176 us
    pallas_call x1, Pallas kernels, closing(): pl.pallas_call(closing_kernel, out_shape=(jax.ShapeDtypeStruct(piece, kin...  105 us
    pallas_call x1, Pallas kernels, run_experts(): pl.pallas_call(expert_kernel, grid_spec=pltpu.PrefetchScalarGridSpec(num_...  51 us
    pallas_call x1, Pallas kernels, expert_step(): pl.pallas_call(expert_step_kernel, grid_spec=pltpu.PrefetchScalarGridSpec...  38.2 us
    pallas_call x1, Pallas kernels, dispatch(): pl.pallas_call(dispatch_kernel, grid_spec=pltpu.PrefetchScalarGridSpec(nu...  15.5 us
    pallas_call x1, Pallas kernels, combine(): pl.pallas_call(combine_kernel, grid=(sources,), in_specs=[pl.BlockSpec((1...  15.3 us

profile of v5, /device:TPU:0, one launch (start us, length us, event | category | flops | bytes accessed | tf_op | source)
XLA Modules:
  0.0 703.4 jit_solution(692543427054528035)
XLA Ops:
  0.7 0.7 convert_element_type.45
  1.4 0.6 fusion.9
  1.9 0.8 pad_maximum_fusion.1.table_ref
  2.7 0.7 convert_element_type.52
  3.4 1.1 fusion.1
  4.5 0.7 maximum_bitcast_fusion.columns_ref
  5.2 0.8 copy.85
  6.0 0.8 copy.86
  6.8 1.7 concatenate.14.pack_ref
  8.4 1.5 copy.87.routes_ref
  9.9 277.6 %shard_map.472 = (bf16[4,256,1536]{2,1,0:T(8,128)(2,1)}, bf16[4,256,128]{2,1,0:T(8,128)(2,1)}, bf16[8,4,48,640]{3,2,1,0:T(8,128)(2,1)}, bf16[4,2,4,48,1664]{4,3,...) custom-call(bf16[256,1536]{1,0:T(8,128)(2,1)} %rows_ref.3, ...), custom_call_target="tpu_custom_call" | custom-call | tf_op jit(solution)/shard_map/pallas_call | solution.py:1395
  287.6 15.5 %shard_map.473 = (bf16[5,512,1664]{2,1,0:T(8,128)(2,1)}, bf16[5,512,1536]{2,1,0:T(8,128)(2,1)}, bf16[8,320,256]{2,1,0:T(8,128)(2,1)}) custom-call(s32[1]{0:T(128)} %bitcast.first_ref, bf16[8,256,1664]{2,1,0:T(8,128)(2,1)} %get-tuple-element.83.rows_ref, bf16[8,256,1536]{2,1,0:T(8,128)(2,1)} %get-tuple-element.84.grads_ref), custom_call_target="tpu_custom_call" | custom-call | flops 1 | bytes 1 | tf_op jit(solution)/shard_map/pallas_call | solution.py:305
  303.1 0.6 stack.85.order_ref
  303.7 0.6 stack.86.slots_ref
  304.3 51.0 %shard_map.474 = (bf16[5,512,1536]{2,1,0:T(8,128)(2,1)}, bf16[5,512,1664]{2,1,0:T(8,128)(2,1)}, bf16[2,5,32,4608]{3,2,1,0:T(8,128)(2,1)}, bf16[2,5,32,4608]{3,2,...) custom-call(s32[1]{0:T(128)} %bitcast.first_ref, ...), custom_call_target="tpu_custom_call" | custom-call | flops 1 | bytes 1 | tf_op jit(solution)/shard_map/pallas_call | solution.py:480
  355.3 15.3 %shard_map.475 = (bf16[8,256,1664]{2,1,0:T(8,128)(2,1)}, bf16[8,256,1536]{2,1,0:T(8,128)(2,1)}) custom-call(bf16[8,320,256]{2,1,0:T(8,128)(2,1)} %get-tuple-element.85.pick_ref, bf16[5,512,1664]{2,1,0:T(8,128)(2,1)} %get-tuple-element.90.refs_0_, bf16[5,512,1536]{2,1,0:T(8,128)(2,1)} %get-tuple-element.91.refs_1_), custom_call_target="tpu_custom_call" | custom-call | flops 1 | bytes 1 | tf_op jit(solution)/shard_map/pallas_call | solution.py:342
  370.7 176.0 %shard_map.476 = (f32[256,1536]{1,0:T(8,128)}, bf16[4,256,384]{2,1,0:T(8,128)(2,1)}, bf16[8,4,48,1664]{3,2,1,0:T(8,128)(2,1)}, bf16[256,1536]{1,0:T(8,128)(2,1)}...) custom-call(bf16[8,256,1664]{2,1,0:T(8,128)(2,1)} %get-tuple-element, ...), custom_call_target="tpu_custom_call" | custom-call | tf_op jit(solution)/shard_map/pallas_call | solution.py:958
  546.7 0.0 copy-start.1
  546.7 0.0 copy-start.3
  546.7 0.0 copy-start.4
  546.7 105.4 %shard_map.477 = (bf16[5,32,4608]{2,1,0:T(8,128)(2,1)}, bf16[5,32,4608]{2,1,0:T(8,128)(2,1)}, bf16[5,32,4608]{2,1,0:T(8,128)(2,1)}, f32[256,1536]{1,0:T(8,128)},...) custom-call(bf16[5,32,4608]{2,1,0:T(8,128)(2,1)} %get-tuple-element.108.ready2, ...), custom_call_target="tpu_custom_call" | custom-call | tf_op jit(solution)/shard_map/pallas_call | solution.py:1140
  652.1 0.0 copy-start.13
  652.1 0.0 copy-start.14
  652.1 0.0 copy-start.15
  652.1 0.0 copy-start.2
  652.1 0.0 copy-start.5
  652.2 0.0 copy-start.6
  652.2 0.0 copy-start.7
  652.2 0.0 copy-start.11
  652.2 0.0 copy-start.16
  652.2 0.0 copy-start.17
  652.2 0.0 copy-start.8
  652.2 0.0 copy-start.9
  652.2 0.9 slice_bitcast_fusion.4
  653.2 0.9 slice_bitcast_fusion
  654.2 0.0 copy-done.1
  654.2 0.0 copy-done.3
  654.2 0.0 copy-done.4
  654.2 1.6 convert_subtract_fusion
  655.8 0.0 copy-start.10
  655.8 0.0 copy-done.13
  655.8 0.0 copy-done.14
  655.8 0.0 copy-done.15
  655.9 0.5 multiply_subtract_fusion.1
  656.4 0.0 copy-done.2
  656.4 0.0 copy-done.5
  656.4 0.0 copy-done.6
  656.4 0.0 copy-done.7
  656.4 1.1 convert_subtract_fusion.1
  657.5 0.2 slice_reduce_fusion
  657.7 0.0 copy-done.11
  657.7 0.0 copy-start.12
  657.7 0.5 multiply_subtract_fusion
  658.3 0.1 copy.92
  658.3 0.1 copy.91
  658.5 0.7 copy.94
  659.1 0.7 copy.95
  659.8 0.7 copy.96
  660.5 0.7 copy.97
  661.2 0.6 pad_add_fusion.places_ref
  661.8 38.2 %shard_map.478 = (f32[20,96,1024]{2,1,0:T(8,128)}, f32[20,96,1024]{2,1,0:T(8,128)}, f32[20,96,1024]{2,1,0:T(8,128)}, f32[20,96,1024]{2,1,0:T(8,128)}, f32[20,32,...) custom-call(s32[4]{0:T(128)} %pad_add_fusion.places_ref, ...), custom_call_target="tpu_custom_call" | custom-call | flops 1 | bytes 1 | tf_op jit(solution)/shard_map/pallas_call | solution.py:1585
  700.0 2.1 copy.114
  702.1 0.0 copy-done
  702.1 1.1 copy.115
  (17 shorter events, 0.2 us)
Async XLA Ops:
  546.7 107.5 %copy-start.1 = (bf16[48,2560]{1,0:T(8,128)(2,1)S(1)}, bf16[48,2560]{1,0:T(8,128)(2,1)}, u32[]{:S(2)}) copy-start(bf16[48,2560]{1,0:T(8,128)(2,1)} %param.32) | copy-start | bytes 737284
  546.7 107.5 %copy-start.3 = (f32[48,2560]{1,0:T(8,128)S(1)}, f32[48,2560]{1,0:T(8,128)}, u32[]{:S(2)}) copy-start(f32[48,2560]{1,0:T(8,128)} %param.34) | copy-start | bytes 1474564
  546.7 107.5 %copy-start.4 = (f32[48,2560]{1,0:T(8,128)S(1)}, f32[48,2560]{1,0:T(8,128)}, u32[]{:S(2)}) copy-start(f32[48,2560]{1,0:T(8,128)} %param.33) | copy-start | bytes 1474564
  652.1 3.7 copy-start.13
  652.1 3.7 copy-start.14
  652.1 3.7 copy-start.15
  652.1 4.3 copy-start.2
  652.1 4.3 copy-start.5
  652.2 4.2 copy-start.6
  652.2 4.2 copy-start.7
  652.2 5.5 copy-start.11
  652.2 5.5 copy-start.16
  652.2 5.5 copy-start.17
  652.2 6.0 copy-start.8
  652.2 6.1 copy-start.9
  655.8 44.2 %copy-start.10 = (f32[48]{0:T(128)}, f32[48]{0:T(128)S(1)}, u32[]{:S(2)}) copy-start(f32[48]{0:T(128)S(1)} %get-tuple-element.287) | copy-start | bytes 580
  657.7 42.3 %copy-start.12 = (f32[48]{0:T(128)}, f32[48]{0:T(128)S(1)}, u32[]{:S(2)}) copy-start(f32[48]{0:T(128)S(1)} %slice_reduce_fusion) | copy-start | bytes 580
  661.8 40.3 %copy-start = (f32[256,1536]{1,0:T(8,128)S(1)}, f32[256,1536]{1,0:T(8,128)}, u32[]{:S(2)}) copy-start(f32[256,1536]{1,0:T(8,128)} %get-tuple-element.286) | copy-start | bytes 4718596
